TPU v7x, 32 devices: a whole 2x2x4 slice. The times are simulated.
32 devices in a mesh: dp: 4 (over y, x), tensor: 8 (over z, core).
Axes of the slice: x: 2, y: 2, z: 4, core: 2. Of those that a mesh axis runs over, the one named last changes fastest.
Arguments:
- layer_input: bfloat16 [2, 4, 1536, 1536], P(None, 'dp', 'tensor'), may hold values from -6 to 6
- lengths: int32 [2, 4], P(None, 'dp'), may hold values from 1 to 1536, as said below
- attn_gain: bfloat16 [1536], P(('dp', 'tensor')), may hold values from 0.099609375 to 1.8984375
- query_proj: bfloat16 [1536, 1536], P(('dp', 'tensor')), may hold values from -0.15625 to 0.15625
- query_bias: bfloat16 [1536], P(('dp', 'tensor')), may hold values from -3 to 3
- key_proj: bfloat16 [1536, 256], P(('dp', 'tensor')), may hold values from -0.15625 to 0.15625
- key_bias: bfloat16 [256], P(('dp', 'tensor')), may hold values from -3 to 3
- value_proj: bfloat16 [1536, 256], P(('dp', 'tensor')), may hold values from -0.15625 to 0.15625
- value_bias: bfloat16 [256], P(('dp', 'tensor')), may hold values from -3 to 3
- out_proj: bfloat16 [1536, 1536], P(('dp', 'tensor')), may hold values from -2 to 2
- mlp_gain: bfloat16 [1536], P(('dp', 'tensor')), may hold values from 0.099609375 to 1.8984375
- gate_proj: bfloat16 [1536, 8960], P(None, 'tensor'), may hold values from -0.15625 to 0.15625
- up_proj: bfloat16 [1536, 8960], P(None, 'tensor'), may hold values from -0.15625 to 0.15625
- down_proj: bfloat16 [8960, 1536], P('tensor'), may hold values from -0.0625 to 0.0625
- cotangent: bfloat16 [2, 4, 1536, 1536], P(None, 'dp', 'tensor'), may hold values from -6 to 6
Outputs:
- layer_output: bfloat16 [2, 4, 1536, 1536], P(None, 'dp', 'tensor')
- grad_input: float32 [2, 4, 1536, 1536], P(None, 'dp', 'tensor')
- grad_attn_gain: float32 [1536], P(('dp', 'tensor'))
- grad_query_proj: float32 [1536, 1536], P(('dp', 'tensor'))
- grad_query_bias: float32 [1536], P(('dp', 'tensor'))
- grad_key_proj: float32 [1536, 256], P(('dp', 'tensor'))
- grad_key_bias: float32 [256], P(('dp', 'tensor'))
- grad_value_proj: float32 [1536, 256], P(('dp', 'tensor'))
- grad_value_bias: float32 [256], P(('dp', 'tensor'))
- grad_out_proj: float32 [1536, 1536], P(('dp', 'tensor'))
- grad_mlp_gain: float32 [1536], P(('dp', 'tensor'))
- grad_gate_proj: float32 [1536, 8960], P(None, 'tensor')
- grad_up_proj: float32 [1536, 8960], P(None, 'tensor')
- grad_down_proj: float32 [8960, 1536], P('tensor')
Inputs may be any that keep to these rules, and one draw needn't show every extreme that they name: `lengths`: right padding: in each column (the 2 sequences of one index of dp) at least one sequence has all 1536 tokens; every sequence has at least one token.
All inputs are finite; a program needn't handle non-finite values.
Results may differ from a plain program's by a relative error of at most 0.025.
Values may be sent and summed in bfloat16 or wider, within the bound.
A program may use at most 320 MiB of HBM per device.

v0:
```python
import jax
import jax.numpy as jnp
from jax import lax
from jax.sharding import PartitionSpec as P

H = 12
KV = 2
HD = 128


ROPE_BASE = 1000000.0
EPS = 1e-06


def rope_tables(positions):
    half = HD // 2
    freqs = ROPE_BASE ** (-(jnp.arange(half, dtype=jnp.float32) * 2.0 / HD))
    angles = positions.astype(jnp.float32)[:, None] * freqs[None, :]
    angles = jnp.concatenate([angles, angles], axis=1)
    return (jnp.cos(angles)[:, None, :], jnp.sin(angles)[:, None, :])


def rotate(values, cosine, sine):
    half = values.shape[-1] // 2
    turned = jnp.concatenate([-values[..., half:], values[..., :half]], axis=-1)
    return values * cosine + turned * sine


def rotate_back(grads, cosine, sine):
    half = grads.shape[-1] // 2
    scaled = grads * sine
    turned = jnp.concatenate([scaled[..., half:], -scaled[..., :half]], axis=-1)
    return grads * cosine + turned


def normalize(rows, gain):
    factor = lax.rsqrt(jnp.mean(rows * rows, axis=-1, keepdims=True) + EPS)
    normed = rows * factor
    return (normed, factor, normed * gain)


def norm_back(grad_out, normed, factor, gain):
    inner = grad_out * gain
    grad_rows = factor * (inner - normed * jnp.mean(inner * normed, axis=-1, keepdims=True))
    return (grad_rows, jnp.sum(grad_out * normed, axis=0))


def widened(piece, count):
    return jnp.zeros((piece.shape[0] * count,) + piece.shape[1:], jnp.float32)


def fetch_weights(gain_one, wquery, bquery, wkey, bkey, wvalue, bvalue, wout, gain_two):
    return (
        lax.all_gather(gain_one, ("dp", "tensor"), axis=0, tiled=True),
        lax.all_gather(wquery, ("dp", "tensor"), axis=0, tiled=True),
        lax.all_gather(bquery, ("dp", "tensor"), axis=0, tiled=True),
        lax.all_gather(wkey, ("dp", "tensor"), axis=0, tiled=True),
        lax.all_gather(bkey, ("dp", "tensor"), axis=0, tiled=True),
        lax.all_gather(wvalue, ("dp", "tensor"), axis=0, tiled=True),
        lax.all_gather(bvalue, ("dp", "tensor"), axis=0, tiled=True),
        lax.all_gather(wout, ("dp", "tensor"), axis=0, tiled=True),
        lax.all_gather(gain_two, ("dp", "tensor"), axis=0, tiled=True),
    )


def on_device(
    layer_input,
    lengths,
    attn_gain,
    query_proj,
    query_bias,
    key_proj,
    key_bias,
    value_proj,
    value_bias,
    out_proj,
    mlp_gain,
    gate_proj,
    up_proj,
    down_proj,
    cotangent,
):
    f32 = jnp.float32
    b16 = jnp.bfloat16
    micro_count = layer_input.shape[0]
    rows = layer_input.shape[2]
    total = rows * lax.axis_size("tensor")
    groups = H // KV
    factor_qk = HD ** (-0.5)
    devices = lax.axis_size(("dp", "tensor"))
    positions = lax.axis_index("tensor") * rows + jnp.arange(rows, dtype=jnp.int32)
    key_positions = jnp.arange(total, dtype=jnp.int32)
    cosine, sine = rope_tables(positions)
    causal = key_positions[None, :] <= positions[:, None]
    acc_gain_one = widened(attn_gain, devices)
    acc_query = widened(query_proj, devices)
    acc_qbias = widened(query_bias, devices)
    acc_key = widened(key_proj, devices)
    acc_kbias = widened(key_bias, devices)
    acc_value = widened(value_proj, devices)
    acc_vbias = widened(value_bias, devices)
    acc_out = widened(out_proj, devices)
    acc_gain_two = widened(mlp_gain, devices)
    acc_gate = jnp.zeros(gate_proj.shape, f32)
    acc_up = jnp.zeros(up_proj.shape, f32)
    acc_down = jnp.zeros(down_proj.shape, f32)
    outputs = []
    input_grads = []
    for micro in range(micro_count):
        gain_one, wquery, bquery, wkey, bkey, wvalue, bvalue, wout, gain_two = fetch_weights(
            attn_gain,
            query_proj,
            query_bias,
            key_proj,
            key_bias,
            value_proj,
            value_bias,
            out_proj,
            mlp_gain,
        )
        gain_one = gain_one.astype(f32)
        gain_two = gain_two.astype(f32)
        inputs = layer_input[micro, 0].astype(f32)
        length = lengths[micro, 0]
        normed_one, factor_one, hidden = normalize(inputs, gain_one)
        hidden = hidden.astype(b16)
        q_lin = jnp.dot(hidden, wquery, preferred_element_type=f32) + bquery.astype(f32)
        k_lin = jnp.dot(hidden, wkey, preferred_element_type=f32) + bkey.astype(f32)
        v_lin = jnp.dot(hidden, wvalue, preferred_element_type=f32) + bvalue.astype(f32)
        queries = rotate(q_lin.reshape(rows, H, HD), cosine, sine).astype(b16)
        grouped = queries.reshape(rows, KV, groups, HD)
        keys_rot = (
            rotate(k_lin.reshape(rows, KV, HD), cosine, sine).astype(b16).reshape(rows, KV * HD)
        )
        values = v_lin.astype(b16)
        all_keys, all_values = (
            lax.all_gather(keys_rot, "tensor", axis=0, tiled=True),
            lax.all_gather(values, "tensor", axis=0, tiled=True),
        )
        all_keys = all_keys.reshape(total, KV, HD)
        all_values = all_values.reshape(total, KV, HD)
        allowed = (causal & (key_positions < length)[None, :])[None, None]
        scores = (
            jnp.einsum("tkgd,ukd->kgtu", grouped, all_keys, preferred_element_type=f32) * factor_qk
        )
        scores = jnp.where(allowed, scores, -1e30)
        top = jnp.max(scores, axis=-1, keepdims=True)
        expd = jnp.exp(scores - top)
        summed = jnp.sum(expd, axis=-1, keepdims=True)
        logsum = top + jnp.log(summed)
        probs_low = (expd / summed).astype(b16)
        attended = jnp.einsum("kgtu,ukd->tkgd", probs_low, all_values, preferred_element_type=f32)
        attended = attended.reshape(rows, H * HD).astype(b16)
        mixed = inputs + jnp.dot(attended, wout, preferred_element_type=f32)
        normed_two, factor_two, hidden_two = normalize(mixed, gain_two)
        hidden_two = hidden_two.astype(b16)
        full_hidden = lax.all_gather(hidden_two, "tensor", axis=0, tiled=True)
        gate = jnp.dot(full_hidden, gate_proj, preferred_element_type=f32)
        up = jnp.dot(full_hidden, up_proj, preferred_element_type=f32)
        sigma = jax.nn.sigmoid(gate)
        silu_gate = gate * sigma
        activ = (silu_gate * up).astype(b16)
        mlp_out = lax.psum_scatter(
            jnp.dot(activ, down_proj, preferred_element_type=f32).astype(jnp.bfloat16),
            "tensor",
            scatter_dimension=0,
            tiled=True,
        ).astype(jnp.float32)
        outputs.append((mixed + mlp_out).astype(b16))
        valid = (positions < length).astype(f32)[:, None]
        grad_rows = cotangent[micro, 0].astype(f32) * valid
        full_grad = lax.all_gather(grad_rows.astype(b16), "tensor", axis=0, tiled=True)
        grad_activ = jnp.dot(full_grad, down_proj.T, preferred_element_type=f32)
        acc_down = acc_down + jnp.dot(activ.T, full_grad, preferred_element_type=f32)
        grad_gate = (grad_activ * up * sigma * (1.0 + gate * (1.0 - sigma))).astype(b16)
        grad_up = (grad_activ * silu_gate).astype(b16)
        acc_gate = acc_gate + jnp.dot(full_hidden.T, grad_gate, preferred_element_type=f32)
        acc_up = acc_up + jnp.dot(full_hidden.T, grad_up, preferred_element_type=f32)
        grad_hidden_two = lax.psum_scatter(
            (
                jnp.dot(grad_gate, gate_proj.T, preferred_element_type=f32)
                + jnp.dot(grad_up, up_proj.T, preferred_element_type=f32)
            ).astype(jnp.bfloat16),
            "tensor",
            scatter_dimension=0,
            tiled=True,
        ).astype(jnp.float32)
        grad_mixed, gain_two_grad = norm_back(grad_hidden_two, normed_two, factor_two, gain_two)
        acc_gain_two = acc_gain_two + gain_two_grad
        grad_mixed = grad_mixed + grad_rows
        grad_mixed_low = grad_mixed.astype(b16)
        acc_out = acc_out + jnp.dot(attended.T, grad_mixed_low, preferred_element_type=f32)
        grad_attended = jnp.dot(grad_mixed_low, wout.T, preferred_element_type=f32).astype(b16)
        grad_attended = grad_attended.reshape(rows, KV, groups, HD)
        again = (
            jnp.einsum("tkgd,ukd->kgtu", grouped, all_keys, preferred_element_type=f32) * factor_qk
        )
        probs = jnp.exp(jnp.where(allowed, again, -1e30) - logsum)
        probs_again = probs.astype(b16)
        grad_probs = jnp.einsum(
            "tkgd,ukd->kgtu", grad_attended, all_values, preferred_element_type=f32
        )
        row_dot = jnp.sum(grad_probs * probs, axis=-1, keepdims=True)
        grad_scores = (probs * (grad_probs - row_dot)).astype(b16)
        grad_queries = (
            jnp.einsum("kgtu,ukd->tkgd", grad_scores, all_keys, preferred_element_type=f32)
            * factor_qk
        )
        grad_keys = (
            jnp.einsum("kgtu,tkgd->ukd", grad_scores, grouped, preferred_element_type=f32)
            * factor_qk
        )
        grad_values = jnp.einsum(
            "kgtu,tkgd->ukd", probs_again, grad_attended, preferred_element_type=f32
        )
        grad_keys, grad_values = (
            lax.psum_scatter(
                grad_keys.astype(jnp.bfloat16), "tensor", scatter_dimension=0, tiled=True
            ).astype(jnp.float32),
            lax.psum_scatter(
                grad_values.astype(jnp.bfloat16), "tensor", scatter_dimension=0, tiled=True
            ).astype(jnp.float32),
        )
        grad_q_lin = (
            rotate_back(grad_queries.reshape(rows, H, HD), cosine, sine)
            .reshape(rows, H * HD)
            .astype(b16)
        )
        grad_k_lin = rotate_back(grad_keys, cosine, sine).reshape(rows, KV * HD).astype(b16)
        grad_v_lin = grad_values.reshape(rows, KV * HD).astype(b16)
        acc_query = acc_query + jnp.dot(hidden.T, grad_q_lin, preferred_element_type=f32)
        acc_key = acc_key + jnp.dot(hidden.T, grad_k_lin, preferred_element_type=f32)
        acc_value = acc_value + jnp.dot(hidden.T, grad_v_lin, preferred_element_type=f32)
        acc_qbias = acc_qbias + jnp.sum(grad_q_lin.astype(f32), axis=0)
        acc_kbias = acc_kbias + jnp.sum(grad_k_lin.astype(f32), axis=0)
        acc_vbias = acc_vbias + jnp.sum(grad_v_lin.astype(f32), axis=0)
        grad_hidden = (
            jnp.dot(grad_q_lin, wquery.T, preferred_element_type=f32)
            + jnp.dot(grad_k_lin, wkey.T, preferred_element_type=f32)
            + jnp.dot(grad_v_lin, wvalue.T, preferred_element_type=f32)
        )
        grad_in, gain_one_grad = norm_back(grad_hidden, normed_one, factor_one, gain_one)
        acc_gain_one = acc_gain_one + gain_one_grad
        input_grads.append(grad_in + grad_mixed)
    summed_grads = (
        lax.psum_scatter(acc_gain_one, ("dp", "tensor"), scatter_dimension=0, tiled=True),
        lax.psum_scatter(acc_query, ("dp", "tensor"), scatter_dimension=0, tiled=True),
        lax.psum_scatter(acc_qbias, ("dp", "tensor"), scatter_dimension=0, tiled=True),
        lax.psum_scatter(acc_key, ("dp", "tensor"), scatter_dimension=0, tiled=True),
        lax.psum_scatter(acc_kbias, ("dp", "tensor"), scatter_dimension=0, tiled=True),
        lax.psum_scatter(acc_value, ("dp", "tensor"), scatter_dimension=0, tiled=True),
        lax.psum_scatter(acc_vbias, ("dp", "tensor"), scatter_dimension=0, tiled=True),
        lax.psum_scatter(acc_out, ("dp", "tensor"), scatter_dimension=0, tiled=True),
        lax.psum_scatter(acc_gain_two, ("dp", "tensor"), scatter_dimension=0, tiled=True),
    )
    gate_total, up_total, down_total = (
        lax.psum(acc_gate.astype(jnp.bfloat16), "dp").astype(jnp.float32),
        lax.psum(acc_up.astype(jnp.bfloat16), "dp").astype(jnp.float32),
        lax.psum(acc_down.astype(jnp.bfloat16), "dp").astype(jnp.float32),
    )
    layer_output = jnp.stack(outputs)[:, None]
    grad_input = jnp.stack(input_grads)[:, None]
    return (
        layer_output,
        grad_input,
        summed_grads[0],
        summed_grads[1],
        summed_grads[2],
        summed_grads[3],
        summed_grads[4],
        summed_grads[5],
        summed_grads[6],
        summed_grads[7],
        summed_grads[8],
        gate_total,
        up_total,
        down_total,
    )


def solution(mesh):
    placed = (
        P(None, "dp", "tensor", None),
        P(None, "dp"),
        P(("dp", "tensor")),
        P(("dp", "tensor"), None),
        P(("dp", "tensor")),
        P(("dp", "tensor"), None),
        P(("dp", "tensor")),
        P(("dp", "tensor"), None),
        P(("dp", "tensor")),
        P(("dp", "tensor"), None),
        P(("dp", "tensor")),
        P(None, "tensor"),
        P(None, "tensor"),
        P("tensor", None),
        P(None, "dp", "tensor", None),
    )
    return jax.shard_map(
        on_device,
        mesh=mesh,
        in_specs=placed,
        out_specs=(
            P(None, "dp", "tensor", None),
            P(None, "dp", "tensor", None),
            P(("dp", "tensor")),
            P(("dp", "tensor"), None),
            P(("dp", "tensor")),
            P(("dp", "tensor"), None),
            P(("dp", "tensor")),
            P(("dp", "tensor"), None),
            P(("dp", "tensor")),
            P(("dp", "tensor"), None),
            P(("dp", "tensor")),
            P(None, "tensor"),
            P(None, "tensor"),
            P("tensor", None),
        ),
        check_vma=False,
    )
```

profile of v0, /device:TPU:0, one launch (start us, length us, event | category | flops | bytes accessed | tf_op | source)
XLA Modules:
  0.0 1686.2 jit_solution(17391819223847771329)
XLA Ops:
  14.6 42.5 %all-reduce.15 = (bf16[256]{0:T(256)(128)(2,1)S(1)}, bf16[1536]{0:T(1024)(128)(2,1)S(1)}, bf16[1536]{0:T(1024)(128)(2,1)S(1)}, bf16[256]{0:T(256)(128)(2,1)S(1)}, bf16[1536]{0:T(1024)(128)(2,1)S(1)}) all-reduce(bf16[256]{0:T(256)(128)(2,1)S(1)} %dynamic-update-slice.2, ...), channel_id=1, replica_groups=mesh['dp'=4,'tensor'=8] {'dp','tensor'}, use_global_device_ids=true, to_apply=%add.2 | all-reduce | flops 5120 | bytes 20480
  57.1 46.8 %all_gather.64 = bf16[1536,256]{1,0:T(8,128)(2,1)S(1)} all-gather(bf16[48,256]{1,0:T(8,128)(2,1)} %param.20), channel_id=1, replica_groups=mesh['dp'=4,'tensor'=8] {'dp','tensor'}, dimensions={0}, use_global_device_ids=true | all-gather | bytes 811008 | tf_op jit(solution)/shard_map/all_gather | solution.py:57
  119.3 19.1 %all_gather.66 = bf16[1536,256]{1,0:T(8,128)(2,1)} all-gather(bf16[192,256]{1,0:T(8,128)(2,1)S(1)} %get-tuple-element.155), channel_id=1, replica_groups=mesh['dp'=4,'tensor'=8] {'tensor'}, dimensions={0}, use_global_device_ids=true | all-gather | bytes 884736 | tf_op jit(solution)/shard_map/all_gather | solution.py:137
  141.1 40.1 %all_gather.61 = bf16[1536,256]{1,0:T(8,128)(2,1)S(1)} all-gather(bf16[48,256]{1,0:T(8,128)(2,1)} %param.22), channel_id=1, replica_groups=mesh['dp'=4,'tensor'=8] {'dp','tensor'}, dimensions={0}, use_global_device_ids=true | all-gather | bytes 811008 | tf_op jit(solution)/shard_map/all_gather | solution.py:59
  183.5 17.3 %all_gather.63 = bf16[1536,256]{1,0:T(8,128)(2,1)} all-gather(bf16[192,256]{1,0:T(8,128)(2,1)S(1)} %fusion.111), channel_id=1, replica_groups=mesh['dp'=4,'tensor'=8] {'tensor'}, dimensions={0}, use_global_device_ids=true | all-gather | bytes 884736 | tf_op jit(solution)/shard_map/all_gather | solution.py:138
  303.7 45.4 %all-gather.11.cloned.1.call-done = bf16[1536,1536]{1,0:T(8,128)(2,1)} async-done(((bf16[192,1536]{1,0:T(8,128)(2,1)}), bf16[1536,1536]{1,0:T(8,128)(2,1)}) %all-gather.11.cloned.1.call-update) | async-done | bytes 4718608 | tf_op jit(solution)/shard_map/all_gather | solution.py:157
  367.3 34.4 %all-gather.15.cloned.1.call-done = bf16[1536,1536]{1,0:T(8,128)(2,1)} async-done(((bf16[192,1536]{1,0:T(8,128)(2,1)}), bf16[1536,1536]{1,0:T(8,128)(2,1)}) %all-gather.15.cloned.1.call-update) | async-done | bytes 4718608 | tf_op jit(solution)/shard_map/all_gather | solution.py:172
  401.7 15.0 multiply_convert_fusion.2
  435.8 20.0 %all_gather.72 = bf16[1536,256]{1,0:T(8,128)(2,1)} all-gather(bf16[192,256]{1,0:T(8,128)(2,1)S(1)} %fusion.112), channel_id=1, replica_groups=mesh['dp'=4,'tensor'=8] {'tensor'}, dimensions={0}, use_global_device_ids=true | all-gather | bytes 884736 | tf_op jit(solution)/shard_map/all_gather | solution.py:138
  458.5 20.2 %all_gather.73 = bf16[1536,256]{1,0:T(8,128)(2,1)} all-gather(bf16[192,256]{1,0:T(8,128)(2,1)S(1)} %copy-done.59), channel_id=1, replica_groups=mesh['dp'=4,'tensor'=8] {'tensor'}, dimensions={0}, use_global_device_ids=true | all-gather | bytes 884736 | tf_op jit(solution)/shard_map/all_gather | solution.py:137
  517.6 50.2 %all-gather.13.cloned.1.call-done = bf16[1536,1536]{1,0:T(8,128)(2,1)} async-done(((bf16[192,1536]{1,0:T(8,128)(2,1)}), bf16[1536,1536]{1,0:T(8,128)(2,1)}) %all-gather.13.cloned.1.call-update) | async-done | bytes 4718608 | tf_op jit(solution)/shard_map/all_gather | solution.py:157
  567.9 10.8 fusion.202
  586.2 33.8 %all-gather.17.cloned.1.call-done = bf16[1536,1536]{1,0:T(8,128)(2,1)} async-done(((bf16[192,1536]{1,0:T(8,128)(2,1)}), bf16[1536,1536]{1,0:T(8,128)(2,1)}) %all-gather.17.cloned.1.call-update) | async-done | bytes 4718608 | tf_op jit(solution)/shard_map/all_gather | solution.py:172
  620.1 14.9 multiply_convert_fusion
  711.0 50.4 %reduce-scatter.9.cloned.1.call-done = bf16[192,1536]{1,0:T(8,128)(2,1)} async-done(((bf16[1536,1536]{1,0:T(8,128)(2,1)}), bf16[192,1536]{1,0:T(8,128)(2,1)}) %reduce-scatter.9.cloned.1.call-update) | async-done | bytes 589840 | tf_op jit(solution)/shard_map/reduce_scatter | solution.py:163
  761.3 55.5 %reduce-scatter.11.cloned.1.call-done = bf16[192,1536]{1,0:T(8,128)(2,1)} async-done(((bf16[1536,1536]{1,0:T(8,128)(2,1)}), bf16[192,1536]{1,0:T(8,128)(2,1)}) %reduce-scatter.11.cloned.1.call-update) | async-done | bytes 589840 | tf_op jit(solution)/shard_map/reduce_scatter | solution.py:163
  905.4 11.0 fusion.11
  928.6 53.1 %all-reduce.21.cloned.1.call-done = (bf16[1536,2,128]{2,1,0:T(2,128)(2,1)}, bf16[1536,2,128]{2,1,0:T(2,128)(2,1)}, bf16[1536,2,128]{2,1,0:T(2,128)(2,1)}, bf16[1536,2,128]{2,1,0:T(2,128)(2,1)}) async-done(((bf16[1536,2,128]{2,1,0:T(2,128)(2,1)}, bf16[1536,2,128]{2,1,0:T(2,128)(2,1)}, bf16[1536,2,128]{2,1,0:T(2,128)(2,1)}, bf16[1536,2,128]{2,1,0:T(2,128)(2,1)}), (bf16[1536,2,128]{2,1,0:T(2,128)(2,1)}, ...) | async-done | bytes 3145744
  1062.6 127.8 %all-reduce.23.cloned.1.call-done = (bf16[1536,1120]{0,1:T(8,128)(2,1)}, bf16[1536,1120]{0,1:T(8,128)(2,1)}, bf16[1120,1536]{1,0:T(8,128)(2,1)}) async-done(((bf16[1536,1120]{0,1:T(8,128)(2,1)}, bf16[1536,1120]{0,1:T(8,128)(2,1)}, bf16[1120,1536]{1,0:T(8,128)(2,1)}), (bf16[1536,1120]{0,1:T(8,128)(2,1)}, bf16[1536,1120]{0,1:T(8,128)(2,1)}, bf16[1120,1536]{1,0:T(8,128)(2,1)})) %all-reduce.23.cloned.1.call-update) | async-done | bytes 10321936 | tf_op jit(solution)/shard_map/psum | solution.py:257
  1209.4 39.7 %all-reduce.14 = (f32[1536]{0:T(1024)S(1)}, f32[1536]{0:T(1024)S(1)}, f32[256]{0:T(256)S(1)}, f32[256]{0:T(256)S(1)}, f32[1536]{0:T(1024)S(1)}) all-reduce(f32[1536]{0:T(1024)S(1)} %add.347, f32[1536]{0:T(1024)S(1)} %add.354, f32[256]{0:T(256)S(1)} %add_bitcast_fusion.1, ...), channel_id=10, replica_groups=mesh['dp'=4,'tensor'=8] {'dp','tensor'}, use_global_device_ids=true, to_apply=%region_24.25.clone | all-reduce | flops 5120 | bytes 40960
  1256.2 37.9 %reduce-scatter.19.cloned.1.call-done = f32[48,256]{1,0:T(8,128)} async-done(((f32[1536,256]{1,0:T(8,128)}), f32[48,256]{1,0:T(8,128)}) %reduce-scatter.19.cloned.1.call-update) | async-done | bytes 49168 | tf_op jit(solution)/shard_map/reduce_scatter | solution.py:249
  1294.1 102.5 %reduce-scatter.21.cloned.1.call-done = f32[48,256]{1,0:T(8,128)} async-done(((f32[1536,256]{1,0:T(8,128)}), f32[48,256]{1,0:T(8,128)}) %reduce-scatter.21.cloned.1.call-update) | async-done | bytes 49168 | tf_op jit(solution)/shard_map/reduce_scatter | solution.py:251
  1396.6 141.9 %reduce-scatter.23.cloned.1.call-done = f32[48,1536]{1,0:T(8,128)} async-done(((f32[1536,1536]{1,0:T(8,128)}), f32[48,1536]{1,0:T(8,128)}) %reduce-scatter.23.cloned.1.call-update) | async-done | bytes 294928 | tf_op jit(solution)/shard_map/reduce_scatter | solution.py:253
  1538.6 140.9 %reduce-scatter.17.cloned.1.call-done = f32[48,1536]{1,0:T(8,128)} async-done(((f32[1536,1536]{1,0:T(8,128)}), f32[48,1536]{1,0:T(8,128)}) %reduce-scatter.17.cloned.1.call-update) | async-done | bytes 294928 | tf_op jit(solution)/shard_map/reduce_scatter | solution.py:247
  (413 shorter events, 499.1 us)
Async XLA Ops:
  7.2 394.5 %copy-start = (bf16[1120,1536]{1,0:T(8,128)(2,1)S(1)}, bf16[1120,1536]{1,0:T(8,128)(2,1)}, u32[]{:S(2)}) copy-start(bf16[1120,1536]{1,0:T(8,128)(2,1)} %param.28) | copy-start | bytes 10321924
  7.2 200.8 %all-gather.7.cloned.1.call-start = ((), (), s32[]{:S(2)}) async-start(), calls=%async_computation.8 | async-start | bytes 4866048 | tf_op jit(solution)/shard_map/all_gather | solution.py:55
  7.9 285.4 %all-gather.9.cloned.1.call-start = ((), (), s32[]{:S(2)}) async-start(), calls=%async_computation.9 | async-start | bytes 4866048 | tf_op jit(solution)/shard_map/all_gather | solution.py:61
  8.7 340.4 %all-gather.11.cloned.1.call-start = ((), (), s32[]{:S(2)}) async-start(), calls=%async_computation.10 | async-start | bytes 5308416 | tf_op jit(solution)/shard_map/all_gather | solution.py:157
  10.3 99.5 %copy-start.64 = (f32[192]{0:T(256)}, f32[192]{0:T(256)S(1)}, u32[]{:S(2)}) copy-start(f32[192]{0:T(256)S(1)} %add_rsqrt_fusion.3) | copy-start | bytes 2308
  57.1 376.4 %copy-start.54 = (f32[1536]{0:T(1024)}, f32[1536]{0:T(1024)S(1)}, u32[]{:S(2)}) copy-start(f32[1536]{0:T(1024)S(1)} %convert_element_type.367) | copy-start | bytes 18436
  116.2 147.1 %copy-start.34 = (f32[192,128]{1,0:T(8,128)}, f32[192,128]{1,0:T(8,128)S(1)}, u32[]{:S(2)}) copy-start(f32[192,128]{1,0:T(8,128)S(1)} %get-tuple-element.163) | copy-start | bytes 294916
  299.2 102.5 %all-gather.15.cloned.1.call-start = ((), (), s32[]{:S(2)}) async-start(), calls=%async_computation.14 | async-start | bytes 5308416 | tf_op jit(solution)/shard_map/all_gather | solution.py:172
  303.7 209.4 %reduce-scatter.13.cloned.1.call-start = ((), (), s32[]{:S(2)}) async-start(), calls=%async_computation.15 | async-start | bytes 5308416 | tf_op jit(solution)/shard_map/reduce_scatter | solution.py:179
  433.5 134.4 %all-gather.13.cloned.1.call-start = ((), (), s32[]{:S(2)}) async-start(), calls=%async_computation.12 | async-start | bytes 5308416 | tf_op jit(solution)/shard_map/all_gather | solution.py:157
  516.8 103.2 %all-gather.17.cloned.1.call-start = ((), (), s32[]{:S(2)}) async-start(), calls=%async_computation.16 | async-start | bytes 5308416 | tf_op jit(solution)/shard_map/all_gather | solution.py:172
  517.6 191.2 %reduce-scatter.15.cloned.1.call-start = ((), (), s32[]{:S(2)}) async-start(), calls=%async_computation.17 | async-start | bytes 5308416 | tf_op jit(solution)/shard_map/reduce_scatter | solution.py:179
  651.7 109.6 %reduce-scatter.9.cloned.1.call-start = ((), (), s32[]{:S(2)}) async-start(), calls=%async_computation.11 | async-start | bytes 5308416 | tf_op jit(solution)/shard_map/reduce_scatter | solution.py:163
  661.8 155.1 %reduce-scatter.11.cloned.1.call-start = ((), (), s32[]{:S(2)}) async-start(), calls=%async_computation.13 | async-start | bytes 5308416 | tf_op jit(solution)/shard_map/reduce_scatter | solution.py:163
  671.8 309.9 %all-reduce.21.cloned.1.call-start = ((), (), s32[]{:S(2)}) async-start(), calls=%async_computation.22 | async-start | bytes 6291456
  708.7 108.1 %copy-start.47 = (bf16[192,1536]{1,0:T(8,128)(2,1)S(1)}, bf16[192,1536]{1,0:T(8,128)(2,1)}, u32[]{:S(2)}) copy-start(bf16[192,1536]{1,0:T(8,128)(2,1)} %reduce-scatter.13.cloned.1.call-done) | copy-start | bytes 1769476
  708.7 108.1 %copy-start.74 = (f32[192]{0:T(256)S(1)}, f32[192]{0:T(256)}, u32[]{:S(2)}) copy-start(f32[192]{0:T(256)} %copy-done.73) | copy-start | bytes 2308
  708.7 108.1 %copy-start.76 = (f32[192]{0:T(256)S(1)}, f32[192]{0:T(256)}, u32[]{:S(2)}) copy-start(f32[192]{0:T(256)} %copy-done.75) | copy-start | bytes 2308
  905.3 285.0 %all-reduce.23.cloned.1.call-start = ((), (), s32[]{:S(2)}) async-start(), calls=%async_computation.23 | async-start | bytes 20643840 | tf_op jit(solution)/shard_map/psum | solution.py:257
  926.8 367.4 %reduce-scatter.19.cloned.1.call-start = ((), (), s32[]{:S(2)}) async-start(), calls=%async_computation.19 | async-start | bytes 1622016 | tf_op jit(solution)/shard_map/reduce_scatter | solution.py:249
  987.8 408.8 %reduce-scatter.21.cloned.1.call-start = ((), (), s32[]{:S(2)}) async-start(), calls=%async_computation.20 | async-start | bytes 1622016 | tf_op jit(solution)/shard_map/reduce_scatter | solution.py:251
  993.6 544.9 %reduce-scatter.23.cloned.1.call-start = ((), (), s32[]{:S(2)}) async-start(), calls=%async_computation.21 | async-start | bytes 9732096 | tf_op jit(solution)/shard_map/reduce_scatter | solution.py:253
  1001.3 678.1 %reduce-scatter.17.cloned.1.call-start = ((), (), s32[]{:S(2)}) async-start(), calls=%async_computation.18 | async-start | bytes 9732096 | tf_op jit(solution)/shard_map/reduce_scatter | solution.py:247
  1254.7 424.8 %copy-start.1 = (bf16[1120,1536]{1,0:T(8,128)(2,1)S(1)}, bf16[1120,1536]{1,0:T(8,128)(2,1)}, u32[]{:S(2)}) copy-start(bf16[1120,1536]{1,0:T(8,128)(2,1)} %param.28) | copy-start | bytes 10321924
  (95 other events, 599.2 us)
Sparse Core Ops, SparseCore 0:
  11.0 67.6 all-gather.6
  81.8 64.0 all-gather.8
  299.3 49.7 all-gather.10
  351.1 50.5 all-gather.14
  433.6 65.5 reduce-scatter.12
  517.0 50.8 all-gather.12
  569.5 50.5 all-gather.16
  651.9 53.7 reduce-scatter.14
  708.0 53.3 reduce-scatter.8
  763.5 53.3 reduce-scatter.10
  905.4 76.1 all-reduce.20
  986.0 204.2 all-reduce.22
  1197.0 97.0 reduce-scatter.18
  1300.6 95.9 reduce-scatter.20
  1404.0 134.5 reduce-scatter.22
  1544.9 134.4 reduce-scatter.16
where the time goes:
time: 1690 us
  waiting for transfers between devices  876 us (52%)
  matrix products  320 us (19%)
  blocking collectives  246 us (15%)
  local copies, waits for them, and re-layouts  120 us (7%)
  other arithmetic  108 us (6%)
    reduce_scatter x1, waiting for transfers between devices, on_device(): lax.psum_scatter(acc_out, ('dp', 'tensor'), scatter_dimension=0, tiled=True)  142 us
    reduce_scatter x1, waiting for transfers between devices, on_device(): lax.psum_scatter(acc_query, ('dp', 'tensor'), scatter_dimension=0, tiled=...  141 us
    psum x1, waiting for transfers between devices, on_device(): lax.psum(acc_gate.astype(jnp.bfloat16), 'dp').astype(jnp.float32)  128 us
    reduce_scatter x2, waiting for transfers between devices, on_device(): lax.psum_scatter(jnp.dot(activ, down_proj, preferred_element_type=f32).as...  106 us
    reduce_scatter x1, waiting for transfers between devices, on_device(): lax.psum_scatter(acc_value, ('dp', 'tensor'), scatter_dimension=0, tiled=...  103 us
    all_gather x2, waiting for transfers between devices, on_device(): full_hidden = lax.all_gather(hidden_two, 'tensor', axis=0, tiled=True)  95.6 us
    unnamed x2, blocking collectives  82.3 us
    all_gather x2, waiting for transfers between devices, on_device(): lax.all_gather(grad_rows.astype(b16), 'tensor', axis=0, tiled=True)  68.2 us
  transfers between devices with their start and end apart: 16, of which 12 were waited for; matrix products, arithmetic and copies ran while one was open for 22% of the time, Pallas kernels for 0%

commit v1 on v0

v1 whole, which is shorter than its diff:
```python
import functools

import jax
import jax.numpy as jnp
from jax import lax
from jax.experimental import pallas as pl
from jax.experimental.pallas import tpu as pltpu
from jax.sharding import PartitionSpec as P

H = 12
KV = 2
HD = 128
GROUPS = H // KV
QW = H * HD
KW = KV * HD
QKV = QW + 2 * KW
EXTRA = 128

ROPE_BASE = 1000000.0
EPS = 1e-06
MASKED = -1e30
F32 = jnp.float32
B16 = jnp.bfloat16
VMEM_LIMIT = 56 * 1024 * 1024


def dot(a, b):
    return jnp.dot(a, b, preferred_element_type=F32)


def dot_t(a, b):
    return lax.dot_general(a, b, (((1,), (1,)), ((), ())), preferred_element_type=F32)


def t_dot(a, b):
    return lax.dot_general(a, b, (((0,), (0,)), ((), ())), preferred_element_type=F32)


def rope_tables(positions):
    half = HD // 2
    freqs = ROPE_BASE ** (-(jnp.arange(half, dtype=F32) * 2.0 / HD))
    angles = positions.astype(F32)[:, None] * freqs[None, :]
    cosine = jnp.cos(angles)
    sine = jnp.sin(angles)
    return (
        jnp.concatenate([cosine, cosine], axis=1),
        jnp.concatenate([-sine, sine], axis=1),
    )


def swap(value, axis, bit):
    count = lax.axis_size(axis)
    return lax.ppermute(value, axis, [(i, i ^ bit) for i in range(count)])


def pick(value, index, axis=0):
    return lax.dynamic_index_in_dim(value, index, axis, keepdims=False)


def ordered(mine, other, index):
    first = index == 0
    return jnp.stack([jnp.where(first, mine, other), jnp.where(first, other, mine)])


def line_gather(block, chips, place):
    count = 2 * chips
    from_left, from_right = [], []
    left = right = block
    for step in range(1, chips):
        left = lax.ppermute(left, "tensor", [(i, i + 2) for i in range(count - 2)])
        right = lax.ppermute(right, "tensor", [(i + 2, i) for i in range(count - 2)])
        from_left.append(left)
        from_right.append(right)
    window = jnp.stack(from_left[::-1] + [block] + from_right)
    return lax.dynamic_slice_in_dim(window, chips - 1 - place, chips, 0)


def line_scatter(part, chips, place):
    count = 2 * chips
    left = right = None
    for step in range(1, chips):
        ahead = part(jnp.minimum(place + chips - step, chips - 1))
        behind = part(jnp.maximum(place - chips + step, 0))
        if left is not None:
            ahead = ahead + left.astype(F32)
            behind = behind + right.astype(F32)
        left = lax.ppermute(
            ahead.astype(B16), "tensor", [(i, i + 2) for i in range(2 * step)]
        )
        right = lax.ppermute(
            behind.astype(B16),
            "tensor",
            [(count - 1 - i, count - 3 - i) for i in range(2 * step)],
        )
    return part(place) + left.astype(F32) + right.astype(F32)


def rows_scatter(partial, rows):
    chips = lax.axis_size("tensor") // 2
    place = lax.axis_index("tensor")
    chip, core = place // 2, place % 2
    width = partial.shape[-1]
    blocks = partial.reshape(chips, 2, rows, width)
    got = swap(pick(blocks, 1 - core, 1), "tensor", 1)

    def part(index):
        own = lax.dynamic_slice(blocks, (index, core, 0, 0), (1, 1, rows, width))
        return own[0, 0].astype(F32) + pick(got, index).astype(F32)

    return line_scatter(part, chips, chip)


def gather_weights(block):
    size, width = block.shape
    devices = lax.axis_size(("dp", "tensor"))
    if lax.axis_size("dp") != 4:
        return lax.all_gather(block, ("dp", "tensor"), axis=0, tiled=True)
    tensor = lax.axis_index("tensor")
    core = tensor % 2
    chips = lax.axis_size("tensor") // 2
    line = line_gather(block, chips, tensor // 2)
    row, col = lax.axis_index("dp") // 2, lax.axis_index("dp") % 2
    cut = chips // 2
    one, two = line[:cut], line[cut:]
    one = ordered(one, swap(one, "dp", 1), col)
    two = ordered(two, swap(two, "dp", 2), row)
    one = ordered(one, swap(one, "dp", 2), row)
    two = ordered(two, swap(two, "dp", 1), col)
    plane = jnp.concatenate([one, two.swapaxes(0, 1)], axis=2)
    whole = ordered(plane, swap(plane, "tensor", 1), core)
    whole = jnp.moveaxis(whole, 0, 3)
    return whole.reshape(devices * size, width)


def scatter_weights(grads):
    total, width = grads.shape
    devices = lax.axis_size(("dp", "tensor"))
    size = total // devices
    if lax.axis_size("dp") != 4:
        return lax.psum_scatter(grads, ("dp", "tensor"), scatter_dimension=0, tiled=True).astype(F32)
    tensor = lax.axis_index("tensor")
    core = tensor % 2
    chips = lax.axis_size("tensor") // 2
    row, col = lax.axis_index("dp") // 2, lax.axis_index("dp") % 2
    blocks = grads.reshape(2, 2, chips, 2, size, width)
    cut = chips // 2

    def halve(value, index, axis, mesh_axis, bit):
        got = swap(pick(value, 1 - index, axis), mesh_axis, bit)
        return (pick(value, index, axis).astype(F32) + got.astype(F32)).astype(B16)

    plane = halve(blocks, core, 3, "tensor", 1)
    one, two = plane[:, :, :cut], plane[:, :, cut:]
    one = halve(one, col, 1, "dp", 1)
    two = halve(two, row, 0, "dp", 2)
    one = halve(one, row, 0, "dp", 2)
    two = halve(two, col, 0, "dp", 1)
    line = jnp.concatenate([one, two], axis=0)
    return line_scatter(lambda index: pick(line, index).astype(F32), chips, tensor // 2)


def project_kernel(hidden_ref, weight_ref, bias_ref, cos_ref, sin_ref, out_ref):
    chunk = pl.program_id(0)
    turned = chunk < (QW + KW) // 256
    lin = dot(hidden_ref[...], weight_ref[...]) + bias_ref[...]
    for head in range(2):
        cut = pl.ds(head * HD, HD)
        one = lin[:, head * HD : (head + 1) * HD]
        rot = one * cos_ref[...] + pltpu.roll(one, HD // 2, 1) * sin_ref[...]
        out_ref[:, cut] = jnp.where(turned, rot, one).astype(B16)


def project(hidden, weights, bias, cosine, sine):
    rows, depth = hidden.shape
    return pl.pallas_call(
        project_kernel,
        grid=(QKV // 256,),
        in_specs=[
            pl.BlockSpec((rows, depth), lambda j: (0, 0)),
            pl.BlockSpec((depth, 256), lambda j: (0, j)),
            pl.BlockSpec((1, 256), lambda j: (0, j)),
            pl.BlockSpec((rows, HD), lambda j: (0, 0)),
            pl.BlockSpec((rows, HD), lambda j: (0, 0)),
        ],
        out_specs=pl.BlockSpec((rows, 256), lambda j: (0, j)),
        out_shape=jax.ShapeDtypeStruct((rows, QKV), B16),
        compiler_params=pltpu.CompilerParams(vmem_limit_bytes=VMEM_LIMIT),
        cost_estimate=pl.CostEstimate(
            flops=2 * rows * depth * QKV,
            bytes_accessed=2 * (depth * QKV + rows * depth + rows * QKV),
            transcendentals=0,
        ),
    )(hidden, weights, bias, cosine, sine)


def fill_bias(info_ref, bias):
    shape = bias.shape
    place = info_ref[1] + lax.broadcasted_iota(jnp.int32, shape, 0)
    keys = lax.broadcasted_iota(jnp.int32, shape, 1)
    bias[...] = jnp.where((keys <= place) & (keys < info_ref[0]), 0.0, MASKED)


def attend_kernel(info_ref, q_ref, k_ref, v_ref, out_ref, log_ref, bias):
    @pl.when(pl.program_id(0) == 0)
    def _():
        fill_bias(info_ref, bias)

    scores = dot_t(q_ref[...], k_ref[...]) * (HD**-0.5) + bias[...]
    top = jnp.max(scores, axis=-1, keepdims=True)
    expd = jnp.exp(scores - top)
    summed = jnp.sum(expd, axis=-1, keepdims=True)
    probs = (expd * (1.0 / summed)).astype(B16)
    out_ref[...] = dot(probs, v_ref[...]).astype(B16)
    log_ref[...] = jnp.broadcast_to(top + jnp.log(summed), log_ref.shape)


def attend(info, micro, qkv, keys_values, rows):
    total = keys_values.shape[0]
    return pl.pallas_call(
        attend_kernel,
        grid_spec=pltpu.PrefetchScalarGridSpec(
            num_scalar_prefetch=1,
            grid=(H,),
            in_specs=[
                pl.BlockSpec((rows, HD), lambda h, info: (micro, h)),
                pl.BlockSpec((total, HD), lambda h, info: (0, h // GROUPS)),
                pl.BlockSpec((total, HD), lambda h, info: (0, KV + h // GROUPS)),
            ],
            out_specs=[
                pl.BlockSpec((rows, HD), lambda h, info: (0, h)),
                pl.BlockSpec((rows, HD), lambda h, info: (0, h)),
            ],
            scratch_shapes=[pltpu.VMEM((rows, total), F32)],
        ),
        out_shape=[
            jax.ShapeDtypeStruct((rows, QW), B16),
            jax.ShapeDtypeStruct((rows, QW), F32),
        ],
        compiler_params=pltpu.CompilerParams(vmem_limit_bytes=VMEM_LIMIT),
        cost_estimate=pl.CostEstimate(
            flops=8 * rows * total * QW,
            bytes_accessed=4 * total * KW + 8 * rows * QW,
            transcendentals=H * rows * total,
        ),
    )(info, qkv, keys_values, keys_values)


def attend_back_kernel(
    info_ref, q_ref, k_ref, v_ref, g_ref, log_ref, cos_ref, sin_ref, dq_ref, dk_ref, dv_ref, bias, dk_acc, dv_acc
):
    head = pl.program_id(0)

    @pl.when(head == 0)
    def _():
        fill_bias(info_ref, bias)

    scale = HD**-0.5
    queries, keys, values, grads = q_ref[...], k_ref[...], v_ref[...], g_ref[...]
    scores = dot_t(queries, keys) * scale + bias[...]
    probs = jnp.exp(scores - log_ref[:, :1])
    grad_probs = dot_t(grads, values)
    inner = jnp.sum(grad_probs * probs, axis=-1, keepdims=True)
    grad_scores = (probs * (grad_probs - inner)).astype(B16)
    grad_q = dot(grad_scores, keys) * scale
    turned = grad_q * cos_ref[...] - pltpu.roll(grad_q, HD // 2, 1) * sin_ref[...]
    dq_ref[...] = turned.astype(B16)
    grad_k = t_dot(grad_scores, queries) * scale
    grad_v = t_dot(probs.astype(B16), grads)
    first = lax.rem(head, GROUPS) == 0

    @pl.when(first)
    def _():
        dk_acc[...] = grad_k
        dv_acc[...] = grad_v

    @pl.when(jnp.logical_not(first))
    def _():
        dk_acc[...] += grad_k
        dv_acc[...] += grad_v

    @pl.when(lax.rem(head, GROUPS) == GROUPS - 1)
    def _():
        dk_ref[...] = dk_acc[...].astype(B16)
        dv_ref[...] = dv_acc[...].astype(B16)


def attend_back(info, micro, qkv, keys_values, grads, logs, cosine, sine, rows):
    total = keys_values.shape[0]
    return pl.pallas_call(
        attend_back_kernel,
        grid_spec=pltpu.PrefetchScalarGridSpec(
            num_scalar_prefetch=1,
            grid=(H,),
            in_specs=[
                pl.BlockSpec((rows, HD), lambda h, info: (micro, h)),
                pl.BlockSpec((total, HD), lambda h, info: (0, h // GROUPS)),
                pl.BlockSpec((total, HD), lambda h, info: (0, KV + h // GROUPS)),
                pl.BlockSpec((rows, HD), lambda h, info: (0, h)),
                pl.BlockSpec((rows, HD), lambda h, info: (0, h)),
                pl.BlockSpec((rows, HD), lambda h, info: (0, 0)),
                pl.BlockSpec((rows, HD), lambda h, info: (0, 0)),
            ],
            out_specs=[
                pl.BlockSpec((rows, HD), lambda h, info: (0, h)),
                pl.BlockSpec((total, HD), lambda h, info: (0, h // GROUPS)),
                pl.BlockSpec((total, HD), lambda h, info: (0, h // GROUPS)),
            ],
            scratch_shapes=[
                pltpu.VMEM((rows, total), F32),
                pltpu.VMEM((total, HD), F32),
                pltpu.VMEM((total, HD), F32),
            ],
        ),
        out_shape=[
            jax.ShapeDtypeStruct((rows, QW), B16),
            jax.ShapeDtypeStruct((total, KW), B16),
            jax.ShapeDtypeStruct((total, KW), B16),
        ],
        compiler_params=pltpu.CompilerParams(vmem_limit_bytes=VMEM_LIMIT),
        cost_estimate=pl.CostEstimate(
            flops=20 * rows * total * QW,
            bytes_accessed=8 * total * KW + 12 * rows * QW,
            transcendentals=H * rows * total,
        ),
    )(info, qkv, keys_values, keys_values, grads, logs, cosine, sine)


def norm_back(grad_out, normed, factor, gain):
    inner = grad_out * gain
    grad_rows = factor * (inner - normed * jnp.mean(inner * normed, axis=-1, keepdims=True))
    return (grad_rows, jnp.sum(grad_out * normed, axis=0))


def normalize(rows, gain):
    factor = lax.rsqrt(jnp.mean(rows * rows, axis=-1, keepdims=True) + EPS)
    normed = rows * factor
    return (normed, factor, (normed * gain).astype(B16))


def on_device(
    layer_input,
    lengths,
    attn_gain,
    query_proj,
    query_bias,
    key_proj,
    key_bias,
    value_proj,
    value_bias,
    out_proj,
    mlp_gain,
    gate_proj,
    up_proj,
    down_proj,
    cotangent,
):
    micros = layer_input.shape[0]
    rows = layer_input.shape[2]
    depth = layer_input.shape[3]
    tensor = lax.axis_index("tensor")
    total = rows * lax.axis_size("tensor")
    devices = lax.axis_size(("dp", "tensor"))
    size = query_proj.shape[0]
    small = key_bias.shape[0]
    offset = tensor * rows
    positions = offset + jnp.arange(rows, dtype=jnp.int32)
    cosine, sine = rope_tables(positions)

    extra = jnp.zeros((size, EXTRA), B16)
    extra = extra.at[:, 0].set(attn_gain).at[:, 1].set(query_bias).at[:, 2].set(mlp_gain)
    extra = extra.at[:small, 3].set(key_bias).at[small : 2 * small, 3].set(value_bias)
    packed = gather_weights(jnp.concatenate([query_proj, key_proj, value_proj, extra], axis=1))
    wout = gather_weights(out_proj)
    vectors = packed[:, QKV : QKV + 4].astype(F32)
    gain_one, gain_two = vectors[:, 0], vectors[:, 2]
    tails = vectors[:, 3].reshape(devices, size)
    bias = jnp.concatenate(
        [vectors[:, 1], tails[:, :small].reshape(-1), tails[:, small : 2 * small].reshape(-1)]
    )[None, :]
    wqkv = packed[:, :QKV]

    valid = (positions[None, :] < lengths).astype(F32)[:, :, None]
    grad_rows = cotangent[:, 0].astype(F32) * valid
    full_grads = [
        lax.all_gather(grad_rows[m].astype(B16), "tensor", axis=0, tiled=True) for m in range(micros)
    ]

    inputs = layer_input[:, 0].astype(F32).reshape(micros * rows, depth)
    normed_one, factor_one, hidden = normalize(inputs, gain_one)
    qkv = project(
        hidden, packed, bias, jnp.tile(cosine, (micros, 1)), jnp.tile(sine, (micros, 1))
    )
    infos = [jnp.stack([lengths[m, 0], offset]) for m in range(micros)]

    all_kv, attended, logs, mixed, norm_two, full_hidden = [], [], [], [], [], []
    for m in range(micros):
        all_kv.append(
            lax.all_gather(qkv[m * rows : (m + 1) * rows, QW:], "tensor", axis=0, tiled=True)
        )
    for m in range(micros):
        out, log = attend(infos[m], m, qkv, all_kv[m], rows)
        attended.append(out)
        logs.append(log)
        mixed.append(inputs[m * rows : (m + 1) * rows] + dot(out, wout))
        normed, factor, hidden_two = normalize(mixed[m], gain_two)
        norm_two.append((normed, factor))
        full_hidden.append(lax.all_gather(hidden_two, "tensor", axis=0, tiled=True))

    acc_gate = acc_up = acc_down = 0.0
    out_parts, grad_mixed, gain_two_grads = [], [], []
    for m in range(micros):
        full = full_hidden[m]
        gate = dot(full, gate_proj)
        up = dot(full, up_proj)
        grad_activ = dot_t(full_grads[m], down_proj)
        sigma = jax.nn.sigmoid(gate)
        silu_gate = gate * sigma
        activ = (silu_gate * up).astype(B16)
        grad_gate = (grad_activ * up * sigma * (1.0 + gate * (1.0 - sigma))).astype(B16)
        grad_up = (grad_activ * silu_gate).astype(B16)
        grad_two = (dot_t(grad_gate, gate_proj) + dot_t(grad_up, up_proj)).astype(B16)
        grad_two = rows_scatter(grad_two, rows)
        out_parts.append(dot(activ, down_proj).astype(B16))
        acc_down = acc_down + t_dot(activ, full_grads[m])
        acc_gate = acc_gate + t_dot(full, grad_gate)
        acc_up = acc_up + t_dot(full, grad_up)
        normed, factor = norm_two[m]
        grad, gain_grad = norm_back(grad_two, normed, factor, gain_two)
        gain_two_grads.append(gain_grad)
        grad_mixed.append(grad + grad_rows[m])

    down_total = lax.psum(acc_down.astype(B16), "dp").astype(F32)
    gate_total = lax.psum(acc_gate.astype(B16), "dp").astype(F32)
    up_total = lax.psum(acc_up.astype(B16), "dp").astype(F32)

    grad_low = jnp.concatenate(grad_mixed, axis=0).astype(B16)
    acc_out = t_dot(jnp.concatenate(attended, axis=0), grad_low).astype(B16)
    grad_q, grad_kv = [], []
    for m in range(micros):
        grad_attended = dot_t(grad_low[m * rows : (m + 1) * rows], wout).astype(B16)
        dq, dk, dv = attend_back(
            infos[m], m, qkv, all_kv[m], grad_attended, logs[m], cosine, sine, rows
        )
        grad_q.append(dq)
        summed = rows_scatter(jnp.concatenate([dk, dv], axis=1), rows)
        heads = summed[:, :KW].reshape(rows, KV, HD)
        turned = jnp.concatenate([heads[..., HD // 2 :], heads[..., : HD // 2]], axis=-1)
        heads = heads * cosine[:, None, :] - turned * sine[:, None, :]
        grad_kv.append(
            jnp.concatenate([heads.reshape(rows, KW), summed[:, KW:]], axis=1).astype(B16)
        )
    grad_qkv = jnp.concatenate(
        [jnp.concatenate(grad_q, axis=0), jnp.concatenate(grad_kv, axis=0)], axis=1
    )
    grad_hidden = dot_t(grad_qkv, wqkv)
    grad_in, gain_one_grad = norm_back(grad_hidden, normed_one, factor_one, gain_one)
    grad_bias = jnp.sum(grad_qkv.astype(F32), axis=0)
    acc_qkv = t_dot(hidden, grad_qkv).astype(B16)
    tails = jnp.concatenate(
        [
            grad_bias[QW : QW + KW].reshape(devices, small),
            grad_bias[QW + KW :].reshape(devices, small),
            jnp.zeros((devices, size - 2 * small), F32),
        ],
        axis=1,
    ).reshape(-1)
    columns = jnp.stack([gain_one_grad, grad_bias[:QW], sum(gain_two_grads), tails], axis=1)
    columns = jnp.pad(columns.astype(B16), ((0, 0), (0, EXTRA - 4)))
    grad_out = scatter_weights(acc_out)
    grad_packed = scatter_weights(jnp.concatenate([acc_qkv, columns], axis=1))

    layer_output = jnp.stack(
        [
            (mixed[m] + rows_scatter(out_parts[m], rows)).astype(B16)
            for m in range(micros)
        ]
    )[:, None]
    grad_input = (grad_in + jnp.concatenate(grad_mixed, axis=0)).reshape(micros, 1, rows, depth)
    return (
        layer_output,
        grad_input,
        grad_packed[:, QKV],
        grad_packed[:, :QW],
        grad_packed[:, QKV + 1],
        grad_packed[:, QW : QW + KW],
        grad_packed[:small, QKV + 3],
        grad_packed[:, QW + KW : QKV],
        grad_packed[small : 2 * small, QKV + 3],
        grad_out,
        grad_packed[:, QKV + 2],
        gate_total,
        up_total,
        down_total,
    )


def solution(mesh):
    rows = P(None, "dp", "tensor", None)
    both = P(("dp", "tensor"))
    wide = P(("dp", "tensor"), None)
    placed = (
        rows,
        P(None, "dp"),
        both,
        wide,
        both,
        wide,
        both,
        wide,
        both,
        wide,
        both,
        P(None, "tensor"),
        P(None, "tensor"),
        P("tensor", None),
        rows,
    )
    return jax.shard_map(
        on_device,
        mesh=mesh,
        in_specs=placed,
        out_specs=(
            rows,
            rows,
            both,
            wide,
            both,
            wide,
            both,
            wide,
            both,
            wide,
            both,
            P(None, "tensor"),
            P(None, "tensor"),
            P("tensor", None),
        ),
        check_vma=False,
    )
```

time: 1690 us -> 1070 us (0.63)
  waiting for transfers between devices: 876 us -> 398 us
  blocking collectives: 246 us -> 0 us
  starting transfers between devices: 1.12 us -> 186 us
  matrix products: 320 us -> 198 us
  Pallas kernels: 0 us -> 80.7 us
  local copies, waits for them, and re-layouts: 120 us -> 63.3 us
    reduce_scatter x8 -> x0, waiting for transfers between devices: 529 us -> none  [the longest x1 142 us: on_device(): lax.psum_scatter(acc_out, ('dp', 'tensor'), scatter_dimension=0, tiled=True)]
    ppermute x0 -> x86, waiting for transfers between devices: none -> 259 us  [the longest x26 124 us: swap(): return lax.ppermute(value, axis, [(i, i ^ bit) for i in range(count)])]
    ppermute x0 -> x86, starting transfers between devices: none -> 186 us  [the longest x24 102 us: line_scatter(): lax.ppermute(ahead.astype(B16), 'tensor', [(i, i + 2) for i in range(2 *...]
    all_gather x6 -> x0, blocking collectives: 163 us -> none  [the longest x1 46.8 us: fetch_weights(): lax.all_gather(wkey, ('dp', 'tensor'), axis=0, tiled=True)]
    psum x1, waiting for transfers between devices: 128 us -> 0.01 us  [on_device(): gate_total = lax.psum(acc_gate.astype(B16), 'dp').astype(F32)]
    dot_general x54 -> x25, matrix products: 320 us -> 198 us  [the longest x9 75.1 us: dot_t(): lax.dot_general(a, b, (((1,), (1,)), ((), ())), preferred_element_type=F32)]
    unnamed x2 -> x0, blocking collectives: 82.3 us -> none
    pallas_call x0 -> x5, Pallas kernels: none -> 80.7 us  [the longest x2 43.5 us: attend_back(): pl.pallas_call(attend_back_kernel, grid_spec=pltpu.PrefetchScalarGridSpec...]
  transfers between devices with their start and end apart: 16 -> 93, of which waited for: 12 -> 37; matrix products, arithmetic and copies ran while one was open for 22% -> 28% of each run, Pallas kernels for 0% -> 6%
where the time goes in v1:
time: 1070 us; the launch traced here: 1060 us
  waiting for transfers between devices  398 us (37%)
  matrix products  198 us (19%)
  starting transfers between devices  186 us (17%)
  other arithmetic  117 us (11%)
  Pallas kernels  80.7 us (8%)
  local copies, waits for them, and re-layouts  63.3 us (6%)
  between operations  16.7 us (2%)
    ppermute x26, waiting for transfers between devices, swap(): return lax.ppermute(value, axis, [(i, i ^ bit) for i in range(count)])  124 us
    ppermute x24, starting transfers between devices, line_scatter(): lax.ppermute(ahead.astype(B16), 'tensor', [(i, i + 2) for i in range(2 *...  102 us
    ppermute x24, waiting for transfers between devices, line_scatter(): lax.ppermute(ahead.astype(B16), 'tensor', [(i, i + 2) for i in range(2 *...  91.4 us
    all_gather x2, waiting for transfers between devices, on_device(): full_hidden.append(lax.all_gather(hidden_two, 'tensor', axis=0, tiled=True))  86.1 us
    dot_general x9, matrix products, dot_t(): lax.dot_general(a, b, (((1,), (1,)), ((), ())), preferred_element_type=F32)  75.1 us
    dot_general x8, matrix products, t_dot(): lax.dot_general(a, b, (((0,), (0,)), ((), ())), preferred_element_type=F32)  61.9 us
    dot_general x8, matrix products, dot(): return jnp.dot(a, b, preferred_element_type=F32)  61.2 us
    pallas_call x2, Pallas kernels, attend_back(): pl.pallas_call(attend_back_kernel, grid_spec=pltpu.PrefetchScalarGridSpec...  43.5 us
  transfers between devices with their start and end apart: 93, of which 37 were waited for; matrix products, arithmetic and copies ran while one was open for 28% of the time, Pallas kernels for 6%

profile of v1, /device:TPU:0, one launch (start us, length us, event | category | flops | bytes accessed | tf_op | source)
XLA Modules:
  0.0 1060.4 jit_solution(4530805567175832971)
XLA Ops:
  85.7 13.2 %collective-permute-done.9 = bf16[2,2,48,2176]{3,2,1,0:T(8,128)(2,1)S(1)} collective-permute-done((bf16[2,2,48,2176]{3,2,1,0:T(8,128)(2,1)S(1)}, bf16[2,2,48,2176]{3,2,1,0:T(8,128)(2,1)S(1)}, u32[]{:S(2)}, u32[]{:S(2)}) %collective-permute-start.9) | collective-permute-done | bytes 835616 | tf_op jit(solution)/shard_map/ppermute | solution.py:53
  119.5 10.5 collective-permute-done.20
  181.5 16.6 %all-gather.7.cloned.1.call-done.k_ref.v_ref = bf16[1536,512]{1,0:T(8,128)(2,1)} async-done(((bf16[192,512]{1,0:T(8,128)(2,1)}), bf16[1536,512]{1,0:T(8,128)(2,1)}) %all-gather.7.cloned.1.call-update) | async-done | bytes 1572880 | tf_op jit(solution)/shard_map/all_gather | solution.py:398
  198.1 14.3 %shard_map.258 = (bf16[192,1536]{1,0:T(8,128)(2,1)}, f32[192,1536]{1,0:T(8,128)}) custom-call(s32[2]{0:T(128)} %pad_add_fusion.info_ref, bf16[384,2048]{1,0:T(8,128)(2,1)} %shard_map.257.q_ref, bf16[1536,512]{1,0:T(8,128)(2,1)} %all-gather.7.cloned.1.call-done.k_ref.v_ref, bf16[1536,512]{1,0:T(8,128)(2,1)} %all-gather.7.cloned.1.call-done.k_ref.v_ref), custom_call_target="tpu_custom_call" | custom-call | flops 3623878656 | bytes 3932160 | tf_op jit(solution)/shard_map/pallas_call | solution.py:219
  222.6 46.0 %all-gather.9.cloned.1.call-done = bf16[1536,1536]{1,0:T(8,128)(2,1)} async-done(((bf16[192,1536]{1,0:T(8,128)(2,1)}), bf16[1536,1536]{1,0:T(8,128)(2,1)}) %all-gather.9.cloned.1.call-update) | async-done | bytes 4718608 | tf_op jit(solution)/shard_map/all_gather | solution.py:407
  268.6 10.0 fusion.163
  286.1 35.3 %all-gather.15.cloned.1.call-done = bf16[1536,1536]{1,0:T(8,128)(2,1)} async-done(((bf16[192,1536]{1,0:T(8,128)(2,1)}), bf16[1536,1536]{1,0:T(8,128)(2,1)}) %all-gather.15.cloned.1.call-update) | async-done | bytes 4718608 | tf_op jit(solution)/shard_map/all_gather | solution.py:385
  321.3 15.1 %multiply_convert_fusion.2 = (bf16[1536,1120]{0,1:T(8,128)(2,1)}, bf16[1536,1120]{0,1:T(8,128)(2,1)S(1)}, bf16[1536,1120]{0,1:T(8,128)(2,1)S(1)}) fusion(f32[1536,1120]{0,1:T(8,128)} %fusion.163, f32[1536,1120]{0,1:T(8,128)} %fusion.164, bf16[1536,1536]{1,0:T(8,128)(2,1)} %all-gather.15.cloned.1.call-done, bf16[1120,1536]{1,0:T(8,128)(2,1)} %param.38), kind=kOutput, calls=%fused_computation.16 | convolution fusion | flops 5310627840 | bytes 32243712 | tf_op jit(solution)/shard_map/dot_general | solution.py:32
  376.0 21.1 %collective-permute-done.37 = bf16[192,1536]{1,0:T(8,128)(2,1)} collective-permute-done((bf16[192,1536]{1,0:T(8,128)(2,1)}, bf16[192,1536]{1,0:T(8,128)(2,1)}, u32[]{:S(2)}, u32[]{:S(2)}) %collective-permute-start.37) | collective-permute-done | bytes 589856 | tf_op jit(solution)/shard_map/ppermute | solution.py:87
  404.8 15.6 %collective-permute-done.23 = bf16[192,1536]{1,0:T(8,128)(2,1)} collective-permute-done((bf16[192,1536]{1,0:T(8,128)(2,1)}, bf16[192,1536]{1,0:T(8,128)(2,1)}, u32[]{:S(2)}, u32[]{:S(2)}) %collective-permute-start.23) | collective-permute-done | bytes 589856 | tf_op jit(solution)/shard_map/ppermute | solution.py:87
  457.9 13.9 %shard_map.259 = (bf16[192,1536]{1,0:T(8,128)(2,1)}, f32[192,1536]{1,0:T(8,128)}) custom-call(s32[2]{0:T(128)} %pad_add_fusion.1.info_ref, bf16[384,2048]{1,0:T(8,128)(2,1)} %shard_map.257.q_ref, bf16[1536,512]{1,0:T(8,128)(2,1)} %all-gather.11.cloned.1.call-done.k_ref.v_ref, bf16[1536,512]{1,0:T(8,128)(2,1)} %all-gather.11.cloned.1.call-done.k_ref.v_ref), custom_call_target="tpu_custom_call" | custom-call | flops 3623878656 | bytes 3932160 | tf_op jit(solution)/shard_map/pallas_call | solution.py:219
  475.9 10.2 collective-permute-start.25
  519.2 10.6 fusion.167
  529.8 40.1 %all-gather.13.cloned.1.call-done = bf16[1536,1536]{1,0:T(8,128)(2,1)} async-done(((bf16[192,1536]{1,0:T(8,128)(2,1)}), bf16[1536,1536]{1,0:T(8,128)(2,1)}) %all-gather.13.cloned.1.call-update) | async-done | bytes 4718608 | tf_op jit(solution)/shard_map/all_gather | solution.py:407
  569.9 10.8 %fusion.165 = f32[1536,1120]{0,1:T(8,128)} fusion(bf16[1536,1536]{1,0:T(8,128)(2,1)} %all-gather.13.cloned.1.call-done, bf16[1536,1120]{0,1:T(8,128)(2,1)} %param.37), kind=kOutput, calls=%fused_computation.413 | convolution fusion | flops 5284823040 | bytes 15040512 | tf_op jit(solution)/shard_map/dot_general | solution.py:28
  580.6 12.9 %multiply_convert_fusion = (bf16[1536,1120]{0,1:T(8,128)(2,1)}, bf16[1536,1120]{0,1:T(8,128)(2,1)}, bf16[1536,1120]{0,1:T(8,128)(2,1)}) fusion(f32[1536,1120]{0,1:T(8,128)S(1)} %copy-done.88, f32[1536,1120]{0,1:T(8,128)} %fusion.165, bf16[1536,1536]{1,0:T(8,128)(2,1)S(1)} %copy-done.82, bf16[1536,1120]{0,1:T(8,128)(2,1)S(1)} %copy-done), kind=kOutput, calls=%fused_computation.14 | convolution fusion | flops 5310627840 | bytes 32243712 | tf_op jit(solution)/shard_map/dot_general | solution.py:28
  593.6 11.0 %fusion.168 = f32[1536,1536]{1,0:T(8,128)} fusion(bf16[1536,1120]{0,1:T(8,128)(2,1)} %get-tuple-element.160, bf16[1536,1120]{0,1:T(8,128)(2,1)S(1)} %copy-done), kind=kOutput, calls=%fused_computation.416 | convolution fusion | flops 5284823040 | bytes 16318464 | tf_op jit(solution)/shard_map/dot_general | solution.py:32
  689.0 10.0 collective-permute-done.31
  770.4 21.7 %shard_map.261 = (bf16[192,1536]{1,0:T(8,128)(2,1)}, bf16[1536,256]{1,0:T(8,128)(2,1)}, bf16[1536,256]{1,0:T(8,128)(2,1)}) custom-call(s32[2]{0:T(128)} %pad_add_fusion.1.info_ref, bf16[384,2048]{1,0:T(8,128)(2,1)} %shard_map.257.q_ref, bf16[1536,512]{1,0:T(8,128)(2,1)} %all-gather.11.cloned.1.call-done.k_ref.v_ref, ...), custom_call_target="tpu_custom_call" | custom-call | flops 9059696640 | bytes 6684672 | tf_op jit(solution)/shard_map/pallas_call | solution.py:289
  793.8 21.7 %shard_map.260 = (bf16[192,1536]{1,0:T(8,128)(2,1)}, bf16[1536,256]{1,0:T(8,128)(2,1)}, bf16[1536,256]{1,0:T(8,128)(2,1)}) custom-call(s32[2]{0:T(128)} %pad_add_fusion.info_ref, bf16[384,2048]{1,0:T(8,128)(2,1)} %shard_map.257.q_ref, bf16[1536,512]{1,0:T(8,128)(2,1)} %all-gather.7.cloned.1.call-done.k_ref.v_ref, ...), custom_call_target="tpu_custom_call" | custom-call | flops 9059696640 | bytes 6684672 | tf_op jit(solution)/shard_map/pallas_call | solution.py:289
  858.9 14.3 %collective-permute-done.63 = bf16[192,512]{1,0:T(8,128)(2,1)S(1)} collective-permute-done((bf16[192,512]{1,0:T(8,128)(2,1)S(1)}, bf16[192,512]{1,0:T(8,128)(2,1)S(1)}, u32[]{:S(2)}, u32[]{:S(2)}) %collective-permute-start.63) | collective-permute-done | bytes 196640 | tf_op jit(solution)/shard_map/ppermute | solution.py:90
  911.2 22.9 %collective-permute-done.76 = bf16[2,2,48,1536]{3,2,1,0:T(8,128)(2,1)S(1)} collective-permute-done((bf16[2,2,48,1536]{3,2,1,0:T(8,128)(2,1)S(1)}, bf16[2,2,48,1536]{3,2,1,0:T(8,128)(2,1)S(1)}, u32[]{:S(2)}, u32[]{:S(2)}) %collective-permute-start.76) | collective-permute-done | bytes 589856 | tf_op jit(solution)/shard_map/ppermute | solution.py:53
  940.1 10.9 %collective-permute-done.77 = bf16[2,48,1536]{2,1,0:T(8,128)(2,1)S(1)} collective-permute-done((bf16[2,48,1536]{2,1,0:T(8,128)(2,1)S(1)}, bf16[2,48,1536]{2,1,0:T(8,128)(2,1)S(1)}, u32[]{:S(2)}, u32[]{:S(2)}) %collective-permute-start.77) | collective-permute-done | bytes 294944 | tf_op jit(solution)/shard_map/ppermute | solution.py:53
  961.0 30.1 %collective-permute-done.65 = bf16[2,2,48,2176]{3,2,1,0:T(8,128)(2,1)S(1)} collective-permute-done((bf16[2,2,48,2176]{3,2,1,0:T(8,128)(2,1)S(1)}, bf16[2,2,48,2176]{3,2,1,0:T(8,128)(2,1)S(1)}, u32[]{:S(2)}, u32[]{:S(2)}) %collective-permute-start.65) | collective-permute-done | bytes 835616 | tf_op jit(solution)/shard_map/ppermute | solution.py:53
  (614 shorter events, 604.7 us)
Async XLA Ops:
  7.2 190.9 %all-gather.7.cloned.1.call-start = ((), (), s32[]{:S(2)}) async-start(), calls=%async_computation | async-start | bytes 1769472 | tf_op jit(solution)/shard_map/all_gather | solution.py:398
  72.0 37.3 %collective-permute-start.19 = (bf16[2,48,1536]{2,1,0:T(8,128)(2,1)}, bf16[2,48,1536]{2,1,0:T(8,128)(2,1)}, u32[]{:S(2)}, u32[]{:S(2)}) collective-permute-start(bf16[2,48,1536]{2,1,0:T(8,128)(2,1)} %get-tuple-element.201), channel_id=1, source_target_pairs={{0,16},{8,24},{16,0},{24,8},{1,17},{9,25},{17,1},{25,9},{2,18},{10... | collective-permute-start | bytes 884744 | tf_op jit(solution)/shard_map/ppermute | solution.py:53
  105.3 29.2 %collective-permute-start.10 = (bf16[2,2,4,48,2176]{4,3,2,0,1:T(8,128)(2,1)}, bf16[2,2,4,48,2176]{4,3,2,0,1:T(8,128)(2,1)}, u32[]{:S(2)}, u32[]{:S(2)}) collective-permute-start(bf16[2,2,4,48,2176]{4,3,2,0,1:T(8,128)(2,1)} %pad_maximum_fusion.1), channel_id=1, source_target_pairs={{0,1},{1,0},{2,3},{3,2},{4,5},{5,4},{6,7},{7,6},{8,9},{9,8},{10,11... | collective-permute-start | bytes 10027016 | tf_op jit(solution)/shard_map/ppermute | solution.py:53
  134.5 42.6 %collective-permute-start.21 = (bf16[2,2,4,48,1536]{4,3,2,1,0:T(8,128)(2,1)}, bf16[2,2,4,48,1536]{4,3,2,1,0:T(8,128)(2,1)}, u32[]{:S(2)}, u32[]{:S(2)}) collective-permute-start(bf16[2,2,4,48,1536]{4,3,2,1,0:T(8,128)(2,1)} %pad_maximum_fusion.2), channel_id=1, source_target_pairs={{0,1},{1,0},{2,3},{3,2},{4,5},{5,4},{6,7},{7,6},{8,9},{9,8},{10,11... | collective-permute-start | bytes 7077896 | tf_op jit(solution)/shard_map/ppermute | solution.py:53
  171.7 96.8 %all-gather.9.cloned.1.call-start = ((), (), s32[]{:S(2)}) async-start(), calls=%async_computation.1 | async-start | bytes 5308416 | tf_op jit(solution)/shard_map/all_gather | solution.py:407
  217.2 104.2 %all-gather.15.cloned.1.call-start = ((), (), s32[]{:S(2)}) async-start(), calls=%async_computation.4 | async-start | bytes 5308416 | tf_op jit(solution)/shard_map/all_gather | solution.py:385
  221.4 236.5 %all-gather.11.cloned.1.call-start = ((), (), s32[]{:S(2)}) async-start(), calls=%async_computation.2 | async-start | bytes 1769472 | tf_op jit(solution)/shard_map/all_gather | solution.py:398
  221.9 297.3 %all-gather.17.cloned.1.call-start = ((), (), s32[]{:S(2)}) async-start(), calls=%async_computation.5 | async-start | bytes 5308416 | tf_op jit(solution)/shard_map/all_gather | solution.py:385
  222.5 347.3 %all-gather.13.cloned.1.call-start = ((), (), s32[]{:S(2)}) async-start(), calls=%async_computation.3 | async-start | bytes 5308416 | tf_op jit(solution)/shard_map/all_gather | solution.py:407
  373.6 46.8 %collective-permute-start.23 = (bf16[192,1536]{1,0:T(8,128)(2,1)}, bf16[192,1536]{1,0:T(8,128)(2,1)}, u32[]{:S(2)}, u32[]{:S(2)}) collective-permute-start(bf16[192,1536]{1,0:T(8,128)(2,1)} %fusion.62), channel_id=1, source_target_pairs={{0,2},{1,3},{8,10},{9,11},{16,18},{17,19},{24,26},{25,27}} | collective-permute-start | bytes 1769480 | tf_op jit(solution)/shard_map/ppermute | solution.py:87
  399.6 33.4 %collective-permute-start.38 = (bf16[192,1536]{1,0:T(8,128)(2,1)}, bf16[192,1536]{1,0:T(8,128)(2,1)}, u32[]{:S(2)}, u32[]{:S(2)}) collective-permute-start(bf16[192,1536]{1,0:T(8,128)(2,1)} %fusion.38), channel_id=1, source_target_pairs={{0,2},{1,3},{2,4},{3,5},{8,10},{9,11},{10,12},{11,13},{16,18},{17,... | collective-permute-start | bytes 1769480 | tf_op jit(solution)/shard_map/ppermute | solution.py:87
  452.6 33.5 %collective-permute-start.41 = (bf16[192,1536]{1,0:T(8,128)(2,1)}, bf16[192,1536]{1,0:T(8,128)(2,1)}, u32[]{:S(2)}, u32[]{:S(2)}) collective-permute-start(bf16[192,1536]{1,0:T(8,128)(2,1)} %fusion.33), channel_id=1, source_target_pairs={{7,5},{6,4},{5,3},{4,2},{15,13},{14,12},{13,11},{12,10},{23,21},{2... | collective-permute-start | bytes 1769480 | tf_op jit(solution)/shard_map/ppermute | solution.py:90
  456.3 32.7 %collective-permute-start.27 = (bf16[192,1536]{1,0:T(8,128)(2,1)}, bf16[192,1536]{1,0:T(8,128)(2,1)}, u32[]{:S(2)}, u32[]{:S(2)}) collective-permute-start(bf16[192,1536]{1,0:T(8,128)(2,1)} %fusion.59), channel_id=1, source_target_pairs={{7,5},{6,4},{5,3},{4,2},{15,13},{14,12},{13,11},{12,10},{23,21},{2... | collective-permute-start | bytes 1769480 | tf_op jit(solution)/shard_map/ppermute | solution.py:90
  518.5 517.1 %all-reduce.5.cloned.1.call-start = ((), (), s32[]{:S(2)}) async-start(), calls=%async_computation.6 | async-start | bytes 20643840 | tf_op jit(solution)/shard_map/psum | solution.py:433
  614.7 31.0 %collective-permute-start.43 = (bf16[4,192,1536]{2,1,0:T(8,128)(2,1)S(1)}, bf16[4,192,1536]{2,1,0:T(8,128)(2,1)S(1)}, u32[]{:S(2)}, u32[]{:S(2)}) collective-permute-start(bf16[4,192,1536]{2,1,0:T(8,128)(2,1)S(1)} %dynamic-slice_bitcast_fusion.2), channel_id=1, source_target_pairs={{0,1},{1,0},{2,3},{3,2},{4,5},{5,4},{6,7},{7,6},{8,9},{9,8},{10,11... | collective-permute-start | bytes 7077896 | tf_op jit(solution)/shard_map/ppermute | solution.py:53
  793.7 31.0 %collective-permute-start.57 = (bf16[4,192,512]{2,1,0:T(8,128)(2,1)S(1)}, bf16[4,192,512]{2,1,0:T(8,128)(2,1)S(1)}, u32[]{:S(2)}, u32[]{:S(2)}) collective-permute-start(bf16[4,192,512]{2,1,0:T(8,128)(2,1)S(1)} %dynamic-slice_bitcast_fusion.8), channel_id=1, source_target_pairs={{0,1},{1,0},{2,3},{3,2},{4,5},{5,4},{6,7},{7,6},{8,9},{9,8},{10,11... | collective-permute-start | bytes 2359304 | tf_op jit(solution)/shard_map/ppermute | solution.py:53
  823.6 79.0 %collective-permute-start.75 = (bf16[2,2,4,48,1536]{4,3,2,1,0:T(8,128)(2,1)}, bf16[2,2,4,48,1536]{4,3,2,1,0:T(8,128)(2,1)}, u32[]{:S(2)}, u32[]{:S(2)}) collective-permute-start(bf16[2,2,4,48,1536]{4,3,2,1,0:T(8,128)(2,1)} %dynamic-slice_bitcast_fusion.1), channel_id=1, source_target_pairs={{0,1},{1,0},{2,3},{3,2},{4,5},{5,4},{6,7},{7,6},{8,9},{9,8},{10,11... | collective-permute-start | bytes 7077896 | tf_op jit(solution)/shard_map/ppermute | solution.py:53
  902.2 48.8 %collective-permute-start.64 = (bf16[2,2,4,48,2176]{4,3,2,1,0:T(8,128)(2,1)S(1)}, bf16[2,2,4,48,2176]{4,3,2,1,0:T(8,128)(2,1)S(1)}, u32[]{:S(2)}, u32[]{:S(2)}) collective-permute-start(bf16[2,2,4,48,2176]{4,3,2,1,0:T(8,128)(2,1)S(1)} %dynamic-slice_bitcast_fusion), channel_id=1, source_target_pairs={{0,1},{1,0},{2,3},{3,2},{4,5},{5,4},{6,7},{7,6},{8,9},{9,8},{10,11... | collective-permute-start | bytes 10027016 | tf_op jit(solution)/shard_map/ppermute | solution.py:53
  905.5 28.6 %collective-permute-start.76 = (bf16[2,2,48,1536]{3,2,1,0:T(8,128)(2,1)S(1)}, bf16[2,2,48,1536]{3,2,1,0:T(8,128)(2,1)S(1)}, u32[]{:S(2)}, u32[]{:S(2)}) collective-permute-start(bf16[2,2,48,1536]{3,2,1,0:T(8,128)(2,1)S(1)} %dynamic-slice_bitcast_fusion.11), channel_id=1, source_target_pairs={{0,8},{8,0},{16,24},{24,16},{1,9},{9,1},{17,25},{25,17},{2,10},{10... | collective-permute-start | bytes 1769480 | tf_op jit(solution)/shard_map/ppermute | solution.py:53
  909.7 28.9 %collective-permute-start.78 = (bf16[2,2,48,1536]{3,2,1,0:T(8,128)(2,1)S(1)}, bf16[2,2,48,1536]{3,2,1,0:T(8,128)(2,1)S(1)}, u32[]{:S(2)}, u32[]{:S(2)}) collective-permute-start(bf16[2,2,48,1536]{3,2,1,0:T(8,128)(2,1)S(1)} %dynamic-slice_bitcast_fusion.10), channel_id=1, source_target_pairs={{0,16},{8,24},{16,0},{24,8},{1,17},{9,25},{17,1},{25,9},{2,18},{10... | collective-permute-start | bytes 1769480 | tf_op jit(solution)/shard_map/ppermute | solution.py:53
  952.3 38.9 %collective-permute-start.65 = (bf16[2,2,48,2176]{3,2,1,0:T(8,128)(2,1)S(1)}, bf16[2,2,48,2176]{3,2,1,0:T(8,128)(2,1)S(1)}, u32[]{:S(2)}, u32[]{:S(2)}) collective-permute-start(bf16[2,2,48,2176]{3,2,1,0:T(8,128)(2,1)S(1)} %dynamic-slice_bitcast_fusion.7), channel_id=1, source_target_pairs={{0,8},{8,0},{16,24},{24,16},{1,9},{9,1},{17,25},{25,17},{2,10},{10... | collective-permute-start | bytes 2506760 | tf_op jit(solution)/shard_map/ppermute | solution.py:53
  954.6 55.5 %collective-permute-start.80 = (bf16[48,1536]{1,0:T(8,128)(2,1)S(1)}, bf16[48,1536]{1,0:T(8,128)(2,1)S(1)}, u32[]{:S(2)}, u32[]{:S(2)}) collective-permute-start(bf16[48,1536]{1,0:T(8,128)(2,1)S(1)} %get-tuple-element.216), channel_id=1, source_target_pairs={{0,2},{1,3},{8,10},{9,11},{16,18},{17,19},{24,26},{25,27}} | collective-permute-start | bytes 442376 | tf_op jit(solution)/shard_map/ppermute | solution.py:87
  958.5 51.6 %collective-permute-start.83 = (bf16[48,1536]{1,0:T(8,128)(2,1)S(1)}, bf16[48,1536]{1,0:T(8,128)(2,1)S(1)}, u32[]{:S(2)}, u32[]{:S(2)}) collective-permute-start(bf16[48,1536]{1,0:T(8,128)(2,1)S(1)} %get-tuple-element.217), channel_id=1, source_target_pairs={{7,5},{6,4},{15,13},{14,12},{23,21},{22,20},{31,29},{30,28}} | collective-permute-start | bytes 442376 | tf_op jit(solution)/shard_map/ppermute | solution.py:90
  959.4 36.9 %collective-permute-start.67 = (bf16[2,2,48,2176]{3,2,1,0:T(8,128)(2,1)S(1)}, bf16[2,2,48,2176]{3,2,1,0:T(8,128)(2,1)S(1)}, u32[]{:S(2)}, u32[]{:S(2)}) collective-permute-start(bf16[2,2,48,2176]{3,2,1,0:T(8,128)(2,1)S(1)} %dynamic-slice_bitcast_fusion.6), channel_id=1, source_target_pairs={{0,16},{8,24},{16,0},{24,8},{1,17},{9,25},{17,1},{25,9},{2,18},{10... | collective-permute-start | bytes 2506760 | tf_op jit(solution)/shard_map/ppermute | solution.py:53
  (177 other events, 3311.6 us)
Sparse Core Ops, SparseCore 0:
  171.8 26.2 all-gather.6
  217.3 51.2 all-gather.8
  270.8 50.5 all-gather.14
  323.4 23.8 all-gather.10
  348.8 69.5 all-gather.16
  518.7 51.1 all-gather.12
  746.8 248.7 all-reduce.4

commit v2 on v1

--- a/solution.py
+++ b/solution.py
@@ -22,6 +22,7 @@
 F32 = jnp.float32
 B16 = jnp.bfloat16
 VMEM_LIMIT = 56 * 1024 * 1024
+MESH = pl.DeviceIdType.MESH
 
 
 def dot(a, b):
@@ -55,24 +56,6 @@
 
 def pick(value, index, axis=0):
     return lax.dynamic_index_in_dim(value, index, axis, keepdims=False)
-
-
-def ordered(mine, other, index):
-    first = index == 0
-    return jnp.stack([jnp.where(first, mine, other), jnp.where(first, other, mine)])
-
-
-def line_gather(block, chips, place):
-    count = 2 * chips
-    from_left, from_right = [], []
-    left = right = block
-    for step in range(1, chips):
-        left = lax.ppermute(left, "tensor", [(i, i + 2) for i in range(count - 2)])
-        right = lax.ppermute(right, "tensor", [(i + 2, i) for i in range(count - 2)])
-        from_left.append(left)
-        from_right.append(right)
-    window = jnp.stack(from_left[::-1] + [block] + from_right)
-    return lax.dynamic_slice_in_dim(window, chips - 1 - place, chips, 0)
 
 
 def line_scatter(part, chips, place):
@@ -110,53 +93,288 @@
     return line_scatter(part, chips, chip)
 
 
-def gather_weights(block):
+def nearest(chips, place, step):
+    found = 0
+    for here in range(chips):
+        order = sorted(range(chips), key=lambda there: abs(there - here))
+        found = found + jnp.where(place == here, order[step], 0)
+    return found
+
+
+class Spot:
+    def __init__(self):
+        self.chips = lax.axis_size("tensor") // 2
+        dp, tensor = lax.axis_index("dp"), lax.axis_index("tensor")
+        self.dp, self.tensor = dp, tensor
+        self.row, self.col = dp // 2, dp % 2
+        self.chip, self.core = tensor // 2, tensor % 2
+        self.over_x = (self.row * 2 + 1 - self.col, tensor)
+        self.over_y = ((1 - self.row) * 2 + self.col, tensor)
+        self.beside = (dp, self.chip * 2 + 1 - self.core)
+        self.left = (dp, jnp.maximum(tensor - 2, 0))
+        self.right = (dp, jnp.minimum(tensor + 2, 2 * self.chips - 1))
+
+    def on_line(self, chip):
+        return (self.dp, chip * 2 + self.core)
+
+    def index(self, row, col, chip, core):
+        return ((row * 2 + col) * self.chips + chip) * 2 + core
+
+
+def greet(spot, plane, line):
+    barrier = pltpu.get_barrier_semaphore()
+    peers = [spot.beside] + ([spot.over_x, spot.over_y] if plane else [])
+    for peer in peers:
+        pl.semaphore_signal(barrier, inc=1, device_id=peer, device_id_type=MESH)
+    count = len(peers)
+    if line == "all":
+        for chip in range(spot.chips):
+
+            @pl.when(spot.chip != chip)
+            def _():
+                pl.semaphore_signal(barrier, inc=1, device_id=spot.on_line(chip), device_id_type=MESH)
+
+        count = count + spot.chips - 1
+    else:
+        has_left, has_right = spot.chip > 0, spot.chip < spot.chips - 1
+
+        @pl.when(has_left)
+        def _():
+            pl.semaphore_signal(barrier, inc=1, device_id=spot.left, device_id_type=MESH)
+
+        @pl.when(has_right)
+        def _():
+            pl.semaphore_signal(barrier, inc=1, device_id=spot.right, device_id_type=MESH)
+
+        count = count + jnp.where(has_left, 1, 0) + jnp.where(has_right, 1, 0)
+    pl.semaphore_wait(barrier, count)
+
+
+def remote(src, dst, send_sem, recv_sem, device):
+    return pltpu.make_async_remote_copy(
+        src_ref=src,
+        dst_ref=dst,
+        send_sem=send_sem,
+        recv_sem=recv_sem,
+        device_id=device,
+        device_id_type=MESH,
+    )
+
+
+def gather_kernel(block_ref, whole_ref, local_sem, send_sem, recv_sem):
+    spot = Spot()
+    chips, chip, core, row, col = spot.chips, spot.chip, spot.core, spot.row, spot.col
+    cut = chips // 2
+    own = spot.index(row, col, chip, core)
+    local = pltpu.make_async_copy(block_ref, whole_ref.at[own], local_sem)
+    local.start()
+    greet(spot, True, "near")
+    local.wait()
+    sent = []
+
+    def send(index, device, when=None):
+        copy = remote(
+            whole_ref.at[index], whole_ref.at[index], send_sem.at[len(sent)], recv_sem.at[index], device
+        )
+        sent.append((copy, when))
+        if when is None:
+            copy.start()
+        else:
+            pl.when(when)(copy.start)
+
+    def arrive(index):
+        remote(
+            whole_ref.at[index], whole_ref.at[index], send_sem.at[0], recv_sem.at[index], spot.beside
+        ).wait_recv()
+
+    order = [nearest(chips, chip, step) for step in range(chips)]
+    for step, there in enumerate(order):
+        index = spot.index(row, col, there, core)
+        if step:
+            arrive(index)
+        send(index, spot.right, (there <= chip) & (chip < chips - 1))
+        send(index, spot.left, (there >= chip) & (chip > 0))
+        send(index, spot.over_x)
+        send(index, spot.over_y)
+        send(index, spot.beside)
+    for there in order:
+        index = spot.index(row, 1 - col, there, core)
+        arrive(index)
+        send(index, spot.over_y, there < cut)
+        send(index, spot.beside)
+        index = spot.index(1 - row, col, there, core)
+        arrive(index)
+        send(index, spot.over_x, there >= cut)
+        send(index, spot.beside)
+    for there in order:
+        index = spot.index(1 - row, 1 - col, there, core)
+        arrive(index)
+        send(index, spot.beside)
+    for plane in range(4):
+        for there in range(chips):
+            arrive(spot.index(plane // 2, plane % 2, there, 1 - core))
+    for copy, when in sent:
+        if when is None:
+            copy.wait_send()
+        else:
+            pl.when(when)(copy.wait_send)
+
+
+def gather_weights(block, collective_id):
     size, width = block.shape
     devices = lax.axis_size(("dp", "tensor"))
     if lax.axis_size("dp") != 4:
         return lax.all_gather(block, ("dp", "tensor"), axis=0, tiled=True)
-    tensor = lax.axis_index("tensor")
-    core = tensor % 2
     chips = lax.axis_size("tensor") // 2
-    line = line_gather(block, chips, tensor // 2)
-    row, col = lax.axis_index("dp") // 2, lax.axis_index("dp") % 2
+    whole = pl.pallas_call(
+        gather_kernel,
+        in_specs=[pl.BlockSpec(memory_space=pl.ANY)],
+        out_specs=pl.BlockSpec(memory_space=pl.ANY),
+        out_shape=jax.ShapeDtypeStruct((devices, size, width), B16),
+        scratch_shapes=[
+            pltpu.SemaphoreType.DMA,
+            pltpu.SemaphoreType.DMA((10 * chips,)),
+            pltpu.SemaphoreType.DMA((devices,)),
+        ],
+        compiler_params=pltpu.CompilerParams(
+            collective_id=collective_id, has_side_effects=True, vmem_limit_bytes=VMEM_LIMIT
+        ),
+        cost_estimate=pl.CostEstimate(flops=0, bytes_accessed=devices * size * width * 8, transcendentals=0),
+    )(block)
+    return whole.reshape(devices * size, width)
+
+
+def scatter_kernel(
+    grads_ref, out_ref, mine, got, over_x, over_y, across_x, across_y, line, load_sem, send_sem, recv_sem
+):
+    spot = Spot()
+    chips, chip, core, row, col = spot.chips, spot.chip, spot.core, spot.row, spot.col
     cut = chips // 2
-    one, two = line[:cut], line[cut:]
-    one = ordered(one, swap(one, "dp", 1), col)
-    two = ordered(two, swap(two, "dp", 2), row)
-    one = ordered(one, swap(one, "dp", 2), row)
-    two = ordered(two, swap(two, "dp", 1), col)
-    plane = jnp.concatenate([one, two.swapaxes(0, 1)], axis=2)
-    whole = ordered(plane, swap(plane, "tensor", 1), core)
-    whole = jnp.moveaxis(whole, 0, 3)
-    return whole.reshape(devices * size, width)
-
-
-def scatter_weights(grads):
+    load = pltpu.make_async_copy(grads_ref.at[:, core], mine, load_sem)
+    load.start()
+    greet(spot, True, "all")
+    swap_copy = remote(grads_ref.at[:, 1 - core], got, send_sem.at[0], recv_sem.at[0], spot.beside)
+    swap_copy.start()
+    load.wait()
+    swap_copy.wait()
+
+    def add(target, start, source, first, count):
+        def body(step, _):
+            target[start + step] = (
+                target[start + step].astype(F32) + source[first + step].astype(F32)
+            ).astype(B16)
+            return 0
+
+        lax.fori_loop(0, count, body, 0)
+
+    add(mine, 0, got, 0, 4 * chips)
+
+    def at(r, c, z):
+        return (r * 2 + c) * chips + z
+
+    copies = []
+    for side in range(2):
+        copies.append(
+            remote(
+                mine.at[pl.ds(at(side, 1 - col, 0), cut)],
+                over_x.at[pl.ds(side * cut, cut)],
+                send_sem.at[1 + side],
+                recv_sem.at[1 + side],
+                spot.over_x,
+            )
+        )
+        copies.append(
+            remote(
+                mine.at[pl.ds(at(1 - row, side, cut), chips - cut)],
+                over_y.at[pl.ds(side * (chips - cut), chips - cut)],
+                send_sem.at[3 + side],
+                recv_sem.at[3 + side],
+                spot.over_y,
+            )
+        )
+    for copy in copies:
+        copy.start()
+    for copy in copies:
+        copy.wait()
+    for side in range(2):
+        add(mine, at(side, col, 0), over_x, side * cut, cut)
+        add(mine, at(row, side, cut), over_y, side * (chips - cut), chips - cut)
+    copies = [
+        remote(
+            mine.at[pl.ds(at(1 - row, col, 0), cut)], across_y, send_sem.at[5], recv_sem.at[5], spot.over_y
+        ),
+        remote(
+            mine.at[pl.ds(at(row, 1 - col, cut), chips - cut)],
+            across_x,
+            send_sem.at[6],
+            recv_sem.at[6],
+            spot.over_x,
+        ),
+    ]
+    for copy in copies:
+        copy.start()
+    for copy in copies:
+        copy.wait()
+    add(mine, at(row, col, 0), across_y, 0, cut)
+    add(mine, at(row, col, cut), across_x, 0, chips - cut)
+
+    def to(other):
+        return remote(
+            mine.at[at(row, col, other)],
+            line.at[chip],
+            send_sem.at[7 + other],
+            recv_sem.at[7 + chip],
+            spot.on_line(other),
+        )
+
+    for other in range(chips):
+        pl.when(chip != other)(to(other).start)
+    total = mine[at(row, col, chip)].astype(F32)
+    line[chip] = jnp.zeros(line.shape[1:], B16)
+    for other in range(chips):
+
+        @pl.when(chip != other)
+        def _():
+            remote(
+                line.at[other], line.at[other], send_sem.at[7 + other], recv_sem.at[7 + other], spot.on_line(other)
+            ).wait_recv()
+
+        total = total + line[other].astype(F32)
+    out_ref[...] = total
+    for other in range(chips):
+        pl.when(chip != other)(to(other).wait_send)
+
+
+def scatter_weights(grads, collective_id):
     total, width = grads.shape
     devices = lax.axis_size(("dp", "tensor"))
     size = total // devices
     if lax.axis_size("dp") != 4:
         return lax.psum_scatter(grads, ("dp", "tensor"), scatter_dimension=0, tiled=True).astype(F32)
-    tensor = lax.axis_index("tensor")
-    core = tensor % 2
     chips = lax.axis_size("tensor") // 2
-    row, col = lax.axis_index("dp") // 2, lax.axis_index("dp") % 2
-    blocks = grads.reshape(2, 2, chips, 2, size, width)
     cut = chips // 2
-
-    def halve(value, index, axis, mesh_axis, bit):
-        got = swap(pick(value, 1 - index, axis), mesh_axis, bit)
-        return (pick(value, index, axis).astype(F32) + got.astype(F32)).astype(B16)
-
-    plane = halve(blocks, core, 3, "tensor", 1)
-    one, two = plane[:, :, :cut], plane[:, :, cut:]
-    one = halve(one, col, 1, "dp", 1)
-    two = halve(two, row, 0, "dp", 2)
-    one = halve(one, row, 0, "dp", 2)
-    two = halve(two, col, 0, "dp", 1)
-    line = jnp.concatenate([one, two], axis=0)
-    return line_scatter(lambda index: pick(line, index).astype(F32), chips, tensor // 2)
+    return pl.pallas_call(
+        scatter_kernel,
+        in_specs=[pl.BlockSpec(memory_space=pl.ANY)],
+        out_specs=pl.BlockSpec(memory_space=pltpu.VMEM),
+        out_shape=jax.ShapeDtypeStruct((size, width), F32),
+        scratch_shapes=[
+            pltpu.VMEM((4 * chips, size, width), B16),
+            pltpu.VMEM((4 * chips, size, width), B16),
+            pltpu.VMEM((2 * cut, size, width), B16),
+            pltpu.VMEM((2 * (chips - cut), size, width), B16),
+            pltpu.VMEM((chips - cut, size, width), B16),
+            pltpu.VMEM((cut, size, width), B16),
+            pltpu.VMEM((chips, size, width), B16),
+            pltpu.SemaphoreType.DMA,
+            pltpu.SemaphoreType.DMA((7 + chips,)),
+            pltpu.SemaphoreType.DMA((7 + chips,)),
+        ],
+        compiler_params=pltpu.CompilerParams(
+            collective_id=collective_id, has_side_effects=True, vmem_limit_bytes=VMEM_LIMIT
+        ),
+        cost_estimate=pl.CostEstimate(flops=0, bytes_accessed=devices * size * width * 8, transcendentals=0),
+    )(grads.reshape(devices // 2, 2, size, width))
 
 
 def project_kernel(hidden_ref, weight_ref, bias_ref, cos_ref, sin_ref, out_ref):
@@ -369,8 +587,10 @@
     extra = jnp.zeros((size, EXTRA), B16)
     extra = extra.at[:, 0].set(attn_gain).at[:, 1].set(query_bias).at[:, 2].set(mlp_gain)
     extra = extra.at[:small, 3].set(key_bias).at[small : 2 * small, 3].set(value_bias)
-    packed = gather_weights(jnp.concatenate([query_proj, key_proj, value_proj, extra], axis=1))
-    wout = gather_weights(out_proj)
+    packed = gather_weights(
+        jnp.concatenate([query_proj, key_proj, value_proj, extra], axis=1), 0
+    )
+    wout = gather_weights(out_proj, 1)
     vectors = packed[:, QKV : QKV + 4].astype(F32)
     gain_one, gain_two = vectors[:, 0], vectors[:, 2]
     tails = vectors[:, 3].reshape(devices, size)
@@ -466,8 +686,8 @@
     ).reshape(-1)
     columns = jnp.stack([gain_one_grad, grad_bias[:QW], sum(gain_two_grads), tails], axis=1)
     columns = jnp.pad(columns.astype(B16), ((0, 0), (0, EXTRA - 4)))
-    grad_out = scatter_weights(acc_out)
-    grad_packed = scatter_weights(jnp.concatenate([acc_qkv, columns], axis=1))
+    grad_out = scatter_weights(acc_out, 2)
+    grad_packed = scatter_weights(jnp.concatenate([acc_qkv, columns], axis=1), 3)
 
     layer_output = jnp.stack(
         [

time: 1070 us -> 995 us (0.930)
  Pallas kernels: 80.7 us -> 289 us
  waiting for transfers between devices: 398 us -> 263 us
  starting transfers between devices: 186 us -> 94.6 us
  other arithmetic: 117 us -> 88.4 us
  local copies, waits for them, and re-layouts: 63.3 us -> 36.8 us
    pallas_call x0 -> x4, Pallas kernels: none -> 208 us  [the longest x2 119 us: scatter_weights(): pl.pallas_call(scatter_kernel, in_specs=[pl.BlockSpec(memory_space=pl.ANY...]
    ppermute x26 -> x6, waiting for transfers between devices: 124 us -> 0.02 us  [swap(): return lax.ppermute(value, axis, [(i, i ^ bit) for i in range(count)])]
    ppermute x12 -> x0, starting transfers between devices: 36.3 us -> none  [the longest x6 28.4 us: line_gather(): left = lax.ppermute(left, 'tensor', [(i, i + 2) for i in range(count - 2)])]
    ppermute x24 -> x18, starting transfers between devices: 102 us -> 74.8 us  [line_scatter(): lax.ppermute(ahead.astype(B16), 'tensor', [(i, i + 2) for i in range(2 *...]
    ppermute x26 -> x6, starting transfers between devices: 23.8 us -> 1.52 us  [swap(): return lax.ppermute(value, axis, [(i, i ^ bit) for i in range(count)])]
    unnamed x227 -> x167, local copies, waits for them, and re-layouts: 27.7 us -> 10.6 us
    all_gather x2, waiting for transfers between devices: 16.6 us -> 0.01 us  [on_device(): lax.all_gather(qkv[m * rows:(m + 1) * rows, QW:], 'tensor', axis=0, tiled...]
    ppermute x24 -> x18, waiting for transfers between devices: 91.4 us -> 105 us  [line_scatter(): lax.ppermute(ahead.astype(B16), 'tensor', [(i, i + 2) for i in range(2 *...]
  transfers between devices with their start and end apart: 93 -> 49, of which waited for: 37 -> 20; matrix products, arithmetic and copies ran while one was open for 28% -> 24% of each run, Pallas kernels for 6% -> 22%
where the time goes in v2:
time: 995 us; the launch traced here: 986 us
  Pallas kernels  289 us (29%)
  waiting for transfers between devices  263 us (26%)
  matrix products  198 us (20%)
  starting transfers between devices  94.6 us (10%)
  other arithmetic  88.4 us (9%)
  local copies, waits for them, and re-layouts  36.8 us (4%)
  between operations  16 us (2%)
    pallas_call x2, Pallas kernels, scatter_weights(): pl.pallas_call(scatter_kernel, in_specs=[pl.BlockSpec(memory_space=pl.ANY...  119 us
    ppermute x18, waiting for transfers between devices, line_scatter(): lax.ppermute(ahead.astype(B16), 'tensor', [(i, i + 2) for i in range(2 *...  105 us
    pallas_call x2, Pallas kernels, gather_weights(): pl.pallas_call(gather_kernel, in_specs=[pl.BlockSpec(memory_space=pl.ANY)...  89 us
    all_gather x2, waiting for transfers between devices, on_device(): full_hidden.append(lax.all_gather(hidden_two, 'tensor', axis=0, tiled=True))  85.1 us
    ppermute x18, starting transfers between devices, line_scatter(): lax.ppermute(ahead.astype(B16), 'tensor', [(i, i + 2) for i in range(2 *...  74.8 us
    dot_general x9, matrix products, dot_t(): lax.dot_general(a, b, (((1,), (1,)), ((), ())), preferred_element_type=F32)  70.2 us
    dot_general x8, matrix products, t_dot(): lax.dot_general(a, b, (((0,), (0,)), ((), ())), preferred_element_type=F32)  65.3 us
    dot_general x8, matrix products, dot(): return jnp.dot(a, b, preferred_element_type=F32)  62.4 us
  transfers between devices with their start and end apart: 49, of which 20 were waited for; matrix products, arithmetic and copies ran while one was open for 24% of the time, Pallas kernels for 22%

profile of v2, /device:TPU:0, one launch (start us, length us, event | category | flops | bytes accessed | tf_op | source)
XLA Modules:
  0.0 985.8 jit_solution(12016191882352127493)
XLA Ops:
  22.0 45.1 %shard_map.257 = bf16[32,48,2176]{2,1,0:T(8,128)(2,1)} custom-call(bf16[48,2176]{1,0:T(8,128)(2,1)} %pad_maximum_fusion.3.block_ref), custom_call_target="tpu_custom_call" | custom-call | bytes 26738688 | tf_op jit(solution)/shard_map/pallas_call | solution.py:229
  90.9 43.8 %shard_map.260 = bf16[32,48,1536]{2,1,0:T(8,128)(2,1)} custom-call(bf16[48,1536]{1,0:T(8,128)(2,1)} %block_ref.1), custom_call_target="tpu_custom_call" | custom-call | bytes 18874368 | tf_op jit(solution)/shard_map/pallas_call | solution.py:229
  136.5 14.3 %shard_map.259 = (bf16[192,1536]{1,0:T(8,128)(2,1)}, f32[192,1536]{1,0:T(8,128)}) custom-call(s32[2]{0:T(128)} %pad_add_fusion.info_ref, bf16[384,2048]{1,0:T(8,128)(2,1)} %shard_map.258.q_ref, bf16[1536,512]{1,0:T(8,128)(2,1)} %all-gather.7.cloned.1.call-done.k_ref.v_ref, bf16[1536,512]{1,0:T(8,128)(2,1)} %all-gather.7.cloned.1.call-done.k_ref.v_ref), custom_call_target="tpu_custom_call" | custom-call | flops 3623878656 | bytes 3932160 | tf_op jit(solution)/shard_map/pallas_call | solution.py:437
  161.1 44.2 %all-gather.9.cloned.1.call-done = bf16[1536,1536]{1,0:T(8,128)(2,1)} async-done(((bf16[192,1536]{1,0:T(8,128)(2,1)}), bf16[1536,1536]{1,0:T(8,128)(2,1)}) %all-gather.9.cloned.1.call-update) | async-done | bytes 4718608 | tf_op jit(solution)/shard_map/all_gather | solution.py:627
  205.3 10.7 %fusion.113 = f32[1536,1120]{0,1:T(8,128)} fusion(bf16[1536,1536]{1,0:T(8,128)(2,1)} %all-gather.9.cloned.1.call-done, bf16[1536,1120]{0,1:T(8,128)(2,1)} %param.36), kind=kOutput, calls=%fused_computation.255 | convolution fusion | flops 5284823040 | bytes 15040512 | tf_op jit(solution)/shard_map/dot_general | solution.py:29
  223.6 34.5 %all-gather.15.cloned.1.call-done = bf16[1536,1536]{1,0:T(8,128)(2,1)} async-done(((bf16[192,1536]{1,0:T(8,128)(2,1)}), bf16[1536,1536]{1,0:T(8,128)(2,1)}) %all-gather.15.cloned.1.call-update) | async-done | bytes 4718608 | tf_op jit(solution)/shard_map/all_gather | solution.py:605
  258.1 13.5 %multiply_convert_fusion.2 = (bf16[1536,1120]{0,1:T(8,128)(2,1)}, bf16[1536,1120]{0,1:T(8,128)(2,1)S(1)}, bf16[1536,1120]{0,1:T(8,128)(2,1)S(1)}) fusion(f32[1536,1120]{0,1:T(8,128)} %fusion.113, f32[1536,1120]{0,1:T(8,128)} %fusion.114, bf16[1536,1536]{1,0:T(8,128)(2,1)} %all-gather.15.cloned.1.call-done, bf16[1120,1536]{1,0:T(8,128)(2,1)S(1)} %copy-done), kind=kOutput, calls=%fused_computation.16 | convolution fusion | flops 5310627840 | bytes 32243712 | tf_op jit(solution)/shard_map/dot_general | solution.py:33
  309.6 21.1 %collective-permute-done.1 = bf16[192,1536]{1,0:T(8,128)(2,1)} collective-permute-done((bf16[192,1536]{1,0:T(8,128)(2,1)}, bf16[192,1536]{1,0:T(8,128)(2,1)}, u32[]{:S(2)}, u32[]{:S(2)}) %collective-permute-start.1) | collective-permute-done | bytes 589856 | tf_op jit(solution)/shard_map/ppermute | solution.py:70
  338.4 17.6 %collective-permute-done.15 = bf16[192,1536]{1,0:T(8,128)(2,1)} collective-permute-done((bf16[192,1536]{1,0:T(8,128)(2,1)}, bf16[192,1536]{1,0:T(8,128)(2,1)}, u32[]{:S(2)}, u32[]{:S(2)}) %collective-permute-start.15) | collective-permute-done | bytes 589856 | tf_op jit(solution)/shard_map/ppermute | solution.py:70
  397.0 13.9 %shard_map.261 = (bf16[192,1536]{1,0:T(8,128)(2,1)}, f32[192,1536]{1,0:T(8,128)}) custom-call(s32[2]{0:T(128)} %pad_add_fusion.1.info_ref, bf16[384,2048]{1,0:T(8,128)(2,1)} %shard_map.258.q_ref, bf16[1536,512]{1,0:T(8,128)(2,1)} %all-gather.11.cloned.1.call-done.k_ref.v_ref, bf16[1536,512]{1,0:T(8,128)(2,1)} %all-gather.11.cloned.1.call-done.k_ref.v_ref), custom_call_target="tpu_custom_call" | custom-call | flops 3623878656 | bytes 3932160 | tf_op jit(solution)/shard_map/pallas_call | solution.py:437
  466.7 41.0 %all-gather.13.cloned.1.call-done = bf16[1536,1536]{1,0:T(8,128)(2,1)} async-done(((bf16[192,1536]{1,0:T(8,128)(2,1)}), bf16[1536,1536]{1,0:T(8,128)(2,1)}) %all-gather.13.cloned.1.call-update) | async-done | bytes 4718608 | tf_op jit(solution)/shard_map/all_gather | solution.py:627
  507.7 10.7 %fusion.115 = f32[1536,1120]{0,1:T(8,128)} fusion(bf16[1536,1536]{1,0:T(8,128)(2,1)} %all-gather.13.cloned.1.call-done, bf16[1536,1120]{0,1:T(8,128)(2,1)} %param.37), kind=kOutput, calls=%fused_computation.257 | convolution fusion | flops 5284823040 | bytes 15040512 | tf_op jit(solution)/shard_map/dot_general | solution.py:29
  518.4 13.3 %multiply_convert_fusion = (bf16[1536,1120]{0,1:T(8,128)(2,1)}, bf16[1536,1120]{0,1:T(8,128)(2,1)}, bf16[1536,1120]{0,1:T(8,128)(2,1)S(1)}) fusion(f32[1536,1120]{0,1:T(8,128)} %fusion.117, f32[1536,1120]{0,1:T(8,128)} %fusion.115, bf16[1536,1536]{1,0:T(8,128)(2,1)S(1)} %copy-done.61, bf16[1536,1120]{0,1:T(8,128)(2,1)S(1)} %copy-done.63), kind=kOutput, calls=%fused_computation.14 | convolution fusion | flops 5310627840 | bytes 32243712 | tf_op jit(solution)/shard_map/dot_general | solution.py:29
  551.1 10.7 %add_convert_fusion = bf16[1536,1536]{1,0:T(8,128)(2,1)S(1)} fusion(f32[1536,1536]{1,0:T(8,128)} %fusion.118, bf16[1536,1120]{0,1:T(8,128)(2,1)} %get-tuple-element.159, bf16[1536,1120]{0,1:T(8,128)(2,1)} %param.37), kind=kOutput, calls=%fused_computation.5 | convolution fusion | flops 5289541632 | bytes 21037056 | tf_op jit(solution)/shard_map/dot_general | solution.py:33
  562.3 11.2 %fusion.121 = f32[1536,1120]{0,1:T(8,128)} fusion(bf16[1536,1120]{0,1:T(8,128)(2,1)} %get-tuple-element.156, bf16[1536,1536]{1,0:T(8,128)(2,1)S(1)} %bitcast.473), kind=kOutput, calls=%fused_computation.263 | convolution fusion | flops 5284823040 | bytes 15040512 | tf_op jit(solution)/shard_map/dot_general | solution.py:37
  623.4 10.9 %collective-permute-done.23 = bf16[192,1536]{1,0:T(8,128)(2,1)S(1)} collective-permute-done((bf16[192,1536]{1,0:T(8,128)(2,1)S(1)}, bf16[192,1536]{1,0:T(8,128)(2,1)S(1)}, u32[]{:S(2)}, u32[]{:S(2)}) %collective-permute-start.23) | collective-permute-done | bytes 589856 | tf_op jit(solution)/shard_map/ppermute | solution.py:70
  636.2 10.2 %fusion.3 = bf16[1536,1120]{0,1:T(8,128)(2,1)} fusion(f32[1536,1120]{0,1:T(8,128)} %fusion.121, bf16[1536,1120]{0,1:T(8,128)(2,1)} %get-tuple-element.159, bf16[1536,1536]{1,0:T(8,128)(2,1)S(1)} %copy-done.61), kind=kOutput, calls=%fused_computation.9 | convolution fusion | flops 5288263680 | bytes 18481152 | tf_op jit(solution)/shard_map/dot_general | solution.py:37
  648.4 10.0 %fusion.2 = bf16[1536,1120]{0,1:T(8,128)(2,1)} fusion(f32[1536,1120]{0,1:T(8,128)} %fusion.120, bf16[1536,1120]{0,1:T(8,128)(2,1)} %get-tuple-element.160, bf16[1536,1536]{1,0:T(8,128)(2,1)S(1)} %copy-done.61), kind=kOutput, calls=%fused_computation.8 | convolution fusion | flops 5288263680 | bytes 18481152 | tf_op jit(solution)/shard_map/dot_general | solution.py:37
  688.8 11.1 %collective-permute-done.27 = bf16[192,1536]{1,0:T(8,128)(2,1)} collective-permute-done((bf16[192,1536]{1,0:T(8,128)(2,1)}, bf16[192,1536]{1,0:T(8,128)(2,1)}, u32[]{:S(2)}, u32[]{:S(2)}) %collective-permute-start.27) | collective-permute-done | bytes 589856 | tf_op jit(solution)/shard_map/ppermute | solution.py:73
  710.2 21.7 %shard_map.262 = (bf16[192,1536]{1,0:T(8,128)(2,1)}, bf16[1536,256]{1,0:T(8,128)(2,1)}, bf16[1536,256]{1,0:T(8,128)(2,1)}) custom-call(s32[2]{0:T(128)} %pad_add_fusion.info_ref, bf16[384,2048]{1,0:T(8,128)(2,1)} %shard_map.258.q_ref, bf16[1536,512]{1,0:T(8,128)(2,1)} %all-gather.7.cloned.1.call-done.k_ref.v_ref, ...), custom_call_target="tpu_custom_call" | custom-call | flops 9059696640 | bytes 6684672 | tf_op jit(solution)/shard_map/pallas_call | solution.py:507
  733.7 21.7 %shard_map.263 = (bf16[192,1536]{1,0:T(8,128)(2,1)}, bf16[1536,256]{1,0:T(8,128)(2,1)}, bf16[1536,256]{1,0:T(8,128)(2,1)}) custom-call(s32[2]{0:T(128)} %pad_add_fusion.1.info_ref, bf16[384,2048]{1,0:T(8,128)(2,1)} %shard_map.258.q_ref, bf16[1536,512]{1,0:T(8,128)(2,1)} %all-gather.11.cloned.1.call-done.k_ref.v_ref, ...), custom_call_target="tpu_custom_call" | custom-call | flops 9059696640 | bytes 6684672 | tf_op jit(solution)/shard_map/pallas_call | solution.py:507
  770.1 56.6 %shard_map.265 = f32[48,1536]{1,0:T(8,128)} custom-call(bf16[16,2,48,1536]{3,2,1,0:T(8,128)(2,1)} %bitcast.455), custom_call_target="tpu_custom_call" | custom-call | bytes 18874368 | tf_op jit(solution)/shard_map/pallas_call | solution.py:356
  855.7 9.9 %collective-permute-done.34 = bf16[192,512]{1,0:T(8,128)(2,1)S(1)} collective-permute-done((bf16[192,512]{1,0:T(8,128)(2,1)S(1)}, bf16[192,512]{1,0:T(8,128)(2,1)S(1)}, u32[]{:S(2)}, u32[]{:S(2)}) %collective-permute-start.34) | collective-permute-done | bytes 196640 | tf_op jit(solution)/shard_map/ppermute | solution.py:73
  893.3 62.7 %shard_map.264 = f32[48,2176]{1,0:T(8,128)} custom-call(bf16[16,2,48,2176]{3,2,1,0:T(8,128)(2,1)} %bitcast.412), custom_call_target="tpu_custom_call" | custom-call | bytes 26738688 | tf_op jit(solution)/shard_map/pallas_call | solution.py:356
  (417 shorter events, 409.2 us)
Async XLA Ops:
  7.2 129.3 %all-gather.7.cloned.1.call-start = ((), (), s32[]{:S(2)}) async-start(), calls=%async_computation | async-start | bytes 1769472 | tf_op jit(solution)/shard_map/all_gather | solution.py:618
  87.8 117.5 %all-gather.9.cloned.1.call-start = ((), (), s32[]{:S(2)}) async-start(), calls=%async_computation.1 | async-start | bytes 5308416 | tf_op jit(solution)/shard_map/all_gather | solution.py:627
  155.5 102.6 %all-gather.15.cloned.1.call-start = ((), (), s32[]{:S(2)}) async-start(), calls=%async_computation.4 | async-start | bytes 5308416 | tf_op jit(solution)/shard_map/all_gather | solution.py:605
  159.7 237.2 %all-gather.11.cloned.1.call-start = ((), (), s32[]{:S(2)}) async-start(), calls=%async_computation.2 | async-start | bytes 1769472 | tf_op jit(solution)/shard_map/all_gather | solution.py:618
  160.3 296.6 %all-gather.17.cloned.1.call-start = ((), (), s32[]{:S(2)}) async-start(), calls=%async_computation.5 | async-start | bytes 5308416 | tf_op jit(solution)/shard_map/all_gather | solution.py:605
  160.9 346.8 %all-gather.13.cloned.1.call-start = ((), (), s32[]{:S(2)}) async-start(), calls=%async_computation.3 | async-start | bytes 5308416 | tf_op jit(solution)/shard_map/all_gather | solution.py:627
  302.2 28.5 %collective-permute-start.1 = (bf16[192,1536]{1,0:T(8,128)(2,1)}, bf16[192,1536]{1,0:T(8,128)(2,1)}, u32[]{:S(2)}, u32[]{:S(2)}) collective-permute-start(bf16[192,1536]{1,0:T(8,128)(2,1)} %fusion.56), channel_id=1, source_target_pairs={{0,2},{1,3},{8,10},{9,11},{16,18},{17,19},{24,26},{25,27}} | collective-permute-start | bytes 1769480 | tf_op jit(solution)/shard_map/ppermute | solution.py:70
  307.2 48.8 %collective-permute-start.15 = (bf16[192,1536]{1,0:T(8,128)(2,1)}, bf16[192,1536]{1,0:T(8,128)(2,1)}, u32[]{:S(2)}, u32[]{:S(2)}) collective-permute-start(bf16[192,1536]{1,0:T(8,128)(2,1)} %fusion.30), channel_id=1, source_target_pairs={{0,2},{1,3},{8,10},{9,11},{16,18},{17,19},{24,26},{25,27}} | collective-permute-start | bytes 1769480 | tf_op jit(solution)/shard_map/ppermute | solution.py:70
  333.2 38.8 %collective-permute-start.2 = (bf16[192,1536]{1,0:T(8,128)(2,1)}, bf16[192,1536]{1,0:T(8,128)(2,1)}, u32[]{:S(2)}, u32[]{:S(2)}) collective-permute-start(bf16[192,1536]{1,0:T(8,128)(2,1)} %fusion.58), channel_id=1, source_target_pairs={{0,2},{1,3},{2,4},{3,5},{8,10},{9,11},{10,12},{11,13},{16,18},{17,... | collective-permute-start | bytes 1769480 | tf_op jit(solution)/shard_map/ppermute | solution.py:70
  358.5 25.9 %collective-permute-start.16 = (bf16[192,1536]{1,0:T(8,128)(2,1)}, bf16[192,1536]{1,0:T(8,128)(2,1)}, u32[]{:S(2)}, u32[]{:S(2)}) collective-permute-start(bf16[192,1536]{1,0:T(8,128)(2,1)} %fusion.32), channel_id=1, source_target_pairs={{0,2},{1,3},{2,4},{3,5},{8,10},{9,11},{10,12},{11,13},{16,18},{17,... | collective-permute-start | bytes 1769480 | tf_op jit(solution)/shard_map/ppermute | solution.py:70
  391.7 29.6 %collective-permute-start.5 = (bf16[192,1536]{1,0:T(8,128)(2,1)}, bf16[192,1536]{1,0:T(8,128)(2,1)}, u32[]{:S(2)}, u32[]{:S(2)}) collective-permute-start(bf16[192,1536]{1,0:T(8,128)(2,1)} %fusion.53), channel_id=1, source_target_pairs={{7,5},{6,4},{5,3},{4,2},{15,13},{14,12},{13,11},{12,10},{23,21},{2... | collective-permute-start | bytes 1769480 | tf_op jit(solution)/shard_map/ppermute | solution.py:73
  395.5 28.8 %collective-permute-start.19 = (bf16[192,1536]{1,0:T(8,128)(2,1)}, bf16[192,1536]{1,0:T(8,128)(2,1)}, u32[]{:S(2)}, u32[]{:S(2)}) collective-permute-start(bf16[192,1536]{1,0:T(8,128)(2,1)} %fusion.27), channel_id=1, source_target_pairs={{7,5},{6,4},{5,3},{4,2},{15,13},{14,12},{13,11},{12,10},{23,21},{2... | collective-permute-start | bytes 1769480 | tf_op jit(solution)/shard_map/ppermute | solution.py:73
  415.0 25.2 %collective-permute-start.17 = (bf16[192,1536]{1,0:T(8,128)(2,1)S(1)}, bf16[192,1536]{1,0:T(8,128)(2,1)S(1)}, u32[]{:S(2)}, u32[]{:S(2)}) collective-permute-start(bf16[192,1536]{1,0:T(8,128)(2,1)S(1)} %copy-done.40), channel_id=1, source_target_pairs={{0,2},{1,3},{2,4},{3,5},{4,6},{5,7},{8,10},{9,11},{10,12},{11,13},... | collective-permute-start | bytes 1769480 | tf_op jit(solution)/shard_map/ppermute | solution.py:70
  425.9 25.8 %collective-permute-start.20 = (bf16[192,1536]{1,0:T(8,128)(2,1)S(1)}, bf16[192,1536]{1,0:T(8,128)(2,1)S(1)}, u32[]{:S(2)}, u32[]{:S(2)}) collective-permute-start(bf16[192,1536]{1,0:T(8,128)(2,1)S(1)} %fusion.29), channel_id=1, source_target_pairs={{7,5},{6,4},{5,3},{4,2},{3,1},{2,0},{15,13},{14,12},{13,11},{12,10... | collective-permute-start | bytes 1769480 | tf_op jit(solution)/shard_map/ppermute | solution.py:73
  456.2 508.0 %all-reduce.5.cloned.1.call-start = ((), (), s32[]{:S(2)}) async-start(), calls=%async_computation.6 | async-start | bytes 20643840 | tf_op jit(solution)/shard_map/psum | solution.py:653
  538.5 42.4 %collective-permute-start.7 = (bf16[4,192,1536]{2,1,0:T(8,128)(2,1)S(1)}, bf16[4,192,1536]{2,1,0:T(8,128)(2,1)S(1)}, u32[]{:S(2)}, u32[]{:S(2)}) collective-permute-start(bf16[4,192,1536]{2,1,0:T(8,128)(2,1)S(1)} %dynamic-slice_bitcast_fusion.2), channel_id=1, source_target_pairs={{0,1},{1,0},{2,3},{3,2},{4,5},{5,4},{6,7},{7,6},{8,9},{9,8},{10,11... | collective-permute-start | bytes 7077896 | tf_op jit(solution)/shard_map/ppermute | solution.py:54
  583.6 26.1 %collective-permute-start.22 = (bf16[192,1536]{1,0:T(8,128)(2,1)S(1)}, bf16[192,1536]{1,0:T(8,128)(2,1)S(1)}, u32[]{:S(2)}, u32[]{:S(2)}) collective-permute-start(bf16[192,1536]{1,0:T(8,128)(2,1)S(1)} %fusion.18), channel_id=1, source_target_pairs={{0,2},{1,3},{8,10},{9,11},{16,18},{17,19},{24,26},{25,27}} | collective-permute-start | bytes 1769480 | tf_op jit(solution)/shard_map/ppermute | solution.py:70
  597.3 25.1 %collective-permute-start.9 = (bf16[192,1536]{1,0:T(8,128)(2,1)S(1)}, bf16[192,1536]{1,0:T(8,128)(2,1)S(1)}, u32[]{:S(2)}, u32[]{:S(2)}) collective-permute-start(bf16[192,1536]{1,0:T(8,128)(2,1)S(1)} %fusion.44), channel_id=1, source_target_pairs={{0,2},{1,3},{2,4},{3,5},{8,10},{9,11},{10,12},{11,13},{16,18},{17,... | collective-permute-start | bytes 1769480 | tf_op jit(solution)/shard_map/ppermute | solution.py:70
  658.4 43.9 %collective-permute-start.10 = (bf16[192,1536]{1,0:T(8,128)(2,1)S(1)}, bf16[192,1536]{1,0:T(8,128)(2,1)}, u32[]{:S(2)}, u32[]{:S(2)}) collective-permute-start(bf16[192,1536]{1,0:T(8,128)(2,1)S(1)} %get-tuple-element.168), channel_id=1, source_target_pairs={{0,2},{1,3},{2,4},{3,5},{4,6},{5,7},{8,10},{9,11},{10,12},{11,13},... | collective-permute-start | bytes 1769480 | tf_op jit(solution)/shard_map/ppermute | solution.py:70
  671.3 30.9 %collective-permute-start.13 = (bf16[192,1536]{1,0:T(8,128)(2,1)}, bf16[192,1536]{1,0:T(8,128)(2,1)}, u32[]{:S(2)}, u32[]{:S(2)}) collective-permute-start(bf16[192,1536]{1,0:T(8,128)(2,1)} %fusion.41), channel_id=1, source_target_pairs={{7,5},{6,4},{5,3},{4,2},{3,1},{2,0},{15,13},{14,12},{13,11},{12,10... | collective-permute-start | bytes 1769480 | tf_op jit(solution)/shard_map/ppermute | solution.py:73
  673.6 26.3 %collective-permute-start.27 = (bf16[192,1536]{1,0:T(8,128)(2,1)}, bf16[192,1536]{1,0:T(8,128)(2,1)}, u32[]{:S(2)}, u32[]{:S(2)}) collective-permute-start(bf16[192,1536]{1,0:T(8,128)(2,1)} %fusion.17), channel_id=1, source_target_pairs={{7,5},{6,4},{5,3},{4,2},{3,1},{2,0},{15,13},{14,12},{13,11},{12,10... | collective-permute-start | bytes 1769480 | tf_op jit(solution)/shard_map/ppermute | solution.py:73
  733.6 30.2 %collective-permute-start.28 = (bf16[4,192,512]{2,1,0:T(8,128)(2,1)S(1)}, bf16[4,192,512]{2,1,0:T(8,128)(2,1)S(1)}, u32[]{:S(2)}, u32[]{:S(2)}) collective-permute-start(bf16[4,192,512]{2,1,0:T(8,128)(2,1)S(1)} %dynamic-slice_bitcast_fusion.5), channel_id=1, source_target_pairs={{0,1},{1,0},{2,3},{3,2},{4,5},{5,4},{6,7},{7,6},{8,9},{9,8},{10,11... | collective-permute-start | bytes 2359304 | tf_op jit(solution)/shard_map/ppermute | solution.py:54
  758.0 68.7 %collective-permute-start.35 = (bf16[4,192,512]{2,1,0:T(8,128)(2,1)}, bf16[4,192,512]{2,1,0:T(8,128)(2,1)S(1)}, u32[]{:S(2)}, u32[]{:S(2)}) collective-permute-start(bf16[4,192,512]{2,1,0:T(8,128)(2,1)} %dynamic-slice_bitcast_fusion.4), channel_id=1, source_target_pairs={{0,1},{1,0},{2,3},{3,2},{4,5},{5,4},{6,7},{7,6},{8,9},{9,8},{10,11... | collective-permute-start | bytes 2359304 | tf_op jit(solution)/shard_map/ppermute | solution.py:54
  763.9 67.5 %collective-permute-start.29 = (bf16[192,512]{1,0:T(8,128)(2,1)S(1)}, bf16[192,512]{1,0:T(8,128)(2,1)S(1)}, u32[]{:S(2)}, u32[]{:S(2)}) collective-permute-start(bf16[192,512]{1,0:T(8,128)(2,1)S(1)} %fusion.88), channel_id=1, source_target_pairs={{0,2},{1,3},{8,10},{9,11},{16,18},{17,19},{24,26},{25,27}} | collective-permute-start | bytes 589832 | tf_op jit(solution)/shard_map/ppermute | solution.py:70
  (108 other events, 2757.0 us)
Sparse Core Ops, SparseCore 0:
  88.0 28.5 all-gather.6
  155.6 49.6 all-gather.8
  207.5 50.5 all-gather.14
  260.2 26.8 all-gather.10
  288.5 74.1 all-gather.16
  456.4 51.2 all-gather.12
  684.4 226.1 all-reduce.4

commit v3 on v1

v3 whole, which is shorter than its diff:
```python
import functools

import jax
import jax.numpy as jnp
from jax import lax
from jax.experimental import pallas as pl
from jax.experimental.pallas import tpu as pltpu
from jax.sharding import PartitionSpec as P

H = 12
KV = 2
HD = 128
GROUPS = H // KV
QW = H * HD
KW = KV * HD
QKV = QW + 2 * KW
EXTRA = 128

ROPE_BASE = 1000000.0
EPS = 1e-06
MASKED = -1e30
F32 = jnp.float32
B16 = jnp.bfloat16
VMEM_LIMIT = 56 * 1024 * 1024
VMEM_MOST = 60 * 1024 * 1024
CHUNK = 256
SCATTER_LANES = 1024
MESH = pl.DeviceIdType.MESH


def dot(a, b):
    return jnp.dot(a, b, preferred_element_type=F32)


def dot_t(a, b):
    return lax.dot_general(a, b, (((1,), (1,)), ((), ())), preferred_element_type=F32)


def t_dot(a, b):
    return lax.dot_general(a, b, (((0,), (0,)), ((), ())), preferred_element_type=F32)


def rope_tables(positions):
    half = HD // 2
    freqs = ROPE_BASE ** (-(jnp.arange(half, dtype=F32) * 2.0 / HD))
    angles = positions.astype(F32)[:, None] * freqs[None, :]
    cosine = jnp.cos(angles)
    sine = jnp.sin(angles)
    return (
        jnp.concatenate([cosine, cosine], axis=1),
        jnp.concatenate([-sine, sine], axis=1),
    )


def swap(value, axis, bit):
    count = lax.axis_size(axis)
    return lax.ppermute(value, axis, [(i, i ^ bit) for i in range(count)])


def nearest(chips, place, step):
    found = 0
    for here in range(chips):
        for at, there in enumerate(sorted(range(chips), key=lambda there: abs(there - here))):
            found = found + jnp.where((place == here) & (step == at), there, 0)
    return found


class Spot:
    def __init__(self):
        self.chips = lax.axis_size("tensor") // 2
        dp, tensor = lax.axis_index("dp"), lax.axis_index("tensor")
        self.dp, self.tensor = dp, tensor
        self.row, self.col = dp // 2, dp % 2
        self.chip, self.core = tensor // 2, tensor % 2
        self.over_x = (self.row * 2 + 1 - self.col, tensor)
        self.over_y = ((1 - self.row) * 2 + self.col, tensor)
        self.beside = (dp, self.chip * 2 + 1 - self.core)
        self.left = (dp, jnp.maximum(tensor - 2, 0))
        self.right = (dp, jnp.minimum(tensor + 2, 2 * self.chips - 1))

    def on_line(self, chip):
        return (self.dp, chip * 2 + self.core)

    def index(self, row, col, chip, core):
        return ((row * 2 + col) * self.chips + chip) * 2 + core


def greet(spot, plane, line):
    barrier = pltpu.get_barrier_semaphore()
    peers = [spot.beside] + ([spot.over_x, spot.over_y] if plane else [])
    for peer in peers:
        pl.semaphore_signal(barrier, inc=1, device_id=peer, device_id_type=MESH)
    count = len(peers)
    if line == "all":
        for chip in range(spot.chips):

            @pl.when(spot.chip != chip)
            def _():
                pl.semaphore_signal(barrier, inc=1, device_id=spot.on_line(chip), device_id_type=MESH)

        count = count + spot.chips - 1
    elif line == "near":
        has_left, has_right = spot.chip > 0, spot.chip < spot.chips - 1

        @pl.when(has_left)
        def _():
            pl.semaphore_signal(barrier, inc=1, device_id=spot.left, device_id_type=MESH)

        @pl.when(has_right)
        def _():
            pl.semaphore_signal(barrier, inc=1, device_id=spot.right, device_id_type=MESH)

        count = count + jnp.where(has_left, 1, 0) + jnp.where(has_right, 1, 0)
    pl.semaphore_wait(barrier, count)


def remote(src, dst, send_sem, recv_sem, device):
    return pltpu.make_async_remote_copy(
        src_ref=src,
        dst_ref=dst,
        send_sem=send_sem,
        recv_sem=recv_sem,
        device_id=device,
        device_id_type=MESH,
    )


class Line:
    def __init__(self, spot, block_ref, line_ref, local_sem, send_sem, recv_sem):
        self.spot, self.line = spot, line_ref
        self.send_sem, self.recv_sem = send_sem, recv_sem
        self.local = pltpu.make_async_copy(block_ref, line_ref.at[spot.chip], local_sem)

    def copy(self, there, way):
        here = self.line.at[there]
        peer = (self.spot.left, self.spot.right)[way]
        return remote(here, here, self.send_sem.at[way, there], self.recv_sem.at[there], peer)

    def ways(self, there):
        chip, chips = self.spot.chip, self.spot.chips
        return ((chip > 0) & (there >= chip), (chip < chips - 1) & (there <= chip))

    def send(self, there):
        for way, when in enumerate(self.ways(there)):
            pl.when(when)(self.copy(there, way).start)

    def start(self):
        self.local.wait()
        self.send(self.spot.chip)

    def forward(self, step):
        for there in (self.spot.chip - step, self.spot.chip + step):

            @pl.when((there >= 0) & (there < self.spot.chips))
            def _():
                here = self.line.at[there]
                remote(here, here, self.send_sem.at[0, there], self.recv_sem.at[there], self.spot.beside).wait_recv()
                self.send(there)

    def end(self):
        for there in range(self.spot.chips):
            for way, when in enumerate(self.ways(there)):
                pl.when(when)(self.copy(there, way).wait_send)


def line_kernel(block_ref, line_ref, local_sem, send_sem, recv_sem):
    spot = Spot()
    line = Line(spot, block_ref, line_ref, local_sem, send_sem, recv_sem)
    line.local.start()
    greet(spot, False, "near")
    line.start()
    for step in range(1, spot.chips):
        line.forward(step)
    line.end()


def plane_kernel(more, line_ref, *refs):
    spot = Spot()
    if more:
        block_ref, whole_ref, next_ref, local_sem, send_sem, recv_sem, *sems = refs
        line = Line(spot, block_ref, next_ref, *sems)
        line.local.start()
    else:
        whole_ref, local_sem, send_sem, recv_sem = refs
    chips, chip, core, row, col = spot.chips, spot.chip, spot.core, spot.row, spot.col
    cut = chips // 2

    def local(there):
        return pltpu.make_async_copy(
            line_ref.at[there], whole_ref.at[spot.index(row, col, there, core)], local_sem.at[there]
        )

    for there in range(chips):
        local(there).start()
    greet(spot, True, "near" if more else None)
    if more:
        line.start()
    sent = []

    def send(index, device, source=None):
        source = whole_ref.at[index] if source is None else source
        copy = remote(source, whole_ref.at[index], send_sem.at[len(sent)], recv_sem.at[index], device)
        sent.append(copy)
        copy.start()

    def arrive(index):
        remote(
            whole_ref.at[index], whole_ref.at[index], send_sem.at[0], recv_sem.at[index], spot.beside
        ).wait_recv()

    for there in range(chips):
        index = spot.index(row, col, there, core)
        for peer in (spot.over_x, spot.over_y, spot.beside):
            send(index, peer, line_ref.at[there])
    for there in range(chips):
        across_x = spot.index(row, 1 - col, there, core)
        arrive(across_x)
        if there < cut:
            send(across_x, spot.over_y)
        send(across_x, spot.beside)
        across_y = spot.index(1 - row, col, there, core)
        arrive(across_y)
        if there >= cut:
            send(across_y, spot.over_x)
        send(across_y, spot.beside)
        if more and 0 < there:
            line.forward(there)
    for there in range(chips):
        index = spot.index(1 - row, 1 - col, there, core)
        arrive(index)
        send(index, spot.beside)
    for plane in range(4):
        for there in range(chips):
            arrive(spot.index(plane // 2, plane % 2, there, 1 - core))
    for there in range(chips):
        local(there).wait()
    for copy in sent:
        copy.wait_send()
    if more:
        line.end()


def gather_line(block, collective_id):
    chips = lax.axis_size("tensor") // 2
    dma = pltpu.SemaphoreType.DMA
    return pl.pallas_call(
        line_kernel,
        in_specs=[pl.BlockSpec(memory_space=pl.ANY)],
        out_specs=pl.BlockSpec(memory_space=pl.ANY),
        out_shape=jax.ShapeDtypeStruct((chips,) + block.shape, B16),
        scratch_shapes=[dma, dma((2, chips)), dma((chips,))],
        compiler_params=pltpu.CompilerParams(
            collective_id=collective_id, has_side_effects=True, vmem_limit_bytes=VMEM_LIMIT
        ),
        cost_estimate=pl.CostEstimate(flops=0, bytes_accessed=block.size * 100, transcendentals=0),
    )(block)


def gather_plane(line, collective_id, more=None):
    chips, size, width = line.shape
    dma = pltpu.SemaphoreType.DMA
    anywhere = pl.BlockSpec(memory_space=pl.ANY)
    shapes = [jax.ShapeDtypeStruct((8 * chips, size, width), B16)]
    sems = [dma((chips,)), dma((10 * chips,)), dma((8 * chips,))]
    if more is not None:
        shapes.append(jax.ShapeDtypeStruct((chips,) + more.shape, B16))
        sems += [dma, dma((2, chips)), dma((chips,))]
    out = pl.pallas_call(
        functools.partial(plane_kernel, more is not None),
        in_specs=[anywhere] * len(shapes),
        out_specs=[anywhere] * len(shapes),
        out_shape=shapes,
        scratch_shapes=sems,
        compiler_params=pltpu.CompilerParams(
            collective_id=collective_id, has_side_effects=True, vmem_limit_bytes=VMEM_LIMIT
        ),
        cost_estimate=pl.CostEstimate(flops=0, bytes_accessed=line.size * 60, transcendentals=0),
    )(line, *([] if more is None else [more]))
    return (out[0].reshape(8 * chips * size, width), *out[1:])


def scatter_kernel(parts, arrays, *refs):
    grads, outs = refs[:arrays], refs[arrays : 2 * arrays]
    mine, got, over_x, over_y, across_x, across_y, line, load_sem, send_sem, recv_sem = refs[2 * arrays :]
    spot = Spot()
    chips, chip, core, row, col = spot.chips, spot.chip, spot.core, spot.row, spot.col
    cut = chips // 2

    def at(r, c, z):
        return (r * 2 + c) * chips + z

    def lanes(p):
        return pl.ds(parts[p][0], parts[p][1])

    def source(p, which):
        _, width, array, start = parts[p]
        return grads[array].at[:, which, :, pl.ds(start, width)]

    def load(p):
        return pltpu.make_async_copy(source(p, core), mine.at[:, :, lanes(p)], load_sem.at[p])

    def swapped(p):
        return remote(
            source(p, 1 - core), got.at[:, :, lanes(p)], send_sem.at[p, 0], recv_sem.at[p, 0], spot.beside
        )

    def first(p):
        cols = lanes(p)
        copies = []
        for side in range(2):
            copies.append(
                remote(
                    mine.at[pl.ds(at(side, 1 - col, 0), cut), :, cols],
                    over_x.at[pl.ds(side * cut, cut), :, cols],
                    send_sem.at[p, 1 + side],
                    recv_sem.at[p, 1 + side],
                    spot.over_x,
                )
            )
            copies.append(
                remote(
                    mine.at[pl.ds(at(1 - row, side, cut), chips - cut), :, cols],
                    over_y.at[pl.ds(side * (chips - cut), chips - cut), :, cols],
                    send_sem.at[p, 3 + side],
                    recv_sem.at[p, 3 + side],
                    spot.over_y,
                )
            )
        return copies

    def second(p):
        cols = lanes(p)
        return [
            remote(
                mine.at[pl.ds(at(1 - row, col, 0), cut), :, cols],
                across_y.at[:, :, cols],
                send_sem.at[p, 5],
                recv_sem.at[p, 5],
                spot.over_y,
            ),
            remote(
                mine.at[pl.ds(at(row, 1 - col, cut), chips - cut), :, cols],
                across_x.at[:, :, cols],
                send_sem.at[p, 6],
                recv_sem.at[p, 6],
                spot.over_x,
            ),
        ]

    def third(p, other):
        cols = lanes(p)
        return remote(
            mine.at[at(row, col, other), :, cols],
            line.at[chip, :, cols],
            send_sem.at[p, 7 + other],
            recv_sem.at[p, 7 + chip],
            spot.on_line(other),
        )

    def add(p, target, start, source, begin, count):
        cols = lanes(p)

        def body(step, _):
            target[start + step, :, cols] = (
                target[start + step, :, cols].astype(F32) + source[begin + step, :, cols].astype(F32)
            ).astype(B16)
            return 0

        lax.fori_loop(0, count, body, 0)

    def stage_one(p):
        load(p).wait()
        swapped(p).wait()
        add(p, mine, 0, got, 0, 4 * chips)
        for copy in first(p):
            copy.start()

    def stage_two(p):
        for copy in first(p):
            copy.wait()
        for side in range(2):
            add(p, mine, at(side, col, 0), over_x, side * cut, cut)
            add(p, mine, at(row, side, cut), over_y, side * (chips - cut), chips - cut)
        for copy in second(p):
            copy.start()

    def stage_three(p):
        for copy in second(p):
            copy.wait()
        add(p, mine, at(row, col, 0), across_y, 0, cut)
        add(p, mine, at(row, col, cut), across_x, 0, chips - cut)
        for other in range(chips):
            pl.when(chip != other)(third(p, other).start)

    def stage_four(p):
        cols = lanes(p)
        total = mine[at(row, col, chip), :, cols].astype(F32)
        for other in range(chips):

            @pl.when(chip != other)
            def _():
                here = line.at[other, :, cols]
                remote(here, here, send_sem.at[p, 7 + other], recv_sem.at[p, 7 + other], spot.beside).wait_recv()

            total = total + line[other, :, cols].astype(F32)
        _, width, array, start = parts[p]
        outs[array][:, start : start + width] = total
        for other in range(chips):
            pl.when(chip != other)(third(p, other).wait_send)

    for p in range(len(parts)):
        load(p).start()
    line[chip] = jnp.zeros(line.shape[1:], B16)
    greet(spot, True, "all")
    for p in range(len(parts)):
        swapped(p).start()
    stages = (stage_one, stage_two, stage_three, stage_four)
    for step in range(len(parts) + len(stages) - 1):
        for late, stage in enumerate(stages):
            if 0 <= step - late < len(parts):
                stage(step - late)


def scatter_weights(grads, collective_id):
    total = grads[0].shape[0]
    devices = lax.axis_size(("dp", "tensor"))
    size = total // devices
    if lax.axis_size("dp") != 4:
        return [
            lax.psum_scatter(array, ("dp", "tensor"), scatter_dimension=0, tiled=True).astype(F32)
            for array in grads
        ]
    chips = lax.axis_size("tensor") // 2
    cut = chips // 2
    parts, width = [], 0
    for at, array in enumerate(grads):
        count = pl.cdiv(array.shape[1], SCATTER_LANES)
        tiles = array.shape[1] // 128
        ends = [tiles * p // count * 128 for p in range(count + 1)]
        for start, end in zip(ends, ends[1:]):
            parts.append((width + start, end - start, at, start))
        width += array.shape[1]
    dma = pltpu.SemaphoreType.DMA
    return pl.pallas_call(
        functools.partial(scatter_kernel, parts, len(grads)),
        in_specs=[pl.BlockSpec(memory_space=pl.ANY)] * len(grads),
        out_specs=[pl.BlockSpec(memory_space=pltpu.VMEM)] * len(grads),
        out_shape=[jax.ShapeDtypeStruct((size, array.shape[1]), F32) for array in grads],
        scratch_shapes=[
            pltpu.VMEM((4 * chips, size, width), B16),
            pltpu.VMEM((4 * chips, size, width), B16),
            pltpu.VMEM((2 * cut, size, width), B16),
            pltpu.VMEM((2 * (chips - cut), size, width), B16),
            pltpu.VMEM((chips - cut, size, width), B16),
            pltpu.VMEM((cut, size, width), B16),
            pltpu.VMEM((chips, size, width), B16),
            dma((len(parts),)),
            dma((len(parts), 7 + chips)),
            dma((len(parts), 7 + chips)),
        ],
        compiler_params=pltpu.CompilerParams(
            collective_id=collective_id, has_side_effects=True, vmem_limit_bytes=VMEM_LIMIT
        ),
        cost_estimate=pl.CostEstimate(flops=0, bytes_accessed=devices * size * width * 8, transcendentals=0),
    )(*[array.reshape(devices // 2, 2, size, array.shape[1]) for array in grads])


class Named:
    def __init__(self, names, refs):
        for name, ref in zip(names, refs, strict=True):
            setattr(self, name, ref)


def project_kernel(hidden_ref, weight_ref, bias_ref, cos_ref, sin_ref, out_ref):
    chunk = pl.program_id(0)
    turned = chunk < (QW + KW) // 256
    lin = dot(hidden_ref[...], weight_ref[...]) + bias_ref[...]
    for head in range(2):
        cut = pl.ds(head * HD, HD)
        one = lin[:, head * HD : (head + 1) * HD]
        rot = one * cos_ref[...] + pltpu.roll(one, HD // 2, 1) * sin_ref[...]
        out_ref[:, cut] = jnp.where(turned, rot, one).astype(B16)


def project(hidden, weights, bias, cosine, sine):
    rows, depth = hidden.shape
    return pl.pallas_call(
        project_kernel,
        grid=(QKV // 256,),
        in_specs=[
            pl.BlockSpec((rows, depth), lambda j: (0, 0)),
            pl.BlockSpec((depth, 256), lambda j: (0, j)),
            pl.BlockSpec((1, 256), lambda j: (0, j)),
            pl.BlockSpec((rows, HD), lambda j: (0, 0)),
            pl.BlockSpec((rows, HD), lambda j: (0, 0)),
        ],
        out_specs=pl.BlockSpec((rows, 256), lambda j: (0, j)),
        out_shape=jax.ShapeDtypeStruct((rows, QKV), B16),
        compiler_params=pltpu.CompilerParams(vmem_limit_bytes=VMEM_LIMIT),
        cost_estimate=pl.CostEstimate(
            flops=2 * rows * depth * QKV,
            bytes_accessed=2 * (depth * QKV + rows * depth + rows * QKV),
            transcendentals=0,
        ),
    )(hidden, weights, bias, cosine, sine)


def fill_bias(info_ref, bias):
    shape = bias.shape
    place = info_ref[1] + lax.broadcasted_iota(jnp.int32, shape, 0)
    keys = lax.broadcasted_iota(jnp.int32, shape, 1)
    bias[...] = jnp.where((keys <= place) & (keys < info_ref[0]), 0.0, MASKED)


def flat(ref):
    return ref[...].reshape(ref.shape[0] * ref.shape[2], ref.shape[3])


def attend_kernel(info_ref, q_ref, k_ref, v_ref, out_ref, log_ref, bias):
    @pl.when(pl.program_id(0) == 0)
    def _():
        fill_bias(info_ref, bias)

    keys, values = flat(k_ref), flat(v_ref)
    scores = dot_t(q_ref[...], keys) * (HD**-0.5) + bias[...]
    top = jnp.max(scores, axis=-1, keepdims=True)
    expd = jnp.exp(scores - top)
    summed = jnp.sum(expd, axis=-1, keepdims=True)
    probs = (expd * (1.0 / summed)).astype(B16)
    out_ref[...] = dot(probs, values).astype(B16)
    log_ref[...] = jnp.broadcast_to(top + jnp.log(summed), log_ref.shape)


def attend(info, micro, qkv, keys_values, rows):
    parts = keys_values.shape[0]
    total = parts * rows
    return pl.pallas_call(
        attend_kernel,
        grid_spec=pltpu.PrefetchScalarGridSpec(
            num_scalar_prefetch=1,
            grid=(H,),
            in_specs=[
                pl.BlockSpec((rows, HD), lambda h, info: (micro, h)),
                pl.BlockSpec((parts, 1, rows, HD), lambda h, info: (0, micro, 0, h // GROUPS)),
                pl.BlockSpec((parts, 1, rows, HD), lambda h, info: (0, micro, 0, KV + h // GROUPS)),
            ],
            out_specs=[
                pl.BlockSpec((rows, HD), lambda h, info: (0, h)),
                pl.BlockSpec((rows, HD), lambda h, info: (0, h)),
            ],
            scratch_shapes=[pltpu.VMEM((rows, total), F32)],
        ),
        out_shape=[
            jax.ShapeDtypeStruct((rows, QW), B16),
            jax.ShapeDtypeStruct((rows, QW), F32),
        ],
        compiler_params=pltpu.CompilerParams(vmem_limit_bytes=VMEM_LIMIT),
        cost_estimate=pl.CostEstimate(
            flops=8 * rows * total * QW,
            bytes_accessed=4 * total * KW + 8 * rows * QW,
            transcendentals=H * rows * total,
        ),
    )(info, qkv, keys_values, keys_values)


def attend_back_kernel(names, parts, *refs):
    r = Named(names, refs)
    spot = Spot()
    chips, chip, core = spot.chips, spot.chip, spot.core
    rows = r.q.shape[0]
    step = pl.program_id(0)
    micros = r.sums.shape[0]
    micro, head = step // H, lax.rem(step, H)
    pieces = micros * KV
    scale = HD**-0.5

    def rows_of(block, which):
        return pl.ds(pl.multiple_of((2 * block + which) * rows, rows), rows)

    def swapped(piece):
        mine = r.part.at[piece, :, 1 - core]
        return remote(mine, r.xrecv.at[piece], r.xsend.at[piece], r.xrecv_sem.at[piece], spot.beside)

    def along(piece, block):
        return remote(
            r.part.at[piece, block, core],
            r.zrecv.at[piece, chip],
            r.zsend.at[piece, block],
            r.zrecv_sem.at[piece, chip],
            spot.on_line(block),
        )

    def spread(piece):
        swapped(piece).wait_recv()
        for block in range(chips):
            total = r.part[piece, block, core].astype(F32) + r.xrecv[piece, block].astype(F32)
            r.part[piece, block, core] = total.astype(B16)
            pl.when(chip != block)(along(piece, block).start)

    @pl.when(step == 0)
    def _():
        greet(spot, False, "all")

    @pl.when(head == 0)
    def _():
        shape = r.bias.shape
        place = spot.tensor * rows + lax.broadcasted_iota(jnp.int32, shape, 0)
        keys_at = lax.broadcasted_iota(jnp.int32, shape, 1)
        r.bias[...] = jnp.where((keys_at <= place) & (keys_at < r.length[micro]), 0.0, MASKED)

    queries, keys, values, grads = r.q[...], flat(r.k), flat(r.v), r.g[...]
    scores = dot_t(queries, keys) * scale + r.bias[...]
    probs = jnp.exp(scores - r.log[:, :1])
    grad_probs = dot_t(grads, values)
    inner = jnp.sum(grad_probs * probs, axis=-1, keepdims=True)
    grad_scores = (probs * (grad_probs - inner)).astype(B16)
    grad_q = dot(grad_scores, keys) * scale
    turned = grad_q * r.cos[...] - pltpu.roll(grad_q, HD // 2, 1) * r.sin[...]
    r.dq[...] = turned.astype(B16)
    grad_k = t_dot(grad_scores, queries) * scale
    grad_v = t_dot(probs.astype(B16), grads)
    first = lax.rem(head, GROUPS) == 0

    @pl.when(first)
    def _():
        r.dk_acc[...] = grad_k
        r.dv_acc[...] = grad_v

    @pl.when(jnp.logical_not(first))
    def _():
        r.dk_acc[...] += grad_k
        r.dv_acc[...] += grad_v

    for piece in range(pieces):

        @pl.when(step == (piece + 1) * GROUPS - 1)
        def _():
            shape = (chips, 2, rows, HD)
            r.part[piece, :, :, :, :HD] = r.dk_acc[...].reshape(shape).astype(B16)
            r.part[piece, :, :, :, HD:] = r.dv_acc[...].reshape(shape).astype(B16)
            swapped(piece).start()

        if piece + 1 < pieces:

            @pl.when(step == (piece + 1) * GROUPS)
            def _():
                spread(piece)

    @pl.when(step == pieces * GROUPS - 1)
    def _():
        spread(pieces - 1)
        for piece in range(pieces):
            total = r.part[piece, chip, core].astype(F32)
            for other in range(chips):

                @pl.when(chip != other)
                def _():
                    here = r.zrecv.at[piece, other]
                    remote(
                        here, here, r.zsend.at[piece, other], r.zrecv_sem.at[piece, other], spot.beside
                    ).wait_recv()

                got = jnp.where(chip != other, r.zrecv[piece, other], jnp.zeros((rows, 2 * HD), B16))
                total = total + got.astype(F32)
            at, group = piece // KV, piece % KV
            grad = total[:, :HD]
            grad = grad * r.cos[...] - pltpu.roll(grad, HD // 2, 1) * r.sin[...]
            r.sums[at, :, group * HD : (group + 1) * HD] = grad.astype(B16)
            r.sums[at, :, KW + group * HD : KW + (group + 1) * HD] = total[:, HD:].astype(B16)
        for piece in range(pieces):
            swapped(piece).wait_send()
            for block in range(chips):
                pl.when(chip != block)(along(piece, block).wait_send)


def attend_back(lengths, qkv, keys_values, grads, logs, cosine, sine, rows, collective_id):
    parts, micros = keys_values.shape[:2]
    chips = parts // 2
    total = parts * rows
    pieces = micros * KV
    dma = pltpu.SemaphoreType.DMA
    vmem = pltpu.VMEM

    def heads(step):
        return (step // H, step % H)

    inputs = {
        "length": (pl.BlockSpec(memory_space=pltpu.SMEM), lengths),
        "q": (pl.BlockSpec((rows, HD), heads), qkv),
        "k": (
            pl.BlockSpec((parts, 1, rows, HD), lambda s: (0, s // H, 0, s % H // GROUPS)),
            keys_values,
        ),
        "v": (
            pl.BlockSpec((parts, 1, rows, HD), lambda s: (0, s // H, 0, KV + s % H // GROUPS)),
            keys_values,
        ),
        "g": (pl.BlockSpec((rows, HD), heads), grads),
        "log": (pl.BlockSpec((rows, HD), heads), logs),
        "cos": (pl.BlockSpec((rows, HD), lambda s: (0, 0)), cosine),
        "sin": (pl.BlockSpec((rows, HD), lambda s: (0, 0)), sine),
    }
    outputs = {
        "dq": (pl.BlockSpec((rows, HD), heads), jax.ShapeDtypeStruct((micros * rows, QW), B16)),
        "sums": (
            pl.BlockSpec((micros, rows, 2 * KW), lambda s: (0, 0, 0)),
            jax.ShapeDtypeStruct((micros, rows, 2 * KW), B16),
        ),
    }
    scratch = {
        "bias": vmem((rows, total), F32),
        "dk_acc": vmem((total, HD), F32),
        "dv_acc": vmem((total, HD), F32),
        "part": vmem((pieces, chips, 2, rows, 2 * HD), B16),
        "xrecv": vmem((pieces, chips, rows, 2 * HD), B16),
        "zrecv": vmem((pieces, chips, rows, 2 * HD), B16),
        "xsend": dma((pieces,)),
        "xrecv_sem": dma((pieces,)),
        "zsend": dma((pieces, chips)),
        "zrecv_sem": dma((pieces, chips)),
    }
    return pl.pallas_call(
        functools.partial(attend_back_kernel, [*inputs, *outputs, *scratch], parts),
        grid=(micros * H,),
        in_specs=[spec for spec, _ in inputs.values()],
        out_specs=[spec for spec, _ in outputs.values()],
        out_shape=[shape for _, shape in outputs.values()],
        scratch_shapes=list(scratch.values()),
        compiler_params=pltpu.CompilerParams(
            collective_id=collective_id, has_side_effects=True, vmem_limit_bytes=VMEM_LIMIT
        ),
        cost_estimate=pl.CostEstimate(
            flops=20 * micros * rows * total * QW,
            bytes_accessed=micros * (8 * total * KW + 12 * rows * QW),
            transcendentals=micros * H * rows * total,
        ),
    )(*[value for _, value in inputs.values()])


def mlp_kernel(names, reduced, *refs):
    r = Named(names, refs)
    has_next, has_prior = "own" in names, "prior" in names
    spot = Spot()
    chips, chip, core, row, col = spot.chips, spot.chip, spot.core, spot.row, spot.col
    units, depth = r.wg.shape
    rows = r.grad.shape[0]
    pair = 2 * rows
    quarter = depth // 4
    chunks = [(i * CHUNK, min(CHUNK, units - i * CHUNK)) for i in range(pl.cdiv(units, CHUNK))]
    whole_chunks, rest = units // CHUNK, units % CHUNK
    wide = depth // 2

    def block_at(step):
        return nearest(chips, chip, chips - 1 - step)

    def span(block):
        return pl.ds(pl.multiple_of(block * pair, pair), pair)

    def rows_of(block, which):
        return pl.ds(pl.multiple_of(block * pair + which * rows, rows), rows)

    def columns(index, width=CHUNK):
        return pl.ds(pl.multiple_of(index * width, width), width)

    def weight_load(index):
        cut = pl.ds(*chunks[index])
        return [
            pltpu.make_async_copy(src.at[cut], dst.at[cut], r.weight_sem.at[i, index])
            for i, (src, dst) in enumerate(((r.wg_hbm, r.wg), (r.wu_hbm, r.wu), (r.wd_hbm, r.wd)))
        ]

    def weights_here(index, width=CHUNK):
        for i, dst in enumerate((r.wg, r.wu, r.wd)):
            cut = dst.at[pl.ds(index * CHUNK, width)]
            pltpu.make_async_copy(cut, cut, r.weight_sem.at[i, index]).wait()

    def h_load(block):
        return pltpu.make_async_copy(r.h_hbm.at[span(block)], r.h.at[span(block)], r.load_sem.at[0, block])

    def g_load(block):
        return pltpu.make_async_copy(r.cot.at[span(block)], r.g.at[span(block)], r.load_sem.at[1, block])

    def gather_send(block, way):
        here = r.whole.at[rows_of(block, core)]
        peer = (spot.left, spot.right, spot.beside)[way]
        return remote(here, here, r.gather_send.at[way, block], r.gather_recv.at[block, core], peer)

    def gather_first(way):
        peer = (spot.left, spot.right, spot.beside)[way]
        here = r.whole.at[rows_of(chip, core)]
        return remote(r.own, here, r.gather_send.at[way, chip], r.gather_recv.at[chip, core], peer)

    def gathered(block, which):
        here = r.whole.at[rows_of(block, which)]
        remote(here, here, r.gather_send.at[2, block], r.gather_recv.at[block, which], spot.beside).wait_recv()

    def own_copy():
        return pltpu.make_async_copy(r.own, r.whole.at[rows_of(chip, core)], r.local_sem)

    def gather_start():
        own_copy().start()
        pl.when(chip > 0)(gather_first(0).start)
        pl.when(chip < chips - 1)(gather_first(1).start)
        gather_first(2).start()

    def gather_forward(step):
        block = chip - step

        @pl.when(block >= 0)
        def _():
            gathered(block, core)
            pl.when(chip < chips - 1)(gather_send(block, 1).start)
            gather_send(block, 2).start()

        after = chip + step

        @pl.when(after < chips)
        def _():
            gathered(after, core)
            pl.when(chip > 0)(gather_send(after, 0).start)
            gather_send(after, 2).start()

    def gather_end():
        own_copy().wait()
        for block in range(chips):
            gathered(block, 1 - core)
        for block in range(chips):
            away = block != chip
            pl.when((chip > 0) & (block >= chip) & away)(gather_send(block, 0).wait_send)
            pl.when((chip < chips - 1) & (block <= chip) & away)(gather_send(block, 1).wait_send)
            pl.when(away)(gather_send(block, 2).wait_send)
        pl.when(chip > 0)(gather_first(0).wait_send)
        pl.when(chip < chips - 1)(gather_first(1).wait_send)
        gather_first(2).wait_send()

    def swapped(block):
        return remote(
            r.part.at[rows_of(block, 1 - core)],
            r.xrecv.at[block],
            r.xsend.at[block],
            r.xrecv_sem.at[block],
            spot.beside,
        )

    def along(block, ahead):
        slot = chips - 1 - block if ahead else chips - block
        return remote(
            r.part.at[rows_of(block, core)],
            r.zrecv.at[slot],
            r.zsend.at[block],
            r.zrecv_sem.at[slot],
            spot.right if ahead else spot.left,
        )

    def finish(block):
        swapped(block).wait_recv()
        total = r.part[rows_of(block, core), :].astype(F32) + r.xrecv[block].astype(F32)

        @pl.when(block == chip)
        def _():
            r.grad[...] = total

        @pl.when(block != chip)
        def _():
            r.part[rows_of(block, core), :] = total.astype(B16)
            pl.when(chip == 0)(along(block, True).start)
            pl.when(chip == chips - 1)(along(block, False).start)

    def relay_one(block, ahead):
        slot = chips - 1 - block if ahead else chips - block
        remote(
            r.zrecv.at[slot], r.zrecv.at[slot], r.zsend.at[block], r.zrecv_sem.at[slot], spot.beside
        ).wait_recv()

        @pl.when(block == chip)
        def _():
            r.grad[...] = r.grad[...] + r.zrecv[slot].astype(F32)

        @pl.when(block != chip)
        def _():
            here = rows_of(block, core)
            r.part[here, :] = (r.part[here, :].astype(F32) + r.zrecv[slot].astype(F32)).astype(B16)
            along(block, ahead).start()

    def relay(point):
        step = point - (chip - 1)

        @pl.when((chip > 0) & (step >= 0) & (step < chips - chip))
        def _():
            relay_one(chips - 1 - step, True)

        back_step = point - (chips - 2 - chip)

        @pl.when((chip < chips - 1) & (back_step >= 0) & (back_step <= chip))
        def _():
            relay_one(back_step, False)

    def gates(step, block):
        here = span(block)

        def one(start, width):
            cut = pl.ds(start, width)
            gate = dot_t(r.h[here, :], r.wg[cut, :])
            up = dot_t(r.h[here, :], r.wu[cut, :])
            grad = dot_t(r.g[here, :], r.wd[cut, :])
            sigma = jax.nn.sigmoid(gate)
            silu = gate * sigma
            r.act[here, cut] = (silu * up).astype(B16)
            r.dg[here, cut] = (grad * up * sigma * (1.0 + gate * (1.0 - sigma))).astype(B16)
            r.du[here, cut] = (grad * silu).astype(B16)

        def chunk(index, _):
            pl.when(step == 0)(functools.partial(weights_here, index))
            one(pl.multiple_of(index * CHUNK, CHUNK), CHUNK)
            return 0

        lax.fori_loop(0, whole_chunks, chunk, 0)
        if rest:
            pl.when(step == 0)(functools.partial(weights_here, whole_chunks, rest))
            one(whole_chunks * CHUNK, rest)

    def back(block):
        here = span(block)

        def chunk(index, _):
            cut = columns(index, wide)
            grad = dot(r.dg[here, :], r.wg[:, cut]) + dot(r.du[here, :], r.wu[:, cut])
            r.part[here, cut] = grad.astype(B16)
            return 0

        lax.fori_loop(0, depth // wide, chunk, 0)
        swapped(block).start()

    def put_out(block, index):
        cut = pl.ds(index * wide, wide)
        return pltpu.make_async_copy(
            r.stage_out.at[:, cut], r.out.at[span(block), cut], r.out_sem.at[index]
        )

    def out_block(block):
        for index in range(2):
            pl.when(block > 0)(put_out(block, index).wait)
            cut = slice(index * wide, (index + 1) * wide)
            r.stage_out[:, cut] = dot(r.act[span(block), :], r.wd[:, cut]).astype(B16)
            put_out(block, index).start()

    def place(matrix, start, width):
        return pl.ds(pl.multiple_of(matrix * units + start, 16), width)

    def exchanged(matrix, index, start, width, over_x):
        here = place(matrix, start, width)
        at = matrix * len(chunks) + index
        source = r.sums.at[:, 1 - col, here] if over_x else r.sums.at[1 - row, :, here]
        peer = spot.over_x if over_x else spot.over_y
        return remote(source, r.landing.at[:, here], r.one_send.at[at], r.one_recv.at[at], peer)

    def exchange_start(matrix, index, start, width):
        first = lax.rem(matrix + index, 2) == 0
        pl.when(first)(exchanged(matrix, index, start, width, True).start)
        pl.when(jnp.logical_not(first))(exchanged(matrix, index, start, width, False).start)

    def exchange_copies(matrix, index, slot):
        start, width = chunks[index]
        here = place(matrix, start, width)
        cut = pl.ds(0, width)
        own = r.sums.at[:, col, here] if (matrix + index) % 2 == 0 else r.sums.at[row, :, here]
        return [
            pltpu.make_async_copy(own, r.held_own.at[slot, :, cut], r.held_sem.at[slot, 0]),
            pltpu.make_async_copy(r.landing.at[:, here], r.held_got.at[slot, :, cut], r.held_sem.at[slot, 1]),
        ]

    def exchange_load(matrix, index, slot):
        exchanged(matrix, index, *chunks[index], (matrix + index) % 2 == 0).wait_recv()
        for copy in exchange_copies(matrix, index, slot):
            copy.start()

    def exchange(matrix, index, slot):
        start, width = chunks[index]
        for copy in exchange_copies(matrix, index, slot):
            copy.wait()
        mine = row if (matrix + index) % 2 == 0 else col
        r.shard[place(matrix, start, width), :] = (
            r.held_own[slot, mine, :width].astype(F32) + r.held_got[slot, mine, :width].astype(F32)
        ).astype(B16)
        at = reduced[matrix, index]
        r.rest[at : at + width, :] = (
            r.held_own[slot, 1 - mine, :width].astype(F32) + r.held_got[slot, 1 - mine, :width].astype(F32)
        ).astype(B16)

    def weight_grads(matrix, left, right):
        def put(start, width, slot):
            return pltpu.make_async_copy(
                r.stage.at[slot, :, :, pl.ds(0, width)],
                r.sums.at[:, :, place(matrix, start, width)],
                r.stage_sem.at[slot],
            )

        def one(index, start, width, slot):
            if has_prior:
                fetch = pltpu.make_async_copy(
                    r.prior.at[:, :, place(matrix, start, width)],
                    r.before.at[:, :, pl.ds(0, width)],
                    r.before_sem,
                )
                fetch.start()
            value = t_dot(left[:, pl.ds(start, width)], right[...])
            if has_prior:
                fetch.wait()
            for at in range(4):
                piece = value[:, at * quarter : (at + 1) * quarter]
                if has_prior:
                    piece = piece + r.before[at // 2, at % 2, :width].astype(F32)
                r.stage[slot, at // 2, at % 2, :width] = piece.astype(B16)
            put(start, width, slot).start()

        def sent(index, start, width, slot):
            put(start, width, slot).wait()
            if reduced:
                exchange_start(matrix, index, start, width)

        def body(index, _):
            slot = lax.rem(index, 2)
            start = pl.multiple_of(index * CHUNK, CHUNK)
            one(index, start, CHUNK, slot)

            @pl.when(index > 0)
            def _():
                sent(index - 1, start - CHUNK, CHUNK, 1 - slot)

            return 0

        lax.fori_loop(0, whole_chunks, body, 0)
        index = whole_chunks
        if rest:
            one(index, index * CHUNK, rest, index % 2)
            if index:
                sent(index - 1, (index - 1) * CHUNK, CHUNK, (index - 1) % 2)
            sent(index, index * CHUNK, rest, index % 2)
        else:
            sent(index - 1, (index - 1) * CHUNK, CHUNK, (index - 1) % 2)

    for step in range(chips):
        h_load(block_at(step)).start()
        g_load(block_at(step)).start()
        if step == 0:
            for index in range(len(chunks)):
                for copy in weight_load(index):
                    copy.start()
    greet(spot, bool(reduced), "near")
    if has_next:
        gather_start()

    def loaded(block):
        h_load(block).wait()
        g_load(block).wait()

    todo = [(matrix, index) for matrix in (2, 0, 1) for index in range(len(chunks))] if reduced else []
    share = pl.cdiv(len(todo), chips)
    loading = []

    def some():
        for _ in range(share):
            if loading:
                exchange(*loading.pop(0))
            if todo:
                loading.append((*todo.pop(0), len(todo) % 2))
                exchange_load(*loading[-1])

    if has_next:

        def unit(step, _):
            block = block_at(step)
            loaded(block)
            gates(step, block)

            @pl.when(step > 0)
            def _():
                finish(block_at(step - 1))

            back(block)
            pl.when(step == 0)(functools.partial(gather_forward, 1))
            return 0

        lax.fori_loop(0, chips, unit, 0)
        finish(block_at(chips - 1))
        gather_forward(2)
        relay(0)
        weight_grads(2, r.act, r.g)
        for step in range(3, chips):
            gather_forward(step)
        weight_grads(0, r.dg, r.h)
        relay(1)
        weight_grads(1, r.du, r.h)
        for point in range(2, chips - 2):
            relay(point)
    else:

        def unit(step, _):
            block = block_at(step)
            loaded(block)
            gates(step, block)
            return 0

        def unit_back(step, _):
            back(block_at(step))

            @pl.when(step > 0)
            def _():
                finish(block_at(step - 1))

            return 0

        lax.fori_loop(0, chips, unit, 0)
        weight_grads(2, r.act, r.g)
        lax.fori_loop(0, chips, unit_back, 0)
        finish(block_at(chips - 1))
        weight_grads(0, r.dg, r.h)
        relay(0)
        weight_grads(1, r.du, r.h)
        for point in range(1, chips - 2):
            relay(point)
    for block in range(chips):
        out_block(jnp.int32(block))
        some()
    relay(chips - 2)
    some()
    for index in range(2):
        put_out(0, index).wait()
    if reduced:
        for matrix in range(3):
            for index, (start, width) in enumerate(chunks):
                exchanged(matrix, index, start, width, (matrix + index) % 2 == 0).wait_send()
    for block in range(chips):
        swapped(block).wait_send()
        pl.when(chip < block)(along(block, True).wait_send)
        pl.when(chip > block)(along(block, False).wait_send)
    if has_next:
        gather_end()


def exchange_rows(units):
    chunks = [min(CHUNK, units - start) for start in range(0, units, CHUNK)]
    keys = [(matrix, index) for matrix in range(3) for index in range(len(chunks))]
    places, at = {}, 0
    for odd in range(2):
        for matrix, index in keys:
            if (matrix + index) % 2 == odd:
                places[matrix, index] = at
                at += chunks[index]
    border = sum(chunks[index] for matrix, index in keys if (matrix + index) % 2 == 0)
    return places, border, [(places[key], chunks[key[1]]) for key in keys]


def mlp(cot, hidden, wg, wu, wd, own, prior, rows, collective_id):
    total, depth = hidden.shape
    units = wg.shape[0]
    chips = total // (2 * rows)
    reduced = exchange_rows(units)[0] if own is None and lax.axis_size("dp") == 4 else {}
    quarter = depth // 4
    count = pl.cdiv(units, CHUNK)
    anywhere = pl.BlockSpec(memory_space=pl.ANY)
    local = pl.BlockSpec(memory_space=pltpu.VMEM)
    dma = pltpu.SemaphoreType.DMA
    vmem = pltpu.VMEM
    held = jax.ShapeDtypeStruct((3 * units, quarter), B16)

    inputs = {"cot": cot, "h_hbm": hidden, "wg_hbm": wg, "wu_hbm": wu, "wd_hbm": wd}
    if own is not None:
        inputs["own"] = own
    if prior is not None:
        inputs["prior"] = prior
    outputs = {
        "out": (anywhere, jax.ShapeDtypeStruct((total, depth), B16)),
        "grad": (local, jax.ShapeDtypeStruct((rows, depth), F32)),
        "sums": (anywhere, jax.ShapeDtypeStruct((2, 2, 3 * units, quarter), B16)),
    }
    if own is not None:
        outputs["whole"] = (anywhere, jax.ShapeDtypeStruct((total, depth), B16))
    if reduced:
        outputs["shard"] = (local, held)
        outputs["rest"] = (local, held)
        outputs["landing"] = (anywhere, jax.ShapeDtypeStruct((2, 3 * units, quarter), B16))
    scratch = {
        "wg": vmem((units, depth), B16),
        "wu": vmem((units, depth), B16),
        "wd": vmem((units, depth), B16),
        "h": vmem((total, depth), B16),
        "g": vmem((total, depth), B16),
        "act": vmem((total, units), B16),
        "dg": vmem((total, units), B16),
        "du": vmem((total, units), B16),
        "part": vmem((total, depth), B16),
        "xrecv": vmem((chips, rows, depth), B16),
        "zrecv": vmem((chips + 1, rows, depth), B16),
        "stage_out": vmem((2 * rows, depth), B16),
        "stage": vmem((2, 2, 2, CHUNK, quarter), B16),
        "weight_sem": dma((3, count)),
        "load_sem": dma((2, chips)),
        "xsend": dma((chips,)),
        "xrecv_sem": dma((chips,)),
        "zsend": dma((chips,)),
        "zrecv_sem": dma((chips + 1,)),
        "out_sem": dma((2,)),
        "stage_sem": dma((2,)),
    }
    if own is not None:
        scratch["local_sem"] = dma
        scratch["gather_send"] = dma((3, chips))
        scratch["gather_recv"] = dma((chips, 2))
    if prior is not None:
        scratch["before"] = vmem((2, 2, CHUNK, quarter), B16)
        scratch["before_sem"] = dma
    if reduced:
        scratch["held_own"] = vmem((2, 2, CHUNK, quarter), B16)
        scratch["held_got"] = vmem((2, 2, CHUNK, quarter), B16)
        scratch["held_sem"] = dma((2, 2))
        scratch["one_send"] = dma((3 * count,))
        scratch["one_recv"] = dma((3 * count,))
    names = [*inputs, *outputs, *scratch]
    out = pl.pallas_call(
        functools.partial(mlp_kernel, names, reduced),
        in_specs=[anywhere] * len(inputs),
        out_specs=[spec for spec, _ in outputs.values()],
        out_shape=[shape for _, shape in outputs.values()],
        scratch_shapes=list(scratch.values()),
        compiler_params=pltpu.CompilerParams(
            collective_id=collective_id, has_side_effects=True, vmem_limit_bytes=VMEM_MOST
        ),
        cost_estimate=pl.CostEstimate(
            flops=18 * total * depth * units, bytes_accessed=40 * total * depth, transcendentals=total * units
        ),
    )(*inputs.values())
    return dict(zip(outputs, out))


def widen_kernel(first_ref, second_ref, third_ref, *outs):
    for source, out in zip((first_ref, second_ref, third_ref), outs):
        quarter = source.shape[2]
        for at in range(4):
            out[:, at * quarter : (at + 1) * quarter] = source[at].astype(F32)


def widen(quarters, units):
    quarter = quarters.shape[2]
    steps = next(n for n in range(4, units) if units % (16 * n) == 0)
    size = units // steps
    return pl.pallas_call(
        widen_kernel,
        grid=(steps,),
        in_specs=[
            pl.BlockSpec((4, size, quarter), functools.partial(lambda base, i: (0, base + i, 0), at * steps))
            for at in range(3)
        ],
        out_specs=[pl.BlockSpec((size, 4 * quarter), lambda i: (i, 0))] * 3,
        out_shape=[jax.ShapeDtypeStruct((units, 4 * quarter), F32)] * 3,
        compiler_params=pltpu.CompilerParams(vmem_limit_bytes=VMEM_LIMIT),
        cost_estimate=pl.CostEstimate(flops=0, bytes_accessed=72 * units * quarter, transcendentals=0),
    )(quarters, quarters, quarters)


def norm_back(grad_out, normed, factor, gain):
    inner = grad_out * gain
    grad_rows = factor * (inner - normed * jnp.mean(inner * normed, axis=-1, keepdims=True))
    return (grad_rows, jnp.sum(grad_out * normed, axis=0))


def normalize(rows, gain):
    factor = lax.rsqrt(jnp.mean(rows * rows, axis=-1, keepdims=True) + EPS)
    normed = rows * factor
    return (normed, factor, (normed * gain).astype(B16))


def on_device(
    layer_input,
    lengths,
    attn_gain,
    query_proj,
    query_bias,
    key_proj,
    key_bias,
    value_proj,
    value_bias,
    out_proj,
    mlp_gain,
    gate_proj,
    up_proj,
    down_proj,
    cotangent,
):
    micros = layer_input.shape[0]
    rows = layer_input.shape[2]
    depth = layer_input.shape[3]
    tensor = lax.axis_index("tensor")
    total = rows * lax.axis_size("tensor")
    devices = lax.axis_size(("dp", "tensor"))
    size = query_proj.shape[0]
    small = key_bias.shape[0]
    offset = tensor * rows
    positions = offset + jnp.arange(rows, dtype=jnp.int32)
    cosine, sine = rope_tables(positions)

    valid = (positions[None, :] < lengths).astype(F32).reshape(micros, rows, 1)
    grad_rows = cotangent[:, 0].astype(F32) * valid
    low_rows = [grad_rows[m].astype(B16) for m in range(micros)]

    tail = jnp.concatenate([key_bias, value_bias, jnp.zeros((size - 2 * small,), B16)])
    extra = jnp.stack([attn_gain, query_bias, mlp_gain, tail], axis=1)
    extra = jnp.pad(extra, ((0, 0), (0, EXTRA - 4)))
    block = jnp.concatenate([query_proj, key_proj, value_proj, extra], axis=1)
    square = lax.axis_size("dp") == 4
    low = low_rows[0]
    if square:
        line = gather_line(block, 0)
        line, low = lax.optimization_barrier((line, low))
    cots = [lax.all_gather(low, "tensor", axis=0, tiled=True)]
    if square:
        packed, wout_line = gather_plane(line, 1, out_proj)
    else:
        packed = lax.all_gather(block, ("dp", "tensor"), axis=0, tiled=True)
    vectors = packed[:, QKV : QKV + 4].astype(F32)
    gain_one, gain_two = vectors[:, 0], vectors[:, 2]
    tails = vectors[:, 3].reshape(devices, size)
    bias = jnp.concatenate(
        [vectors[:, 1], tails[:, :small].reshape(-1), tails[:, small : 2 * small].reshape(-1)]
    )[None, :]

    inputs = layer_input[:, 0].astype(F32).reshape(micros * rows, depth)
    normed_one, factor_one, hidden = normalize(inputs, gain_one)
    qkv = project(
        hidden, packed, bias, jnp.tile(cosine, (micros, 1)), jnp.tile(sine, (micros, 1))
    )
    infos = [jnp.stack([lengths[m, 0], offset]) for m in range(micros)]

    own_kv = qkv[:, QW:].reshape(micros, rows, 2 * KW)
    own_kv, *cots = lax.optimization_barrier((own_kv, *cots))
    all_kv = lax.all_gather(own_kv, "tensor", axis=0)
    if square:
        wout_line, own_kv = lax.optimization_barrier((wout_line, own_kv))
        (wout,) = gather_plane(wout_line, 6)
    else:
        wout = lax.all_gather(out_proj, ("dp", "tensor"), axis=0, tiled=True)
    attended, logs, mixed, norm_two, hidden_two = [], [], [], [], []
    for m in range(micros):
        out, log = attend(infos[m], m, qkv, all_kv, rows)
        attended.append(out)
        logs.append(log)
        mixed.append(inputs[m * rows : (m + 1) * rows] + dot(out, wout))
        normed, factor, low = normalize(mixed[m], gain_two)
        norm_two.append((normed, factor))
        hidden_two.append(low)
        if m == 0:
            low, all_kv = lax.optimization_barrier((low, all_kv))
            whole = lax.all_gather(low, "tensor", axis=0, tiled=True)
    units = down_proj.shape[0]
    prior, grad_two, out_sums = None, [], []
    for m in range(1, micros):
        low, whole, *hidden_two = lax.optimization_barrier((low_rows[m], whole, *hidden_two))
        cots.append(lax.all_gather(low, "tensor", axis=0, tiled=True))
    for m in range(micros):
        own = hidden_two[m + 1] if m + 1 < micros else None
        done = mlp(cots[m], whole, gate_proj.T, up_proj.T, down_proj, own, prior, rows, 7 + m)
        whole, prior = done.get("whole"), done["sums"]
        grad_two.append(done["grad"])
        out_sums.append(lax.psum_scatter(done["out"], "tensor", scatter_dimension=0, tiled=True))
    if square:
        _, border, spans = exchange_rows(units)
        rest = done["rest"]
        got = jnp.concatenate([swap(rest[:border], "dp", 2), swap(rest[border:], "dp", 1)], axis=0)
    grad_mixed, gain_two_grads = [], []
    for m in range(micros):
        normed, factor = norm_two[m]
        grad, gain_grad = norm_back(grad_two[m], normed, factor, gain_two)
        gain_two_grads.append(gain_grad)
        grad_mixed.append(grad + grad_rows[m])

    grad_low = jnp.concatenate(grad_mixed, axis=0).astype(B16)
    acc_out = t_dot(jnp.concatenate(attended, axis=0), grad_low).astype(B16)
    grad_attended = dot_t(grad_low, wout).astype(B16)
    if square:
        got, grad_attended, acc_out = lax.optimization_barrier((got, grad_attended, acc_out))
        got = jnp.concatenate([got[at : at + width] for at, width in spans], axis=0)
        shard = (done["shard"].astype(F32) + got.astype(F32)).astype(B16)
        shard, grad_attended = lax.optimization_barrier((shard, grad_attended))
        weight_grads = lax.all_gather(shard, "dp", axis=0)
    else:
        weight_grads = lax.psum(prior, "dp").reshape(4, 3 * units, depth // 4)
    grad_q, grad_kv = attend_back(
        lengths[:, 0], qkv, all_kv, grad_attended, jnp.concatenate(logs, axis=0), cosine, sine, rows, 3
    )
    grad_kv = grad_kv.reshape(micros * rows, 2 * KW)
    grad_hidden = dot_t(grad_q, packed[:, :QW]) + dot_t(grad_kv, packed[:, QW:QKV])
    grad_in, gain_one_grad = norm_back(grad_hidden, normed_one, factor_one, gain_one)
    grad_bias = jnp.concatenate(
        [jnp.sum(grad_q.astype(F32), axis=0), jnp.sum(grad_kv.astype(F32), axis=0)]
    )
    acc_q = t_dot(hidden, grad_q).astype(B16)
    acc_kv = t_dot(hidden, grad_kv).astype(B16)
    tails = jnp.concatenate(
        [
            grad_bias[QW : QW + KW].reshape(devices, small),
            grad_bias[QW + KW :].reshape(devices, small),
            jnp.zeros((devices, size - 2 * small), F32),
        ],
        axis=1,
    ).reshape(-1)
    columns = jnp.stack([gain_one_grad, grad_bias[:QW], sum(gain_two_grads), tails], axis=1)
    columns = jnp.pad(columns.astype(B16), ((0, 0), (0, EXTRA - 4)))
    summed = scatter_weights([acc_out, acc_q, jnp.concatenate([acc_kv, columns], axis=1)], 2)
    out_sums, weight_grads, summed = lax.optimization_barrier((out_sums, weight_grads, summed))
    gate_total, up_total, down_total = widen(weight_grads, units)
    grad_out, grad_query, grad_rest = summed
    layer_output = jnp.stack(
        [(mixed[m] + out_sums[m].astype(F32)).astype(B16) for m in range(micros)]
    )[:, None]
    grad_input = (grad_in + jnp.concatenate(grad_mixed, axis=0)).reshape(micros, 1, rows, depth)
    return (
        layer_output,
        grad_input,
        grad_rest[:, 2 * KW],
        grad_query,
        grad_rest[:, 2 * KW + 1],
        grad_rest[:, :KW],
        grad_rest[:small, 2 * KW + 3],
        grad_rest[:, KW : 2 * KW],
        grad_rest[small : 2 * small, 2 * KW + 3],
        grad_out,
        grad_rest[:, 2 * KW + 2],
        gate_total.T,
        up_total.T,
        down_total,
    )


def solution(mesh):
    rows = P(None, "dp", "tensor", None)
    both = P(("dp", "tensor"))
    wide = P(("dp", "tensor"), None)
    placed = (
        rows,
        P(None, "dp"),
        both,
        wide,
        both,
        wide,
        both,
        wide,
        both,
        wide,
        both,
        P(None, "tensor"),
        P(None, "tensor"),
        P("tensor", None),
        rows,
    )
    return jax.shard_map(
        on_device,
        mesh=mesh,
        in_specs=placed,
        out_specs=(
            rows,
            rows,
            both,
            wide,
            both,
            wide,
            both,
            wide,
            both,
            wide,
            both,
            P(None, "tensor"),
            P(None, "tensor"),
            P("tensor", None),
        ),
        check_vma=False,
    )
```

time: 1070 us -> 683 us (0.64)
  Pallas kernels: 80.7 us -> 503 us
  waiting for transfers between devices: 398 us -> 59.8 us
  starting transfers between devices: 186 us -> 2.38 us
  matrix products: 198 us -> 29.6 us
  other arithmetic: 117 us -> 32.9 us
  local copies, waits for them, and re-layouts: 63.3 us -> 31.5 us
    pallas_call x2 -> x8, Pallas kernels: 43.5 us -> 465 us  [the longest x2 205 us: mlp(): pl.pallas_call(functools.partial(mlp_kernel, names, reduced), in_specs=[a...]
    ppermute x60 -> x0, starting transfers between devices: 162 us -> none  [the longest x24 102 us: line_scatter(): lax.ppermute(ahead.astype(B16), 'tensor', [(i, i + 2) for i in range(2 *...]
    ppermute x60 -> x0, waiting for transfers between devices: 135 us -> none  [the longest x24 91.4 us: line_scatter(): lax.ppermute(ahead.astype(B16), 'tensor', [(i, i + 2) for i in range(2 *...]
    ppermute x26 -> x2, waiting for transfers between devices: 124 us -> 19.8 us  [swap(): return lax.ppermute(value, axis, [(i, i ^ bit) for i in range(count)])]
    all_gather x6 -> x5, waiting for transfers between devices: 138 us -> 39.9 us  [the longest x1 30.3 us: on_device(): whole = lax.all_gather(low, 'tensor', axis=0, tiled=True)]
    dot_general x9 -> x3, matrix products: 75.1 us -> 12.3 us  [dot_t(): lax.dot_general(a, b, (((1,), (1,)), ((), ())), preferred_element_type=F32)]
    dot_general x8 -> x2, matrix products: 61.2 us -> 5.31 us  [dot(): return jnp.dot(a, b, preferred_element_type=F32)]
    dot_general x8 -> x3, matrix products: 61.9 us -> 12 us  [t_dot(): lax.dot_general(a, b, (((0,), (0,)), ((), ())), preferred_element_type=F32)]
  transfers between devices with their start and end apart: 93 -> 9, of which waited for: 37 -> 4; matrix products, arithmetic and copies ran while one was open for 28% -> 10% of each run, Pallas kernels for 6% -> 67%
where the time goes in v3:
time: 683 us; the launch traced here: 675 us
  Pallas kernels  503 us (74%)
  waiting for transfers between devices  59.8 us (9%)
  other arithmetic  32.9 us (5%)
  local copies, waits for them, and re-layouts  31.5 us (5%)
  matrix products  29.6 us (4%)
  between operations  15.3 us (2%)
    pallas_call x2, Pallas kernels, mlp(): pl.pallas_call(functools.partial(mlp_kernel, names, reduced), in_specs=[a...  205 us
    pallas_call x1, Pallas kernels, scatter_weights(): pl.pallas_call(functools.partial(scatter_kernel, parts, len(grads)), in_s...  90.4 us
    pallas_call x2, Pallas kernels, gather_plane(): pl.pallas_call(functools.partial(plane_kernel, more is not None), in_spec...  70.3 us
    pallas_call x1, Pallas kernels, attend_back(): pl.pallas_call(functools.partial(attend_back_kernel, [*inputs, *outputs,...  60.1 us
    all_gather x1, waiting for transfers between devices, on_device(): whole = lax.all_gather(low, 'tensor', axis=0, tiled=True)  30.3 us
    pallas_call x2, Pallas kernels, attend(): pl.pallas_call(attend_kernel, grid_spec=pltpu.PrefetchScalarGridSpec(num_...  29 us
    pallas_call x1, Pallas kernels, gather_line(): pl.pallas_call(line_kernel, in_specs=[pl.BlockSpec(memory_space=pl.ANY)],...  28.4 us
    ppermute x2, waiting for transfers between devices, swap(): return lax.ppermute(value, axis, [(i, i ^ bit) for i in range(count)])  19.8 us
  transfers between devices with their start and end apart: 9, of which 4 were waited for; matrix products, arithmetic and copies ran while one was open for 10% of the time, Pallas kernels for 67%

profile of v3, /device:TPU:0, one launch (start us, length us, event | category | flops | bytes accessed | tf_op | source)
XLA Modules:
  0.0 674.6 jit_solution(8121440858317162956)
XLA Ops:
  11.0 28.4 %shard_map.257.line_ref = bf16[4,48,2176]{2,1,0:T(8,128)(2,1)} custom-call(bf16[48,2176]{1,0:T(8,128)(2,1)} %fusion.19.block_ref), custom_call_target="tpu_custom_call" | custom-call | bytes 10444800 | tf_op jit(solution)/shard_map/pallas_call | solution.py:246
  45.1 43.7 %shard_map.258 = (bf16[32,48,2176]{2,1,0:T(8,128)(2,1)}, bf16[4,48,1536]{2,1,0:T(8,128)(2,1)}) custom-call(bf16[4,48,2176]{2,1,0:T(8,128)(2,1)} %shard_map.257.line_ref, bf16[48,1536]{1,0:T(8,128)(2,1)} %refs_0_.1), custom_call_target="tpu_custom_call" | custom-call | bytes 25067520 | tf_op jit(solution)/shard_map/pallas_call | solution.py:268
  95.8 8.9 %shard_map.259.q_ref.refs_1_ = bf16[384,2048]{1,0:T(8,128)(2,1)} custom-call(bf16[384,1536]{1,0:T(8,128)(2,1)} %multiply_convert_fusion.1.hidden_ref, bf16[1536,2176]{1,0:T(8,128)(2,1)} %bitcast.95, f32[1,2048]{1,0:T(1,128)} %bitcast.107, f32[384,128]{1,0:T(8,128)} %bitcast.105, f32[384,128]{1,0:T(8,128)} %bitcast.106), custom_call_target="tpu_custom_call" | custom-call | flops 2415919104 | bytes 9043968 | tf_op jit(solution)/shard_map/pallas_call | solution.py:487
  110.0 26.6 %shard_map.261 = bf16[32,48,1536]{2,1,0:T(8,128)(2,1)} custom-call(bf16[4,48,1536]{2,1,0:T(8,128)(2,1)} %get-tuple-element.63.line_ref), custom_call_target="tpu_custom_call" | custom-call | bytes 17694720 | tf_op jit(solution)/shard_map/pallas_call | solution.py:268
  136.6 9.6 %all-gather.14.cloned.1.call-done = bf16[16,192,512]{2,1,0:T(8,128)(2,1)} async-done(((bf16[2,192,512]{2,1,0:T(8,128)(2,1)}), bf16[16,192,512]{2,1,0:T(8,128)(2,1)}) %all-gather.14.cloned.1.call-update) | async-done | bytes 3145744 | tf_op jit(solution)/shard_map/all_gather | solution.py:1336
  146.2 14.5 %shard_map.260 = (bf16[192,1536]{1,0:T(8,128)(2,1)}, f32[192,1536]{1,0:T(8,128)}) custom-call(s32[2]{0:T(128)} %pad_add_fusion.info_ref, bf16[384,2048]{1,0:T(8,128)(2,1)} %shard_map.259.q_ref.refs_1_, bf16[8,2,192,512]{3,2,1,0:T(8,128)(2,1)} %bitcast.119, bf16[8,2,192,512]{3,2,1,0:T(8,128)(2,1)} %bitcast.120), custom_call_target="tpu_custom_call" | custom-call | flops 3623878656 | bytes 3932160 | tf_op jit(solution)/shard_map/pallas_call | solution.py:537
  160.7 2.6 multiply_reduce_fusion.8
  166.3 14.5 %shard_map.262 = (bf16[192,1536]{1,0:T(8,128)(2,1)}, f32[192,1536]{1,0:T(8,128)}) custom-call(s32[2]{0:T(128)} %pad_add_fusion.1.info_ref, bf16[384,2048]{1,0:T(8,128)(2,1)} %shard_map.259.q_ref.refs_1_, bf16[8,2,192,512]{3,2,1,0:T(8,128)(2,1)} %bitcast.121, bf16[8,2,192,512]{3,2,1,0:T(8,128)(2,1)} %bitcast.122), custom_call_target="tpu_custom_call" | custom-call | flops 3623878656 | bytes 3932160 | tf_op jit(solution)/shard_map/pallas_call | solution.py:537
  180.8 2.7 multiply_reduce_fusion.7
  185.5 30.3 %all-gather.10.cloned.1.call-done.refs_1_ = bf16[1536,1536]{1,0:T(8,128)(2,1)} async-done(((bf16[192,1536]{1,0:T(8,128)(2,1)}), bf16[1536,1536]{1,0:T(8,128)(2,1)}) %all-gather.10.cloned.1.call-update) | async-done | bytes 4718608 | tf_op jit(solution)/shard_map/all_gather | solution.py:1353
  215.8 105.6 %shard_map.263 = (bf16[1536,1536]{1,0:T(8,128)(2,1)}, f32[192,1536]{1,0:T(8,128)}, bf16[2,2,3360,384]{3,2,1,0:T(8,128)(2,1)}, bf16[1536,1536]{1,0:T(8,128)(2,1)}) custom-call(bf16[1536,1536]{1,0:T(8,128)(2,1)} %all-gather.8.cloned.1.call-done.refs_0_, bf16[1536,1536]{1,0:T(8,128)(2,1)} %all-gather.10.cloned.1.call-done.refs_1_, ...), custom_call_target="tpu_custom_call" | custom-call | flops 47563407360 | bytes 94371840 | tf_op jit(solution)/shard_map/pallas_call | solution.py:1220
  321.6 99.1 %shard_map.264 = (bf16[1536,1536]{1,0:T(8,128)(2,1)}, f32[192,1536]{1,0:T(8,128)}, bf16[2,2,3360,384]{3,2,1,0:T(8,128)(2,1)}, bf16[3360,384]{1,0:T(8,128)(2,1)},...) custom-call(bf16[1536,1536]{1,0:T(8,128)(2,1)} %all-gather.12.cloned.1.call-done.refs_0_, ...), custom_call_target="tpu_custom_call" | custom-call | flops 47563407360 | bytes 94371840 | tf_op jit(solution)/shard_map/pallas_call | solution.py:1220
  428.9 4.5 convolution_convert_fusion.1
  433.4 3.0 convolution_convert_fusion.3.refs_4_
  436.5 17.0 %collective-permute-done.1 = bf16[1632,384]{1,0:T(8,128)(2,1)S(1)} collective-permute-done((bf16[1632,384]{1,0:T(8,128)(2,1)S(1)}, bf16[1632,384]{1,0:T(8,128)(2,1)S(1)}, u32[]{:S(2)}, u32[]{:S(2)}) %collective-permute-start.1) | collective-permute-done | bytes 1253408 | tf_op jit(solution)/shard_map/ppermute | solution.py:57
  453.5 2.8 collective-permute-done
  458.3 2.2 add_convert_fusion
  465.5 60.1 %shard_map.265 = (bf16[384,1536]{1,0:T(8,128)(2,1)}, bf16[2,192,512]{2,1,0:T(8,128)(2,1)}) custom-call(s32[2]{0:T(128)} %bitcast.109, bf16[384,2048]{1,0:T(8,128)(2,1)} %shard_map.259.q_ref.refs_1_, bf16[8,2,192,512]{3,2,1,0:T(8,128)(2,1)} %bitcast.123, bf16[8,2,192,512]{3,2,1,0:T(8,128)(2,1)} %bitcast.124, ...), custom_call_target="tpu_custom_call" | custom-call | flops 18119393280 | bytes 13369344 | tf_op jit(solution)/shard_map/pallas_call | solution.py:722
  532.5 4.8 fusion
  537.3 4.5 multiply_reduce_fusion
  544.3 4.2 copy.47
  548.6 6.5 convolution_convert_fusion
  555.0 90.4 %shard_map.266 = (f32[48,1536]{1,0:T(8,128)}, f32[48,1536]{1,0:T(8,128)}, f32[48,640]{1,0:T(8,128)}) custom-call(bf16[16,2,48,1536]{3,2,1,0:T(8,128)(2,1)} %bitcast.99, bf16[16,2,48,1536]{3,2,1,0:T(8,128)(2,1)} %bitcast.100, bf16[16,2,48,640]{3,2,1,0:T(8,128)(2,1)} %bitcast.93), custom_call_target="tpu_custom_call" | custom-call | bytes 45613056 | tf_op jit(solution)/shard_map/pallas_call | solution.py:444
  653.3 11.4 %shard_map.267 = (f32[1120,1536]{1,0:T(8,128)}, f32[1120,1536]{1,0:T(8,128)}, f32[1120,1536]{1,0:T(8,128)}) custom-call(bf16[4,3360,384]{2,1,0:T(8,128)(2,1)} %bitcast.83, bf16[4,3360,384]{2,1,0:T(8,128)(2,1)} %bitcast.84, bf16[4,3360,384]{2,1,0:T(8,128)(2,1)} %bitcast.85), custom_call_target="tpu_custom_call" | custom-call | bytes 30965760 | tf_op jit(solution)/shard_map/pallas_call | solution.py:1247
  (194 shorter events, 61.5 us)
Async XLA Ops:
  7.2 99.3 %all-gather.8.cloned.1.call-start = ((), (), s32[]{:S(2)}) async-start(), calls=%async_computation.2 | async-start | bytes 5308416 | tf_op jit(solution)/shard_map/all_gather | solution.py:1315
  44.2 102.0 %all-gather.14.cloned.1.call-start = ((), (), s32[]{:S(2)}) async-start(), calls=%async_computation.7 | async-start | bytes 3538944 | tf_op jit(solution)/shard_map/all_gather | solution.py:1336
  45.0 46.4 %copy-start.32 = (f32[2,192]{1,0:T(2,128)}, f32[2,192]{1,0:T(2,128)S(1)}, u32[]{:S(2)}) copy-start(f32[2,192]{1,0:T(2,128)S(1)} %add_rsqrt_fusion) | copy-start | bytes 4612
  45.1 47.9 %copy-start.29 = (f32[384]{0:T(512)}, f32[384]{0:T(512)S(1)}, u32[]{:S(2)}) copy-start(f32[384]{0:T(512)S(1)} %rsqrt.29) | copy-start | bytes 4612
  92.9 11.8 %copy-start.21 = (f32[192,128]{1,0:T(8,128)}, f32[192,128]{1,0:T(8,128)S(1)}, u32[]{:S(2)}) copy-start(f32[192,128]{1,0:T(8,128)S(1)} %pad_maximum_fusion.4.refs_6_) | copy-start | bytes 294916
  93.0 11.7 %copy-start.22 = (f32[192,128]{1,0:T(8,128)}, f32[192,128]{1,0:T(8,128)S(1)}, u32[]{:S(2)}) copy-start(f32[192,128]{1,0:T(8,128)S(1)} %pad_maximum_fusion.5.refs_7_) | copy-start | bytes 294916
  106.5 109.3 %all-gather.10.cloned.1.call-start = ((), (), s32[]{:S(2)}) async-start(), calls=%async_computation.3 | async-start | bytes 5308416 | tf_op jit(solution)/shard_map/all_gather | solution.py:1353
  146.2 14.5 %copy-start = (bf16[32,48,1536]{2,1,0:T(8,128)(2,1)S(1)}, bf16[32,48,1536]{2,1,0:T(8,128)(2,1)}, u32[]{:S(2)}) copy-start(bf16[32,48,1536]{2,1,0:T(8,128)(2,1)} %shard_map.261) | copy-start | bytes 14155780
  165.0 15.8 %slice-start = ((s8[4718592]{0:T(1024)(128)(4,1)}), s8[524288]{0:T(1024)(128)(4,1)S(1)}, s32[]{:S(2)}) async-start(s8[4718592]{0:T(1024)(128)(4,1)} %bitcast.87), calls=%async_computation.9 | async-start | bytes 1048576
  165.0 156.6 %all-gather.12.cloned.1.call-start = ((), (), s32[]{:S(2)}) async-start(), calls=%async_computation.5 | async-start | bytes 5308416 | tf_op jit(solution)/shard_map/all_gather | solution.py:1358
  166.3 14.5 %slice-start.1 = ((s8[4718592]{0:T(1024)(128)(4,1)}), s8[4194304]{0:T(1024)(128)(4,1)S(1)}, s32[]{:S(2)}) async-start(s8[4718592]{0:T(1024)(128)(4,1)} %bitcast.87), calls=%async_computation.10 | async-start | bytes 8388608
  215.8 431.7 %reduce-scatter.3.cloned.1.call-start = ((), (), s32[]{:S(2)}) async-start(), calls=%async_computation.4 | async-start | bytes 5308416 | tf_op jit(solution)/shard_map/reduce_scatter | solution.py:1364
  321.5 326.0 %reduce-scatter.5.cloned.1.call-start = ((), (), s32[]{:S(2)}) async-start(), calls=%async_computation.6 | async-start | bytes 5308416 | tf_op jit(solution)/shard_map/reduce_scatter | solution.py:1364
  420.7 226.8 %all-gather.16.cloned.1.call-start = ((), (), s32[]{:S(2)}) async-start(), calls=%async_computation.8 | async-start | bytes 12902400 | tf_op jit(solution)/shard_map/all_gather | solution.py:1384
  420.8 5.2 copy-start.3
  423.9 29.7 %collective-permute-start.1 = (bf16[1632,384]{1,0:T(8,128)(2,1)S(1)}, bf16[1632,384]{1,0:T(8,128)(2,1)S(1)}, u32[]{:S(2)}, u32[]{:S(2)}) collective-permute-start(bf16[1632,384]{1,0:T(8,128)(2,1)S(1)} %slice.171), channel_id=1, source_target_pairs={{0,8},{8,0},{16,24},{24,16},{1,9},{9,1},{17,25},{25,17},{2,10},{10... | collective-permute-start | bytes 3760136 | tf_op jit(solution)/shard_map/ppermute | solution.py:57
  425.4 30.9 %collective-permute-start = (bf16[1728,384]{1,0:T(8,128)(2,1)S(1)}, bf16[1728,384]{1,0:T(8,128)(2,1)S(1)}, u32[]{:S(2)}, u32[]{:S(2)}) collective-permute-start(bf16[1728,384]{1,0:T(8,128)(2,1)S(1)} %slice.170), channel_id=1, source_target_pairs={{0,16},{8,24},{16,0},{24,8},{1,17},{9,25},{17,1},{25,9},{2,18},{10... | collective-permute-start | bytes 3981320 | tf_op jit(solution)/shard_map/ppermute | solution.py:57
  427.7 5.7 slice-start.2
  555.0 90.4 %copy-start.39 = (f32[384]{0:T(512)S(1)}, f32[384]{0:T(512)}, u32[]{:S(2)}) copy-start(f32[384]{0:T(512)} %get-tuple-element.142) | copy-start | bytes 4612
  555.0 90.4 %copy-start.7 = (f32[192,1536]{1,0:T(8,128)S(1)}, f32[192,1536]{1,0:T(8,128)}, u32[]{:S(2)}) copy-start(f32[192,1536]{1,0:T(8,128)} %copy-done.6) | copy-start | bytes 3538948
  555.0 90.4 %copy-start.9 = (f32[192,1536]{1,0:T(8,128)S(1)}, f32[192,1536]{1,0:T(8,128)}, u32[]{:S(2)}) copy-start(f32[192,1536]{1,0:T(8,128)} %copy-done.8) | copy-start | bytes 3538948
  555.0 90.4 %copy-start.14 = (f32[384,1536]{1,0:T(8,128)S(1)}, f32[384,1536]{1,0:T(8,128)}, u32[]{:S(2)}) copy-start(f32[384,1536]{1,0:T(8,128)} %get-tuple-element.180) | copy-start | bytes 7077892
  555.0 90.4 %copy-start.31 = (f32[384]{0:T(512)S(1)}, f32[384]{0:T(512)}, u32[]{:S(2)}) copy-start(f32[384]{0:T(512)} %copy-done.29) | copy-start | bytes 4612
  647.5 5.7 copy-start.20
  (29 other events, 83.9 us)
Sparse Core Ops, SparseCore 0:
  44.3 55.1 all-gather.7
  106.6 39.5 all-gather.13
  165.1 50.6 all-gather.9
  217.3 70.6 all-gather.11
  321.6 63.2 reduce-scatter.2
  420.8 60.9 reduce-scatter.4
  484.2 124.8 all-gather.15

commit v4 on v3

--- a/solution.py
+++ b/solution.py
@@ -19,6 +19,8 @@
 ROPE_BASE = 1000000.0
 EPS = 1e-06
 MASKED = -1e30
+LOG2E = 1.4426950408889634
+HEADS = 3
 F32 = jnp.float32
 B16 = jnp.bfloat16
 VMEM_LIMIT = 56 * 1024 * 1024
@@ -522,13 +524,14 @@
         fill_bias(info_ref, bias)
 
     keys, values = flat(k_ref), flat(v_ref)
-    scores = dot_t(q_ref[...], keys) * (HD**-0.5) + bias[...]
-    top = jnp.max(scores, axis=-1, keepdims=True)
-    expd = jnp.exp(scores - top)
-    summed = jnp.sum(expd, axis=-1, keepdims=True)
-    probs = (expd * (1.0 / summed)).astype(B16)
-    out_ref[...] = dot(probs, values).astype(B16)
-    log_ref[...] = jnp.broadcast_to(top + jnp.log(summed), log_ref.shape)
+    for head in range(HEADS):
+        cut = slice(head * HD, (head + 1) * HD)
+        scores = dot_t(q_ref[:, cut], keys) * (HD**-0.5 * LOG2E) + bias[...]
+        top = jnp.max(scores, axis=-1, keepdims=True)
+        expd = jnp.exp2(scores - top)
+        summed = jnp.sum(expd, axis=-1, keepdims=True)
+        out_ref[:, cut] = (dot(expd.astype(B16), values) * (1.0 / summed)).astype(B16)
+        log_ref[:, cut] = jnp.broadcast_to(top + jnp.log2(summed), (q_ref.shape[0], HD))
 
 
 def attend(info, micro, qkv, keys_values, rows):
@@ -538,15 +541,15 @@
         attend_kernel,
         grid_spec=pltpu.PrefetchScalarGridSpec(
             num_scalar_prefetch=1,
-            grid=(H,),
+            grid=(H // HEADS,),
             in_specs=[
-                pl.BlockSpec((rows, HD), lambda h, info: (micro, h)),
-                pl.BlockSpec((parts, 1, rows, HD), lambda h, info: (0, micro, 0, h // GROUPS)),
-                pl.BlockSpec((parts, 1, rows, HD), lambda h, info: (0, micro, 0, KV + h // GROUPS)),
+                pl.BlockSpec((rows, HEADS * HD), lambda h, info: (micro, h)),
+                pl.BlockSpec((parts, 1, rows, HD), lambda h, info: (0, micro, 0, h * HEADS // GROUPS)),
+                pl.BlockSpec((parts, 1, rows, HD), lambda h, info: (0, micro, 0, KV + h * HEADS // GROUPS)),
             ],
             out_specs=[
-                pl.BlockSpec((rows, HD), lambda h, info: (0, h)),
-                pl.BlockSpec((rows, HD), lambda h, info: (0, h)),
+                pl.BlockSpec((rows, HEADS * HD), lambda h, info: (0, h)),
+                pl.BlockSpec((rows, HEADS * HD), lambda h, info: (0, h)),
             ],
             scratch_shapes=[pltpu.VMEM((rows, total), F32)],
         ),
@@ -570,7 +573,9 @@
     rows = r.q.shape[0]
     step = pl.program_id(0)
     micros = r.sums.shape[0]
-    micro, head = step // H, lax.rem(step, H)
+    turns = H // HEADS
+    micro, turn = step // turns, lax.rem(step, turns)
+    span = GROUPS // HEADS
     pieces = micros * KV
     scale = HD**-0.5
 
@@ -601,25 +606,29 @@
     def _():
         greet(spot, False, "all")
 
-    @pl.when(head == 0)
+    @pl.when(turn == 0)
     def _():
         shape = r.bias.shape
         place = spot.tensor * rows + lax.broadcasted_iota(jnp.int32, shape, 0)
         keys_at = lax.broadcasted_iota(jnp.int32, shape, 1)
         r.bias[...] = jnp.where((keys_at <= place) & (keys_at < r.length[micro]), 0.0, MASKED)
 
-    queries, keys, values, grads = r.q[...], flat(r.k), flat(r.v), r.g[...]
-    scores = dot_t(queries, keys) * scale + r.bias[...]
-    probs = jnp.exp(scores - r.log[:, :1])
-    grad_probs = dot_t(grads, values)
-    inner = jnp.sum(grad_probs * probs, axis=-1, keepdims=True)
-    grad_scores = (probs * (grad_probs - inner)).astype(B16)
-    grad_q = dot(grad_scores, keys) * scale
-    turned = grad_q * r.cos[...] - pltpu.roll(grad_q, HD // 2, 1) * r.sin[...]
-    r.dq[...] = turned.astype(B16)
-    grad_k = t_dot(grad_scores, queries) * scale
-    grad_v = t_dot(probs.astype(B16), grads)
-    first = lax.rem(head, GROUPS) == 0
+    keys, values = flat(r.k), flat(r.v)
+    grad_k = grad_v = 0.0
+    for head in range(HEADS):
+        cut = slice(head * HD, (head + 1) * HD)
+        queries, grads = r.q[:, cut], r.g[:, cut]
+        scores = dot_t(queries, keys) * (scale * LOG2E) + r.bias[...]
+        probs = jnp.exp2(scores - r.log[:, head * HD : head * HD + 1])
+        grad_probs = dot_t(grads, values)
+        inner = jnp.sum(grad_probs * probs, axis=-1, keepdims=True)
+        grad_scores = (probs * (grad_probs - inner)).astype(B16)
+        grad_q = dot(grad_scores, keys) * scale
+        turned = grad_q * r.cos[...] - pltpu.roll(grad_q, HD // 2, 1) * r.sin[...]
+        r.dq[:, cut] = turned.astype(B16)
+        grad_k = grad_k + t_dot(grad_scores, queries)
+        grad_v = grad_v + t_dot(probs.astype(B16), grads)
+    first = lax.rem(turn, span) == 0
 
     @pl.when(first)
     def _():
@@ -633,20 +642,20 @@
 
     for piece in range(pieces):
 
-        @pl.when(step == (piece + 1) * GROUPS - 1)
+        @pl.when(step == (piece + 1) * span - 1)
         def _():
             shape = (chips, 2, rows, HD)
-            r.part[piece, :, :, :, :HD] = r.dk_acc[...].reshape(shape).astype(B16)
+            r.part[piece, :, :, :, :HD] = (r.dk_acc[...] * scale).reshape(shape).astype(B16)
             r.part[piece, :, :, :, HD:] = r.dv_acc[...].reshape(shape).astype(B16)
             swapped(piece).start()
 
         if piece + 1 < pieces:
 
-            @pl.when(step == (piece + 1) * GROUPS)
+            @pl.when(step == (piece + 1) * span)
             def _():
                 spread(piece)
 
-    @pl.when(step == pieces * GROUPS - 1)
+    @pl.when(step == pieces * span - 1)
     def _():
         spread(pieces - 1)
         for piece in range(pieces):
@@ -678,30 +687,31 @@
     chips = parts // 2
     total = parts * rows
     pieces = micros * KV
+    turns = H // HEADS
     dma = pltpu.SemaphoreType.DMA
     vmem = pltpu.VMEM
 
     def heads(step):
-        return (step // H, step % H)
+        return (step // turns, step % turns)
 
     inputs = {
         "length": (pl.BlockSpec(memory_space=pltpu.SMEM), lengths),
-        "q": (pl.BlockSpec((rows, HD), heads), qkv),
+        "q": (pl.BlockSpec((rows, HEADS * HD), heads), qkv),
         "k": (
-            pl.BlockSpec((parts, 1, rows, HD), lambda s: (0, s // H, 0, s % H // GROUPS)),
+            pl.BlockSpec((parts, 1, rows, HD), lambda s: (0, s // turns, 0, s % turns * HEADS // GROUPS)),
             keys_values,
         ),
         "v": (
-            pl.BlockSpec((parts, 1, rows, HD), lambda s: (0, s // H, 0, KV + s % H // GROUPS)),
+            pl.BlockSpec((parts, 1, rows, HD), lambda s: (0, s // turns, 0, KV + s % turns * HEADS // GROUPS)),
             keys_values,
         ),
-        "g": (pl.BlockSpec((rows, HD), heads), grads),
-        "log": (pl.BlockSpec((rows, HD), heads), logs),
+        "g": (pl.BlockSpec((rows, HEADS * HD), heads), grads),
+        "log": (pl.BlockSpec((rows, HEADS * HD), heads), logs),
         "cos": (pl.BlockSpec((rows, HD), lambda s: (0, 0)), cosine),
         "sin": (pl.BlockSpec((rows, HD), lambda s: (0, 0)), sine),
     }
     outputs = {
-        "dq": (pl.BlockSpec((rows, HD), heads), jax.ShapeDtypeStruct((micros * rows, QW), B16)),
+        "dq": (pl.BlockSpec((rows, HEADS * HD), heads), jax.ShapeDtypeStruct((micros * rows, QW), B16)),
         "sums": (
             pl.BlockSpec((micros, rows, 2 * KW), lambda s: (0, 0, 0)),
             jax.ShapeDtypeStruct((micros, rows, 2 * KW), B16),
@@ -721,7 +731,7 @@
     }
     return pl.pallas_call(
         functools.partial(attend_back_kernel, [*inputs, *outputs, *scratch], parts),
-        grid=(micros * H,),
+        grid=(micros * turns,),
         in_specs=[spec for spec, _ in inputs.values()],
         out_specs=[spec for spec, _ in outputs.values()],
         out_shape=[shape for _, shape in outputs.values()],
@@ -982,10 +992,17 @@
         r.shard[place(matrix, start, width), :] = (
             r.held_own[slot, mine, :width].astype(F32) + r.held_got[slot, mine, :width].astype(F32)
         ).astype(B16)
-        at = reduced[matrix, index]
-        r.rest[at : at + width, :] = (
+        r.rest[place(matrix, start, width), :] = (
             r.held_own[slot, 1 - mine, :width].astype(F32) + r.held_got[slot, 1 - mine, :width].astype(F32)
         ).astype(B16)
+        passed(matrix, index).start()
+
+    def passed(matrix, index):
+        start, width = chunks[index]
+        here = place(matrix, start, width)
+        at = matrix * len(chunks) + index
+        peer = spot.over_y if (matrix + index) % 2 == 0 else spot.over_x
+        return remote(r.rest.at[here], r.got_rest.at[here], r.two_send.at[at], r.two_recv.at[at], peer)
 
     def weight_grads(matrix, left, right):
         def put(start, width, slot):
@@ -1046,7 +1063,7 @@
             for index in range(len(chunks)):
                 for copy in weight_load(index):
                     copy.start()
-    greet(spot, bool(reduced), "near")
+    greet(spot, reduced, "near")
     if has_next:
         gather_start()
 
@@ -1055,7 +1072,7 @@
         g_load(block).wait()
 
     todo = [(matrix, index) for matrix in (2, 0, 1) for index in range(len(chunks))] if reduced else []
-    share = pl.cdiv(len(todo), chips)
+    share = pl.cdiv(len(todo), chips + 2)
     loading = []
 
     def some():
@@ -1115,8 +1132,10 @@
         lax.fori_loop(0, chips, unit_back, 0)
         finish(block_at(chips - 1))
         weight_grads(0, r.dg, r.h)
+        some()
         relay(0)
         weight_grads(1, r.du, r.h)
+        some()
         for point in range(1, chips - 2):
             relay(point)
     for block in range(chips):
@@ -1127,8 +1146,14 @@
     for index in range(2):
         put_out(0, index).wait()
     if reduced:
+        for matrix in (2, 0, 1):
+            for index, (start, width) in enumerate(chunks):
+                here = place(matrix, start, width)
+                passed(matrix, index).wait_recv()
+                r.shard[here, :] = (r.shard[here, :].astype(F32) + r.got_rest[here, :].astype(F32)).astype(B16)
         for matrix in range(3):
             for index, (start, width) in enumerate(chunks):
+                passed(matrix, index).wait_send()
                 exchanged(matrix, index, start, width, (matrix + index) % 2 == 0).wait_send()
     for block in range(chips):
         swapped(block).wait_send()
@@ -1138,24 +1163,11 @@
         gather_end()
 
 
-def exchange_rows(units):
-    chunks = [min(CHUNK, units - start) for start in range(0, units, CHUNK)]
-    keys = [(matrix, index) for matrix in range(3) for index in range(len(chunks))]
-    places, at = {}, 0
-    for odd in range(2):
-        for matrix, index in keys:
-            if (matrix + index) % 2 == odd:
-                places[matrix, index] = at
-                at += chunks[index]
-    border = sum(chunks[index] for matrix, index in keys if (matrix + index) % 2 == 0)
-    return places, border, [(places[key], chunks[key[1]]) for key in keys]
-
-
 def mlp(cot, hidden, wg, wu, wd, own, prior, rows, collective_id):
     total, depth = hidden.shape
     units = wg.shape[0]
     chips = total // (2 * rows)
-    reduced = exchange_rows(units)[0] if own is None and lax.axis_size("dp") == 4 else {}
+    reduced = own is None and lax.axis_size("dp") == 4
     quarter = depth // 4
     count = pl.cdiv(units, CHUNK)
     anywhere = pl.BlockSpec(memory_space=pl.ANY)
@@ -1178,7 +1190,6 @@
         outputs["whole"] = (anywhere, jax.ShapeDtypeStruct((total, depth), B16))
     if reduced:
         outputs["shard"] = (local, held)
-        outputs["rest"] = (local, held)
         outputs["landing"] = (anywhere, jax.ShapeDtypeStruct((2, 3 * units, quarter), B16))
     scratch = {
         "wg": vmem((units, depth), B16),
@@ -1211,6 +1222,10 @@
         scratch["before"] = vmem((2, 2, CHUNK, quarter), B16)
         scratch["before_sem"] = dma
     if reduced:
+        scratch["rest"] = vmem(held.shape, B16)
+        scratch["got_rest"] = vmem(held.shape, B16)
+        scratch["two_send"] = dma((3 * count,))
+        scratch["two_recv"] = dma((3 * count,))
         scratch["held_own"] = vmem((2, 2, CHUNK, quarter), B16)
         scratch["held_got"] = vmem((2, 2, CHUNK, quarter), B16)
         scratch["held_sem"] = dma((2, 2))
@@ -1361,11 +1376,13 @@
         done = mlp(cots[m], whole, gate_proj.T, up_proj.T, down_proj, own, prior, rows, 7 + m)
         whole, prior = done.get("whole"), done["sums"]
         grad_two.append(done["grad"])
-        out_sums.append(lax.psum_scatter(done["out"], "tensor", scatter_dimension=0, tiled=True))
+        if m + 1 < micros:
+            out_sums.append(lax.psum_scatter(done["out"], "tensor", scatter_dimension=0, tiled=True))
     if square:
-        _, border, spans = exchange_rows(units)
-        rest = done["rest"]
-        got = jnp.concatenate([swap(rest[:border], "dp", 2), swap(rest[border:], "dp", 1)], axis=0)
+        shard, *out_sums = lax.optimization_barrier((done["shard"], *out_sums))
+        weight_grads = lax.all_gather(shard, "dp", axis=0)
+    else:
+        weight_grads = lax.psum(prior, "dp").reshape(4, 3 * units, depth // 4)
     grad_mixed, gain_two_grads = [], []
     for m in range(micros):
         normed, factor = norm_two[m]
@@ -1376,14 +1393,6 @@
     grad_low = jnp.concatenate(grad_mixed, axis=0).astype(B16)
     acc_out = t_dot(jnp.concatenate(attended, axis=0), grad_low).astype(B16)
     grad_attended = dot_t(grad_low, wout).astype(B16)
-    if square:
-        got, grad_attended, acc_out = lax.optimization_barrier((got, grad_attended, acc_out))
-        got = jnp.concatenate([got[at : at + width] for at, width in spans], axis=0)
-        shard = (done["shard"].astype(F32) + got.astype(F32)).astype(B16)
-        shard, grad_attended = lax.optimization_barrier((shard, grad_attended))
-        weight_grads = lax.all_gather(shard, "dp", axis=0)
-    else:
-        weight_grads = lax.psum(prior, "dp").reshape(4, 3 * units, depth // 4)
     grad_q, grad_kv = attend_back(
         lengths[:, 0], qkv, all_kv, grad_attended, jnp.concatenate(logs, axis=0), cosine, sine, rows, 3
     )
@@ -1405,7 +1414,12 @@
     ).reshape(-1)
     columns = jnp.stack([gain_one_grad, grad_bias[:QW], sum(gain_two_grads), tails], axis=1)
     columns = jnp.pad(columns.astype(B16), ((0, 0), (0, EXTRA - 4)))
-    summed = scatter_weights([acc_out, acc_q, jnp.concatenate([acc_kv, columns], axis=1)], 2)
+    acc_rest = jnp.concatenate([acc_kv, columns], axis=1)
+    out_part, weight_grads, acc_out, acc_q, acc_rest = lax.optimization_barrier(
+        (done["out"], weight_grads, acc_out, acc_q, acc_rest)
+    )
+    out_sums.append(lax.psum_scatter(out_part, "tensor", scatter_dimension=0, tiled=True))
+    summed = scatter_weights([acc_out, acc_q, acc_rest], 2)
     out_sums, weight_grads, summed = lax.optimization_barrier((out_sums, weight_grads, summed))
     gate_total, up_total, down_total = widen(weight_grads, units)
     grad_out, grad_query, grad_rest = summed

time: 683 us -> 664 us (0.972)
  waiting for transfers between devices: 59.8 us -> 51.5 us
    pallas_call x2, Pallas kernels: 205 us -> 232 us  [mlp(): pl.pallas_call(functools.partial(mlp_kernel, names, reduced), in_specs=[a...]
    ppermute x2 -> x0, waiting for transfers between devices: 19.8 us -> none  [swap(): return lax.ppermute(value, axis, [(i, i ^ bit) for i in range(count)])]
    pallas_call x1, Pallas kernels: 90.4 us -> 75.4 us  [scatter_weights(): pl.pallas_call(functools.partial(scatter_kernel, parts, len(grads)), in_s...]
    pallas_call x1, Pallas kernels: 60.1 us -> 50.5 us  [attend_back(): pl.pallas_call(functools.partial(attend_back_kernel, [*inputs, *outputs,...]
    all_gather x1, waiting for transfers between devices: 0.01 us -> 7.6 us  [on_device(): weight_grads = lax.all_gather(shard, 'dp', axis=0)]
    pallas_call x2, Pallas kernels: 29 us -> 21.5 us  [attend(): pl.pallas_call(attend_kernel, grid_spec=pltpu.PrefetchScalarGridSpec(num_...]
  transfers between devices with their start and end apart: 9 -> 7, of which waited for: 4 -> 3; matrix products, arithmetic and copies ran while one was open for 10% -> 10% of each run, Pallas kernels for 67% -> 69%
where the time goes in v4:
time: 664 us; the launch traced here: 653 us
  Pallas kernels  498 us (75%)
  waiting for transfers between devices  51.5 us (8%)
  other arithmetic  33.1 us (5%)
  local copies, waits for them, and re-layouts  28.1 us (4%)
  matrix products  27.4 us (4%)
  between operations  14.9 us (2%)
    pallas_call x2, Pallas kernels, mlp(): pl.pallas_call(functools.partial(mlp_kernel, names, reduced), in_specs=[a...  232 us
    pallas_call x1, Pallas kernels, scatter_weights(): pl.pallas_call(functools.partial(scatter_kernel, parts, len(grads)), in_s...  75.4 us
    pallas_call x2, Pallas kernels, gather_plane(): pl.pallas_call(functools.partial(plane_kernel, more is not None), in_spec...  70.4 us
    pallas_call x1, Pallas kernels, attend_back(): pl.pallas_call(functools.partial(attend_back_kernel, [*inputs, *outputs,...  50.5 us
    all_gather x1, waiting for transfers between devices, on_device(): whole = lax.all_gather(low, 'tensor', axis=0, tiled=True)  34 us
    pallas_call x1, Pallas kernels, gather_line(): pl.pallas_call(line_kernel, in_specs=[pl.BlockSpec(memory_space=pl.ANY)],...  28.4 us
    pallas_call x2, Pallas kernels, attend(): pl.pallas_call(attend_kernel, grid_spec=pltpu.PrefetchScalarGridSpec(num_...  21.5 us
  transfers between devices with their start and end apart: 7, of which 3 were waited for; matrix products, arithmetic and copies ran while one was open for 10% of the time, Pallas kernels for 69%

profile of v4, /device:TPU:0, one launch (start us, length us, event | category | flops | bytes accessed | tf_op | source)
XLA Modules:
  0.0 653.5 jit_solution(15656042189827922252)
XLA Ops:
  11.1 28.4 %shard_map.257.line_ref = bf16[4,48,2176]{2,1,0:T(8,128)(2,1)} custom-call(bf16[48,2176]{1,0:T(8,128)(2,1)} %fusion.19.block_ref), custom_call_target="tpu_custom_call" | custom-call | bytes 10444800 | tf_op jit(solution)/shard_map/pallas_call | solution.py:248
  42.4 43.7 %shard_map.258 = (bf16[32,48,2176]{2,1,0:T(8,128)(2,1)}, bf16[4,48,1536]{2,1,0:T(8,128)(2,1)}) custom-call(bf16[4,48,2176]{2,1,0:T(8,128)(2,1)} %shard_map.257.line_ref, bf16[48,1536]{1,0:T(8,128)(2,1)} %refs_0_.1), custom_call_target="tpu_custom_call" | custom-call | bytes 25067520 | tf_op jit(solution)/shard_map/pallas_call | solution.py:270
  93.0 8.9 %shard_map.259.q_ref.refs_1_ = bf16[384,2048]{1,0:T(8,128)(2,1)} custom-call(bf16[384,1536]{1,0:T(8,128)(2,1)} %multiply_convert_fusion.1.hidden_ref, bf16[1536,2176]{1,0:T(8,128)(2,1)} %bitcast.95, f32[1,2048]{1,0:T(1,128)} %bitcast.107, f32[384,128]{1,0:T(8,128)} %bitcast.105, f32[384,128]{1,0:T(8,128)} %bitcast.106), custom_call_target="tpu_custom_call" | custom-call | flops 2415919104 | bytes 9043968 | tf_op jit(solution)/shard_map/pallas_call | solution.py:489
  107.2 26.7 %shard_map.261 = bf16[32,48,1536]{2,1,0:T(8,128)(2,1)} custom-call(bf16[4,48,1536]{2,1,0:T(8,128)(2,1)} %get-tuple-element.64.line_ref), custom_call_target="tpu_custom_call" | custom-call | bytes 17694720 | tf_op jit(solution)/shard_map/pallas_call | solution.py:270
  134.0 9.7 %all-gather.14.cloned.1.call-done = bf16[16,192,512]{2,1,0:T(8,128)(2,1)} async-done(((bf16[2,192,512]{2,1,0:T(8,128)(2,1)}), bf16[16,192,512]{2,1,0:T(8,128)(2,1)}) %all-gather.14.cloned.1.call-update) | async-done | bytes 3145744 | tf_op jit(solution)/shard_map/all_gather | solution.py:1351
  143.7 10.7 %shard_map.260 = (bf16[192,1536]{1,0:T(8,128)(2,1)}, f32[192,1536]{1,0:T(8,128)}) custom-call(s32[2]{0:T(128)} %pad_add_fusion.info_ref, bf16[384,2048]{1,0:T(8,128)(2,1)} %shard_map.259.q_ref.refs_1_, bf16[8,2,192,512]{3,2,1,0:T(8,128)(2,1)} %bitcast.119, bf16[8,2,192,512]{3,2,1,0:T(8,128)(2,1)} %bitcast.120), custom_call_target="tpu_custom_call" | custom-call | flops 3623878656 | bytes 3932160 | tf_op jit(solution)/shard_map/pallas_call | solution.py:540
  154.5 2.6 multiply_reduce_fusion.8
  160.1 10.7 %shard_map.262 = (bf16[192,1536]{1,0:T(8,128)(2,1)}, f32[192,1536]{1,0:T(8,128)}) custom-call(s32[2]{0:T(128)} %pad_add_fusion.1.info_ref, bf16[384,2048]{1,0:T(8,128)(2,1)} %shard_map.259.q_ref.refs_1_, bf16[8,2,192,512]{3,2,1,0:T(8,128)(2,1)} %bitcast.121, bf16[8,2,192,512]{3,2,1,0:T(8,128)(2,1)} %bitcast.122), custom_call_target="tpu_custom_call" | custom-call | flops 3623878656 | bytes 3932160 | tf_op jit(solution)/shard_map/pallas_call | solution.py:540
  170.8 2.7 multiply_reduce_fusion.7
  175.5 34.0 %all-gather.10.cloned.1.call-done.refs_1_ = bf16[1536,1536]{1,0:T(8,128)(2,1)} async-done(((bf16[192,1536]{1,0:T(8,128)(2,1)}), bf16[1536,1536]{1,0:T(8,128)(2,1)}) %all-gather.10.cloned.1.call-update) | async-done | bytes 4718608 | tf_op jit(solution)/shard_map/all_gather | solution.py:1368
  209.5 105.8 %shard_map.263 = (bf16[1536,1536]{1,0:T(8,128)(2,1)}, f32[192,1536]{1,0:T(8,128)}, bf16[2,2,3360,384]{3,2,1,0:T(8,128)(2,1)}, bf16[1536,1536]{1,0:T(8,128)(2,1)}) custom-call(bf16[1536,1536]{1,0:T(8,128)(2,1)} %all-gather.8.cloned.1.call-done.refs_0_, bf16[1536,1536]{1,0:T(8,128)(2,1)} %all-gather.10.cloned.1.call-done.refs_1_, ...), custom_call_target="tpu_custom_call" | custom-call | flops 47563407360 | bytes 94371840 | tf_op jit(solution)/shard_map/pallas_call | solution.py:1235
  315.5 125.9 %shard_map.264 = (bf16[1536,1536]{1,0:T(8,128)(2,1)}, f32[192,1536]{1,0:T(8,128)}, bf16[2,2,3360,384]{3,2,1,0:T(8,128)(2,1)}, bf16[3360,384]{1,0:T(8,128)(2,1)}, bf16[2,3360,384]{2,1,0:T(8,128)(2,1)}) custom-call(bf16[1536,1536]{1,0:T(8,128)(2,1)} %all-gather.12.cloned.1.call-done.refs_0_, bf16[1536,1536]{1,0:T(8,128)(2,1)} %get-tuple-element.72.refs_1_, ...), custom_call_target="tpu_custom_call" | custom-call | flops 47563407360 | bytes 94371840 | tf_op jit(solution)/shard_map/pallas_call | solution.py:1235
  441.5 2.2 multiply_convert_fusion
  450.6 3.0 convolution_convert_fusion.3.refs_4_
  453.7 50.5 %shard_map.265 = (bf16[384,1536]{1,0:T(8,128)(2,1)}, bf16[2,192,512]{2,1,0:T(8,128)(2,1)}) custom-call(s32[2]{0:T(128)} %bitcast.108, bf16[384,2048]{1,0:T(8,128)(2,1)} %shard_map.259.q_ref.refs_1_, bf16[8,2,192,512]{3,2,1,0:T(8,128)(2,1)} %bitcast.123, bf16[8,2,192,512]{3,2,1,0:T(8,128)(2,1)} %bitcast.124, ...), custom_call_target="tpu_custom_call" | custom-call | flops 18119393280 | bytes 13369344 | tf_op jit(solution)/shard_map/pallas_call | solution.py:732
  513.3 4.8 fusion
  518.1 4.5 multiply_reduce_fusion
  522.8 4.3 convolution_convert_fusion.1
  530.5 4.4 convolution_convert_fusion
  534.9 7.6 %all-gather.16.cloned.1.call-done = bf16[13440,384]{1,0:T(8,128)(2,1)} async-done(((bf16[3360,384]{1,0:T(8,128)(2,1)}), bf16[13440,384]{1,0:T(8,128)(2,1)}) %all-gather.16.cloned.1.call-update) | async-done | bytes 10321936 | tf_op jit(solution)/shard_map/all_gather | solution.py:1383
  543.2 4.0 multiply_add_fusion
  547.2 4.0 copy.47
  551.2 75.4 %shard_map.266 = (f32[48,1536]{1,0:T(8,128)}, f32[48,1536]{1,0:T(8,128)}, f32[48,640]{1,0:T(8,128)}) custom-call(bf16[16,2,48,1536]{3,2,1,0:T(8,128)(2,1)} %bitcast.99, bf16[16,2,48,1536]{3,2,1,0:T(8,128)(2,1)} %bitcast.100, bf16[16,2,48,640]{3,2,1,0:T(8,128)(2,1)} %bitcast.93), custom_call_target="tpu_custom_call" | custom-call | bytes 45613056 | tf_op jit(solution)/shard_map/pallas_call | solution.py:446
  632.5 11.4 %shard_map.267 = (f32[1120,1536]{1,0:T(8,128)}, f32[1120,1536]{1,0:T(8,128)}, f32[1120,1536]{1,0:T(8,128)}) custom-call(bf16[4,3360,384]{2,1,0:T(8,128)(2,1)} %bitcast.83, bf16[4,3360,384]{2,1,0:T(8,128)(2,1)} %bitcast.84, bf16[4,3360,384]{2,1,0:T(8,128)(2,1)} %bitcast.85), custom_call_target="tpu_custom_call" | custom-call | bytes 30965760 | tf_op jit(solution)/shard_map/pallas_call | solution.py:1262
  (169 shorter events, 52.4 us)
Async XLA Ops:
  7.2 32.3 %copy-start.37 = (s32[2,1]{0,1:T(1,128)S(1)}, s32[2,1]{0,1:T(1,128)}, u32[]{:S(2)}) copy-start(s32[2,1]{0,1:T(1,128)} %param.16) | copy-start | bytes 28
  7.2 32.4 %copy-start.14 = (bf16[2,1,192,1536]{3,2,1,0:T(8,128)(2,1)S(1)}, bf16[2,1,192,1536]{3,2,1,0:T(8,128)(2,1)}, u32[]{:S(2)}) copy-start(bf16[2,1,192,1536]{3,2,1,0:T(8,128)(2,1)} %param.29) | copy-start | bytes 3538948
  7.2 96.4 %all-gather.8.cloned.1.call-start = ((), (), s32[]{:S(2)}) async-start(), calls=%async_computation.2 | async-start | bytes 5308416 | tf_op jit(solution)/shard_map/all_gather | solution.py:1330
  41.6 102.1 %all-gather.14.cloned.1.call-start = ((), (), s32[]{:S(2)}) async-start(), calls=%async_computation.7 | async-start | bytes 3538944 | tf_op jit(solution)/shard_map/all_gather | solution.py:1351
  42.3 46.3 %copy-start.32 = (f32[2,192]{1,0:T(2,128)}, f32[2,192]{1,0:T(2,128)S(1)}, u32[]{:S(2)}) copy-start(f32[2,192]{1,0:T(2,128)S(1)} %add_rsqrt_fusion) | copy-start | bytes 4612
  42.4 47.8 %copy-start.29 = (f32[384]{0:T(512)}, f32[384]{0:T(512)S(1)}, u32[]{:S(2)}) copy-start(f32[384]{0:T(512)S(1)} %rsqrt.29) | copy-start | bytes 4612
  103.7 105.8 %all-gather.10.cloned.1.call-start = ((), (), s32[]{:S(2)}) async-start(), calls=%async_computation.3 | async-start | bytes 5308416 | tf_op jit(solution)/shard_map/all_gather | solution.py:1368
  143.7 10.7 %copy-start = (bf16[32,48,1536]{2,1,0:T(8,128)(2,1)S(1)}, bf16[32,48,1536]{2,1,0:T(8,128)(2,1)}, u32[]{:S(2)}) copy-start(bf16[32,48,1536]{2,1,0:T(8,128)(2,1)} %shard_map.261) | copy-start | bytes 14155780
  158.7 12.1 %slice-start = ((s8[4718592]{0:T(1024)(128)(4,1)}), s8[524288]{0:T(1024)(128)(4,1)S(1)}, s32[]{:S(2)}) async-start(s8[4718592]{0:T(1024)(128)(4,1)} %bitcast.87), calls=%async_computation.9 | async-start | bytes 1048576
  158.7 156.7 %all-gather.12.cloned.1.call-start = ((), (), s32[]{:S(2)}) async-start(), calls=%async_computation.4 | async-start | bytes 5308416 | tf_op jit(solution)/shard_map/all_gather | solution.py:1373
  160.0 10.7 %slice-start.1 = ((s8[4718592]{0:T(1024)(128)(4,1)}), s8[4194304]{0:T(1024)(128)(4,1)S(1)}, s32[]{:S(2)}) async-start(s8[4718592]{0:T(1024)(128)(4,1)} %bitcast.87), calls=%async_computation.10 | async-start | bytes 8388608
  209.5 231.9 %reduce-scatter.3.cloned.1.call-start = ((), (), s32[]{:S(2)}) async-start(), calls=%async_computation.5 | async-start | bytes 5308416 | tf_op jit(solution)/shard_map/reduce_scatter | solution.py:1380
  315.4 227.1 %all-gather.16.cloned.1.call-start = ((), (), s32[]{:S(2)}) async-start(), calls=%async_computation.8 | async-start | bytes 12902400 | tf_op jit(solution)/shard_map/all_gather | solution.py:1383
  441.4 185.2 %reduce-scatter.5.cloned.1.call-start = ((), (), s32[]{:S(2)}) async-start(), calls=%async_computation.6 | async-start | bytes 5308416 | tf_op jit(solution)/shard_map/reduce_scatter | solution.py:1421
  453.7 52.2 %copy-start.25 = (f32[1536]{0:T(1024)S(1)}, f32[1536]{0:T(1024)}, u32[]{:S(2)}) copy-start(f32[1536]{0:T(1024)} %get-tuple-element.148) | copy-start | bytes 18436
  513.3 4.8 copy-start.13
  513.3 4.8 copy-start.30
  518.1 4.6 copy-start.26
  518.1 4.6 copy-start.27
  518.1 4.6 copy-start.28
  518.1 4.6 copy-start.8
  518.1 4.6 copy-start.18
  518.1 4.6 copy-start.19
  551.2 79.9 %copy-start.4 = (f32[192,1536]{1,0:T(8,128)S(1)}, f32[192,1536]{1,0:T(8,128)}, u32[]{:S(2)}) copy-start(f32[192,1536]{1,0:T(8,128)} %copy-done.2) | copy-start | bytes 3538948
  (26 other events, 54.0 us)
Sparse Core Ops, SparseCore 0:
  41.7 54.9 all-gather.7
  103.8 39.8 all-gather.13
  158.8 50.5 all-gather.9
  210.9 70.9 all-gather.11
  315.5 63.3 reduce-scatter.2
  441.6 100.9 all-gather.15
  544.8 75.4 reduce-scatter.4

commit v5 on v4

--- a/solution.py
+++ b/solution.py
@@ -862,6 +862,24 @@
             spot.right if ahead else spot.left,
         )
 
+    def straight(block):
+        return remote(
+            r.part.at[rows_of(block, core)],
+            r.zrecv.at[chip],
+            r.zsend.at[block],
+            r.zrecv_sem.at[chip],
+            spot.on_line(block),
+        )
+
+    def straight_sum():
+        for other in range(chips):
+
+            @pl.when(chip != other)
+            def _():
+                here = r.zrecv.at[other]
+                remote(here, here, r.zsend.at[other], r.zrecv_sem.at[other], spot.beside).wait_recv()
+                r.grad[...] = r.grad[...] + r.zrecv[other].astype(F32)
+
     def finish(block):
         swapped(block).wait_recv()
         total = r.part[rows_of(block, core), :].astype(F32) + r.xrecv[block].astype(F32)
@@ -873,8 +891,11 @@
         @pl.when(block != chip)
         def _():
             r.part[rows_of(block, core), :] = total.astype(B16)
-            pl.when(chip == 0)(along(block, True).start)
-            pl.when(chip == chips - 1)(along(block, False).start)
+            if has_next:
+                pl.when(chip == 0)(along(block, True).start)
+                pl.when(chip == chips - 1)(along(block, False).start)
+            else:
+                straight(block).start()
 
     def relay_one(block, ahead):
         slot = chips - 1 - block if ahead else chips - block
@@ -905,29 +926,29 @@
         def _():
             relay_one(back_step, False)
 
+    def gate(here, start, width):
+        cut = pl.ds(start, width)
+        gate = dot_t(r.h[here, :], r.wg[cut, :])
+        up = dot_t(r.h[here, :], r.wu[cut, :])
+        grad = dot_t(r.g[here, :], r.wd[cut, :])
+        sigma = jax.nn.sigmoid(gate)
+        silu = gate * sigma
+        r.act[here, cut] = (silu * up).astype(B16)
+        r.dg[here, cut] = (grad * up * sigma * (1.0 + gate * (1.0 - sigma))).astype(B16)
+        r.du[here, cut] = (grad * silu).astype(B16)
+
     def gates(step, block):
         here = span(block)
 
-        def one(start, width):
-            cut = pl.ds(start, width)
-            gate = dot_t(r.h[here, :], r.wg[cut, :])
-            up = dot_t(r.h[here, :], r.wu[cut, :])
-            grad = dot_t(r.g[here, :], r.wd[cut, :])
-            sigma = jax.nn.sigmoid(gate)
-            silu = gate * sigma
-            r.act[here, cut] = (silu * up).astype(B16)
-            r.dg[here, cut] = (grad * up * sigma * (1.0 + gate * (1.0 - sigma))).astype(B16)
-            r.du[here, cut] = (grad * silu).astype(B16)
-
         def chunk(index, _):
             pl.when(step == 0)(functools.partial(weights_here, index))
-            one(pl.multiple_of(index * CHUNK, CHUNK), CHUNK)
+            gate(here, pl.multiple_of(index * CHUNK, CHUNK), CHUNK)
             return 0
 
         lax.fori_loop(0, whole_chunks, chunk, 0)
         if rest:
             pl.when(step == 0)(functools.partial(weights_here, whole_chunks, rest))
-            one(whole_chunks * CHUNK, rest)
+            gate(here, whole_chunks * CHUNK, rest)
 
     def back(block):
         here = span(block)
@@ -1063,7 +1084,7 @@
             for index in range(len(chunks)):
                 for copy in weight_load(index):
                     copy.start()
-    greet(spot, reduced, "near")
+    greet(spot, reduced, "near" if has_next else "all")
     if has_next:
         gather_start()
 
@@ -1071,12 +1092,13 @@
         h_load(block).wait()
         g_load(block).wait()
 
-    todo = [(matrix, index) for matrix in (2, 0, 1) for index in range(len(chunks))] if reduced else []
-    share = pl.cdiv(len(todo), chips + 2)
+    todo = []
+    if reduced:
+        todo = [(matrix, index) for matrix in (2, 0, 1) for index in range(len(chunks))]
     loading = []
 
-    def some():
-        for _ in range(share):
+    def some(count=2):
+        for _ in range(count):
             if loading:
                 exchange(*loading.pop(0))
             if todo:
@@ -1129,20 +1151,21 @@
 
         lax.fori_loop(0, chips, unit, 0)
         weight_grads(2, r.act, r.g)
+        weight_grads(0, r.dg, r.h)
+        some(1)
         lax.fori_loop(0, chips, unit_back, 0)
         finish(block_at(chips - 1))
-        weight_grads(0, r.dg, r.h)
-        some()
-        relay(0)
         weight_grads(1, r.du, r.h)
-        some()
-        for point in range(1, chips - 2):
-            relay(point)
+        some(5)
+        some(3)
     for block in range(chips):
         out_block(jnp.int32(block))
-        some()
-    relay(chips - 2)
-    some()
+        some(2)
+    if has_next:
+        relay(chips - 2)
+    some(len(todo) + 1)
+    if not has_next:
+        straight_sum()
     for index in range(2):
         put_out(0, index).wait()
     if reduced:
@@ -1157,8 +1180,11 @@
                 exchanged(matrix, index, start, width, (matrix + index) % 2 == 0).wait_send()
     for block in range(chips):
         swapped(block).wait_send()
-        pl.when(chip < block)(along(block, True).wait_send)
-        pl.when(chip > block)(along(block, False).wait_send)
+        if has_next:
+            pl.when(chip < block)(along(block, True).wait_send)
+            pl.when(chip > block)(along(block, False).wait_send)
+        else:
+            pl.when(chip != block)(straight(block).wait_send)
     if has_next:
         gather_end()
 
@@ -1414,15 +1440,14 @@
     ).reshape(-1)
     columns = jnp.stack([gain_one_grad, grad_bias[:QW], sum(gain_two_grads), tails], axis=1)
     columns = jnp.pad(columns.astype(B16), ((0, 0), (0, EXTRA - 4)))
-    acc_rest = jnp.concatenate([acc_kv, columns], axis=1)
-    out_part, weight_grads, acc_out, acc_q, acc_rest = lax.optimization_barrier(
-        (done["out"], weight_grads, acc_out, acc_q, acc_rest)
+    out_part, weight_grads, acc_out, acc_q, acc_kv, columns = lax.optimization_barrier(
+        (done["out"], weight_grads, acc_out, acc_q, acc_kv, columns)
     )
     out_sums.append(lax.psum_scatter(out_part, "tensor", scatter_dimension=0, tiled=True))
-    summed = scatter_weights([acc_out, acc_q, acc_rest], 2)
+    summed = scatter_weights([acc_out, acc_q, acc_kv, columns], 2)
     out_sums, weight_grads, summed = lax.optimization_barrier((out_sums, weight_grads, summed))
     gate_total, up_total, down_total = widen(weight_grads, units)
-    grad_out, grad_query, grad_rest = summed
+    grad_out, grad_query, grad_kv, grad_rest = summed
     layer_output = jnp.stack(
         [(mixed[m] + out_sums[m].astype(F32)).astype(B16) for m in range(micros)]
     )[:, None]
@@ -1430,15 +1455,15 @@
     return (
         layer_output,
         grad_input,
-        grad_rest[:, 2 * KW],
+        grad_rest[:, 0],
         grad_query,
-        grad_rest[:, 2 * KW + 1],
-        grad_rest[:, :KW],
-        grad_rest[:small, 2 * KW + 3],
-        grad_rest[:, KW : 2 * KW],
-        grad_rest[small : 2 * small, 2 * KW + 3],
+        grad_rest[:, 1],
+        grad_kv[:, :KW],
+        grad_rest[:small, 3],
+        grad_kv[:, KW:],
+        grad_rest[small : 2 * small, 3],
         grad_out,
-        grad_rest[:, 2 * KW + 2],
+        grad_rest[:, 2],
         gate_total.T,
         up_total.T,
         down_total,

time: 664 us -> 656 us (0.988)
  Pallas kernels: 498 us -> 491 us
    pallas_call x2, Pallas kernels: 232 us -> 224 us  [mlp(): pl.pallas_call(functools.partial(mlp_kernel, names, reduced), in_specs=[a...]
  transfers between devices with their start and end apart: 7 -> 7, of which waited for: 3 -> 3; matrix products, arithmetic and copies ran while one was open for 10% -> 10% of each run, Pallas kernels for 69% -> 68%
where the time goes in v5:
time: 656 us; the launch traced here: 646 us
  Pallas kernels  491 us (75%)
  waiting for transfers between devices  53.7 us (8%)
  other arithmetic  32.4 us (5%)
  matrix products  28.6 us (4%)
  local copies, waits for them, and re-layouts  25.1 us (4%)
  between operations  15.1 us (2%)
    pallas_call x2, Pallas kernels, mlp(): pl.pallas_call(functools.partial(mlp_kernel, names, reduced), in_specs=[a...  224 us
    pallas_call x1, Pallas kernels, scatter_weights(): pl.pallas_call(functools.partial(scatter_kernel, parts, len(grads)), in_s...  78.4 us
    pallas_call x2, Pallas kernels, gather_plane(): pl.pallas_call(functools.partial(plane_kernel, more is not None), in_spec...  70.4 us
    pallas_call x1, Pallas kernels, attend_back(): pl.pallas_call(functools.partial(attend_back_kernel, [*inputs, *outputs,...  48.8 us
    all_gather x1, waiting for transfers between devices, on_device(): whole = lax.all_gather(low, 'tensor', axis=0, tiled=True)  34 us
    pallas_call x1, Pallas kernels, gather_line(): pl.pallas_call(line_kernel, in_specs=[pl.BlockSpec(memory_space=pl.ANY)],...  28.4 us
    pallas_call x2, Pallas kernels, attend(): pl.pallas_call(attend_kernel, grid_spec=pltpu.PrefetchScalarGridSpec(num_...  21.5 us
  transfers between devices with their start and end apart: 7, of which 3 were waited for; matrix products, arithmetic and copies ran while one was open for 10% of the time, Pallas kernels for 68%

profile of v5, /device:TPU:0, one launch (start us, length us, event | category | flops | bytes accessed | tf_op | source)
XLA Modules:
  0.0 646.4 jit_solution(1406853727714765326)
XLA Ops:
  11.1 28.4 %shard_map.257.line_ref = bf16[4,48,2176]{2,1,0:T(8,128)(2,1)} custom-call(bf16[48,2176]{1,0:T(8,128)(2,1)} %fusion.19.block_ref), custom_call_target="tpu_custom_call" | custom-call | bytes 10444800 | tf_op jit(solution)/shard_map/pallas_call | solution.py:248
  42.4 43.7 %shard_map.258 = (bf16[32,48,2176]{2,1,0:T(8,128)(2,1)}, bf16[4,48,1536]{2,1,0:T(8,128)(2,1)}) custom-call(bf16[4,48,2176]{2,1,0:T(8,128)(2,1)} %shard_map.257.line_ref, bf16[48,1536]{1,0:T(8,128)(2,1)} %refs_0_.1), custom_call_target="tpu_custom_call" | custom-call | bytes 25067520 | tf_op jit(solution)/shard_map/pallas_call | solution.py:270
  93.0 8.9 %shard_map.259.q_ref.refs_1_ = bf16[384,2048]{1,0:T(8,128)(2,1)} custom-call(bf16[384,1536]{1,0:T(8,128)(2,1)} %multiply_convert_fusion.1.hidden_ref, bf16[1536,2176]{1,0:T(8,128)(2,1)} %bitcast.95, f32[1,2048]{1,0:T(1,128)} %bitcast.109, f32[384,128]{1,0:T(8,128)} %bitcast.105, f32[384,128]{1,0:T(8,128)} %bitcast.106), custom_call_target="tpu_custom_call" | custom-call | flops 2415919104 | bytes 9043968 | tf_op jit(solution)/shard_map/pallas_call | solution.py:489
  107.2 26.7 %shard_map.261 = bf16[32,48,1536]{2,1,0:T(8,128)(2,1)} custom-call(bf16[4,48,1536]{2,1,0:T(8,128)(2,1)} %get-tuple-element.67.line_ref), custom_call_target="tpu_custom_call" | custom-call | bytes 17694720 | tf_op jit(solution)/shard_map/pallas_call | solution.py:270
  134.0 9.7 %all-gather.14.cloned.1.call-done = bf16[16,192,512]{2,1,0:T(8,128)(2,1)} async-done(((bf16[2,192,512]{2,1,0:T(8,128)(2,1)}), bf16[16,192,512]{2,1,0:T(8,128)(2,1)}) %all-gather.14.cloned.1.call-update) | async-done | bytes 3145744 | tf_op jit(solution)/shard_map/all_gather | solution.py:1377
  143.7 10.8 %shard_map.260 = (bf16[192,1536]{1,0:T(8,128)(2,1)}, f32[192,1536]{1,0:T(8,128)}) custom-call(s32[2]{0:T(128)} %pad_add_fusion.info_ref, bf16[384,2048]{1,0:T(8,128)(2,1)} %shard_map.259.q_ref.refs_1_, bf16[8,2,192,512]{3,2,1,0:T(8,128)(2,1)} %bitcast.121, bf16[8,2,192,512]{3,2,1,0:T(8,128)(2,1)} %bitcast.122), custom_call_target="tpu_custom_call" | custom-call | flops 3623878656 | bytes 3932160 | tf_op jit(solution)/shard_map/pallas_call | solution.py:540
  154.5 2.6 multiply_reduce_fusion.8
  160.1 10.7 %shard_map.262 = (bf16[192,1536]{1,0:T(8,128)(2,1)}, f32[192,1536]{1,0:T(8,128)}) custom-call(s32[2]{0:T(128)} %pad_add_fusion.1.info_ref, bf16[384,2048]{1,0:T(8,128)(2,1)} %shard_map.259.q_ref.refs_1_, bf16[8,2,192,512]{3,2,1,0:T(8,128)(2,1)} %bitcast.123, bf16[8,2,192,512]{3,2,1,0:T(8,128)(2,1)} %bitcast.124), custom_call_target="tpu_custom_call" | custom-call | flops 3623878656 | bytes 3932160 | tf_op jit(solution)/shard_map/pallas_call | solution.py:540
  170.8 2.7 multiply_reduce_fusion.7
  175.5 34.0 %all-gather.10.cloned.1.call-done.refs_1_ = bf16[1536,1536]{1,0:T(8,128)(2,1)} async-done(((bf16[192,1536]{1,0:T(8,128)(2,1)}), bf16[1536,1536]{1,0:T(8,128)(2,1)}) %all-gather.10.cloned.1.call-update) | async-done | bytes 4718608 | tf_op jit(solution)/shard_map/all_gather | solution.py:1394
  209.5 105.6 %shard_map.263 = (bf16[1536,1536]{1,0:T(8,128)(2,1)}, f32[192,1536]{1,0:T(8,128)}, bf16[2,2,3360,384]{3,2,1,0:T(8,128)(2,1)}, bf16[1536,1536]{1,0:T(8,128)(2,1)}) custom-call(bf16[1536,1536]{1,0:T(8,128)(2,1)} %all-gather.8.cloned.1.call-done.refs_0_, bf16[1536,1536]{1,0:T(8,128)(2,1)} %all-gather.10.cloned.1.call-done.refs_1_, ...), custom_call_target="tpu_custom_call" | custom-call | flops 47563407360 | bytes 94371840 | tf_op jit(solution)/shard_map/pallas_call | solution.py:1261
  315.2 118.0 %shard_map.264 = (bf16[1536,1536]{1,0:T(8,128)(2,1)}, f32[192,1536]{1,0:T(8,128)}, bf16[2,2,3360,384]{3,2,1,0:T(8,128)(2,1)}, bf16[3360,384]{1,0:T(8,128)(2,1)}, bf16[2,3360,384]{2,1,0:T(8,128)(2,1)}) custom-call(bf16[1536,1536]{1,0:T(8,128)(2,1)} %all-gather.12.cloned.1.call-done.refs_0_, bf16[1536,1536]{1,0:T(8,128)(2,1)} %get-tuple-element.75.refs_1_, ...), custom_call_target="tpu_custom_call" | custom-call | flops 47563407360 | bytes 94371840 | tf_op jit(solution)/shard_map/pallas_call | solution.py:1261
  433.3 2.2 multiply_convert_fusion
  442.4 3.0 convolution_convert_fusion.3.refs_4_
  445.5 48.8 %shard_map.265 = (bf16[384,1536]{1,0:T(8,128)(2,1)}, bf16[2,192,512]{2,1,0:T(8,128)(2,1)}) custom-call(s32[2]{0:T(128)} %bitcast.110, bf16[384,2048]{1,0:T(8,128)(2,1)} %shard_map.259.q_ref.refs_1_, bf16[8,2,192,512]{3,2,1,0:T(8,128)(2,1)} %bitcast.125, bf16[8,2,192,512]{3,2,1,0:T(8,128)(2,1)} %bitcast.126, ...), custom_call_target="tpu_custom_call" | custom-call | flops 18119393280 | bytes 13369344 | tf_op jit(solution)/shard_map/pallas_call | solution.py:732
  503.4 4.8 fusion
  508.2 4.5 multiply_reduce_fusion
  513.6 4.3 convolution_convert_fusion.1
  517.9 2.2 convolution_convert_fusion.2
  520.1 4.5 convolution_convert_fusion
  524.6 9.8 %all-gather.16.cloned.1.call-done = bf16[13440,384]{1,0:T(8,128)(2,1)} async-done(((bf16[3360,384]{1,0:T(8,128)(2,1)}), bf16[13440,384]{1,0:T(8,128)(2,1)}) %all-gather.16.cloned.1.call-update) | async-done | bytes 10321936 | tf_op jit(solution)/shard_map/all_gather | solution.py:1409
  535.1 4.0 multiply_add_fusion
  541.0 78.4 %shard_map.266 = (f32[48,1536]{1,0:T(8,128)}, f32[48,1536]{1,0:T(8,128)}, f32[48,512]{1,0:T(8,128)}, f32[48,128]{1,0:T(8,128)}) custom-call(bf16[16,2,48,1536]{3,2,1,0:T(8,128)(2,1)} %bitcast.98, bf16[16,2,48,1536]{3,2,1,0:T(8,128)(2,1)} %bitcast.99, bf16[16,2,48,512]{3,2,1,0:T(8,128)(2,1)} %bitcast.103, bf16[16,2,48,128]{3,2,1,0:T(8,128)(2,1)} %bitcast.101), custom_call_target="tpu_custom_call" | custom-call | bytes 45613056 | tf_op jit(solution)/shard_map/pallas_call | solution.py:446
  625.2 11.4 %shard_map.267 = (f32[1120,1536]{1,0:T(8,128)}, f32[1120,1536]{1,0:T(8,128)}, f32[1120,1536]{1,0:T(8,128)}) custom-call(bf16[4,3360,384]{2,1,0:T(8,128)(2,1)} %bitcast.84, bf16[4,3360,384]{2,1,0:T(8,128)(2,1)} %bitcast.85, bf16[4,3360,384]{2,1,0:T(8,128)(2,1)} %bitcast.86), custom_call_target="tpu_custom_call" | custom-call | bytes 30965760 | tf_op jit(solution)/shard_map/pallas_call | solution.py:1288
  (170 shorter events, 51.7 us)
Async XLA Ops:
  7.2 32.3 %copy-start.38 = (s32[2,1]{0,1:T(1,128)S(1)}, s32[2,1]{0,1:T(1,128)}, u32[]{:S(2)}) copy-start(s32[2,1]{0,1:T(1,128)} %param.16) | copy-start | bytes 28
  7.2 32.4 %copy-start.12 = (bf16[2,1,192,1536]{3,2,1,0:T(8,128)(2,1)S(1)}, bf16[2,1,192,1536]{3,2,1,0:T(8,128)(2,1)}, u32[]{:S(2)}) copy-start(bf16[2,1,192,1536]{3,2,1,0:T(8,128)(2,1)} %param.29) | copy-start | bytes 3538948
  7.2 96.4 %all-gather.8.cloned.1.call-start = ((), (), s32[]{:S(2)}) async-start(), calls=%async_computation.2 | async-start | bytes 5308416 | tf_op jit(solution)/shard_map/all_gather | solution.py:1356
  41.6 102.1 %all-gather.14.cloned.1.call-start = ((), (), s32[]{:S(2)}) async-start(), calls=%async_computation.7 | async-start | bytes 3538944 | tf_op jit(solution)/shard_map/all_gather | solution.py:1377
  42.3 46.3 %copy-start.33 = (f32[2,192]{1,0:T(2,128)}, f32[2,192]{1,0:T(2,128)S(1)}, u32[]{:S(2)}) copy-start(f32[2,192]{1,0:T(2,128)S(1)} %add_rsqrt_fusion) | copy-start | bytes 4612
  42.4 47.8 %copy-start.30 = (f32[384]{0:T(512)}, f32[384]{0:T(512)S(1)}, u32[]{:S(2)}) copy-start(f32[384]{0:T(512)S(1)} %rsqrt.29) | copy-start | bytes 4612
  103.7 105.8 %all-gather.10.cloned.1.call-start = ((), (), s32[]{:S(2)}) async-start(), calls=%async_computation.3 | async-start | bytes 5308416 | tf_op jit(solution)/shard_map/all_gather | solution.py:1394
  143.7 10.8 %copy-start = (bf16[32,48,1536]{2,1,0:T(8,128)(2,1)S(1)}, bf16[32,48,1536]{2,1,0:T(8,128)(2,1)}, u32[]{:S(2)}) copy-start(bf16[32,48,1536]{2,1,0:T(8,128)(2,1)} %shard_map.261) | copy-start | bytes 14155780
  158.7 12.1 %slice-start = ((s8[4718592]{0:T(1024)(128)(4,1)}), s8[524288]{0:T(1024)(128)(4,1)S(1)}, s32[]{:S(2)}) async-start(s8[4718592]{0:T(1024)(128)(4,1)} %bitcast.88), calls=%async_computation.9 | async-start | bytes 1048576
  158.7 156.5 %all-gather.12.cloned.1.call-start = ((), (), s32[]{:S(2)}) async-start(), calls=%async_computation.4 | async-start | bytes 5308416 | tf_op jit(solution)/shard_map/all_gather | solution.py:1399
  160.1 10.7 %slice-start.1 = ((s8[4718592]{0:T(1024)(128)(4,1)}), s8[4194304]{0:T(1024)(128)(4,1)S(1)}, s32[]{:S(2)}) async-start(s8[4718592]{0:T(1024)(128)(4,1)} %bitcast.88), calls=%async_computation.10 | async-start | bytes 8388608
  209.5 223.7 %reduce-scatter.3.cloned.1.call-start = ((), (), s32[]{:S(2)}) async-start(), calls=%async_computation.5 | async-start | bytes 5308416 | tf_op jit(solution)/shard_map/reduce_scatter | solution.py:1406
  315.1 219.3 %all-gather.16.cloned.1.call-start = ((), (), s32[]{:S(2)}) async-start(), calls=%async_computation.8 | async-start | bytes 12902400 | tf_op jit(solution)/shard_map/all_gather | solution.py:1409
  433.3 186.2 %reduce-scatter.5.cloned.1.call-start = ((), (), s32[]{:S(2)}) async-start(), calls=%async_computation.6 | async-start | bytes 5308416 | tf_op jit(solution)/shard_map/reduce_scatter | solution.py:1446
  445.5 50.5 %copy-start.26 = (f32[1536]{0:T(1024)S(1)}, f32[1536]{0:T(1024)}, u32[]{:S(2)}) copy-start(f32[1536]{0:T(1024)} %get-tuple-element.154) | copy-start | bytes 18436
  503.4 4.8 copy-start.20
  503.4 4.8 copy-start.31
  508.2 4.6 copy-start.27
  508.2 4.6 copy-start.28
  508.2 4.6 copy-start.29
  508.2 5.4 copy-start.8
  508.2 5.4 copy-start.17
  508.2 5.4 copy-start.18
  541.0 81.4 %copy-start.4 = (f32[192,1536]{1,0:T(8,128)S(1)}, f32[192,1536]{1,0:T(8,128)}, u32[]{:S(2)}) copy-start(f32[192,1536]{1,0:T(8,128)} %copy-done.2) | copy-start | bytes 3538948
  (27 other events, 55.2 us)
Sparse Core Ops, SparseCore 0:
  41.7 54.9 all-gather.7
  103.8 39.8 all-gather.13
  158.8 50.5 all-gather.9
  210.9 70.6 all-gather.11
  315.2 54.9 reduce-scatter.2
  433.4 100.9 all-gather.15
  536.7 77.0 reduce-scatter.4

commit v6 on v5

--- a/solution.py
+++ b/solution.py
@@ -1440,8 +1440,9 @@
     ).reshape(-1)
     columns = jnp.stack([gain_one_grad, grad_bias[:QW], sum(gain_two_grads), tails], axis=1)
     columns = jnp.pad(columns.astype(B16), ((0, 0), (0, EXTRA - 4)))
-    out_part, weight_grads, acc_out, acc_q, acc_kv, columns = lax.optimization_barrier(
-        (done["out"], weight_grads, acc_out, acc_q, acc_kv, columns)
+    grad_input = (grad_in + jnp.concatenate(grad_mixed, axis=0)).reshape(micros, 1, rows, depth)
+    out_part, weight_grads, acc_out, acc_q, acc_kv, columns, grad_input = lax.optimization_barrier(
+        (done["out"], weight_grads, acc_out, acc_q, acc_kv, columns, grad_input)
     )
     out_sums.append(lax.psum_scatter(out_part, "tensor", scatter_dimension=0, tiled=True))
     summed = scatter_weights([acc_out, acc_q, acc_kv, columns], 2)
@@ -1451,7 +1452,6 @@
     layer_output = jnp.stack(
         [(mixed[m] + out_sums[m].astype(F32)).astype(B16) for m in range(micros)]
     )[:, None]
-    grad_input = (grad_in + jnp.concatenate(grad_mixed, axis=0)).reshape(micros, 1, rows, depth)
     return (
         layer_output,
         grad_input,

time: 656 us -> 656 us (level)
  transfers between devices with their start and end apart: 7 -> 7, of which waited for: 3 -> 3; matrix products, arithmetic and copies ran while one was open for 10% -> 9% of each run, Pallas kernels for 68% -> 69%
where the time goes in v6:
time: 656 us; the launch traced here: 644 us
  Pallas kernels  494 us (75%)
  waiting for transfers between devices  53.5 us (8%)
  other arithmetic  29.7 us (5%)
  matrix products  26.7 us (4%)
  local copies, waits for them, and re-layouts  25.1 us (4%)
  between operations  15.1 us (2%)
    pallas_call x2, Pallas kernels, mlp(): pl.pallas_call(functools.partial(mlp_kernel, names, reduced), in_specs=[a...  224 us
    pallas_call x1, Pallas kernels, scatter_weights(): pl.pallas_call(functools.partial(scatter_kernel, parts, len(grads)), in_s...  80.6 us
    pallas_call x2, Pallas kernels, gather_plane(): pl.pallas_call(functools.partial(plane_kernel, more is not None), in_spec...  70.4 us
    pallas_call x1, Pallas kernels, attend_back(): pl.pallas_call(functools.partial(attend_back_kernel, [*inputs, *outputs,...  48.8 us
    all_gather x1, waiting for transfers between devices, on_device(): whole = lax.all_gather(low, 'tensor', axis=0, tiled=True)  34 us
    pallas_call x1, Pallas kernels, gather_line(): pl.pallas_call(line_kernel, in_specs=[pl.BlockSpec(memory_space=pl.ANY)],...  28.4 us
    pallas_call x2, Pallas kernels, attend(): pl.pallas_call(attend_kernel, grid_spec=pltpu.PrefetchScalarGridSpec(num_...  21.5 us
  transfers between devices with their start and end apart: 7, of which 3 were waited for; matrix products, arithmetic and copies ran while one was open for 9% of the time, Pallas kernels for 69%

profile of v6, /device:TPU:0, one launch (start us, length us, event | category | flops | bytes accessed | tf_op | source)
XLA Modules:
  0.0 643.9 jit_solution(3805875591423790921)
XLA Ops:
  11.1 28.4 %shard_map.257.line_ref = bf16[4,48,2176]{2,1,0:T(8,128)(2,1)} custom-call(bf16[48,2176]{1,0:T(8,128)(2,1)} %fusion.19.block_ref), custom_call_target="tpu_custom_call" | custom-call | bytes 10444800 | tf_op jit(solution)/shard_map/pallas_call | solution.py:248
  42.4 43.7 %shard_map.258 = (bf16[32,48,2176]{2,1,0:T(8,128)(2,1)}, bf16[4,48,1536]{2,1,0:T(8,128)(2,1)}) custom-call(bf16[4,48,2176]{2,1,0:T(8,128)(2,1)} %shard_map.257.line_ref, bf16[48,1536]{1,0:T(8,128)(2,1)} %refs_0_.1), custom_call_target="tpu_custom_call" | custom-call | bytes 25067520 | tf_op jit(solution)/shard_map/pallas_call | solution.py:270
  93.0 8.9 %shard_map.259.q_ref.refs_1_ = bf16[384,2048]{1,0:T(8,128)(2,1)} custom-call(bf16[384,1536]{1,0:T(8,128)(2,1)} %multiply_convert_fusion.1.hidden_ref, bf16[1536,2176]{1,0:T(8,128)(2,1)} %bitcast.94, f32[1,2048]{1,0:T(1,128)} %bitcast.108, f32[384,128]{1,0:T(8,128)} %bitcast.104, f32[384,128]{1,0:T(8,128)} %bitcast.105), custom_call_target="tpu_custom_call" | custom-call | flops 2415919104 | bytes 9043968 | tf_op jit(solution)/shard_map/pallas_call | solution.py:489
  107.2 26.7 %shard_map.261 = bf16[32,48,1536]{2,1,0:T(8,128)(2,1)} custom-call(bf16[4,48,1536]{2,1,0:T(8,128)(2,1)} %get-tuple-element.68.line_ref), custom_call_target="tpu_custom_call" | custom-call | bytes 17694720 | tf_op jit(solution)/shard_map/pallas_call | solution.py:270
  134.0 9.7 %all-gather.14.cloned.1.call-done = bf16[16,192,512]{2,1,0:T(8,128)(2,1)} async-done(((bf16[2,192,512]{2,1,0:T(8,128)(2,1)}), bf16[16,192,512]{2,1,0:T(8,128)(2,1)}) %all-gather.14.cloned.1.call-update) | async-done | bytes 3145744 | tf_op jit(solution)/shard_map/all_gather | solution.py:1377
  143.7 10.8 %shard_map.260 = (bf16[192,1536]{1,0:T(8,128)(2,1)}, f32[192,1536]{1,0:T(8,128)}) custom-call(s32[2]{0:T(128)} %pad_add_fusion.info_ref, bf16[384,2048]{1,0:T(8,128)(2,1)} %shard_map.259.q_ref.refs_1_, bf16[8,2,192,512]{3,2,1,0:T(8,128)(2,1)} %bitcast.120, bf16[8,2,192,512]{3,2,1,0:T(8,128)(2,1)} %bitcast.121), custom_call_target="tpu_custom_call" | custom-call | flops 3623878656 | bytes 3932160 | tf_op jit(solution)/shard_map/pallas_call | solution.py:540
  154.5 2.6 multiply_reduce_fusion.8
  160.1 10.7 %shard_map.262 = (bf16[192,1536]{1,0:T(8,128)(2,1)}, f32[192,1536]{1,0:T(8,128)}) custom-call(s32[2]{0:T(128)} %pad_add_fusion.1.info_ref, bf16[384,2048]{1,0:T(8,128)(2,1)} %shard_map.259.q_ref.refs_1_, bf16[8,2,192,512]{3,2,1,0:T(8,128)(2,1)} %bitcast.122, bf16[8,2,192,512]{3,2,1,0:T(8,128)(2,1)} %bitcast.123), custom_call_target="tpu_custom_call" | custom-call | flops 3623878656 | bytes 3932160 | tf_op jit(solution)/shard_map/pallas_call | solution.py:540
  170.8 2.7 multiply_reduce_fusion.7
  175.5 34.0 %all-gather.10.cloned.1.call-done.refs_1_ = bf16[1536,1536]{1,0:T(8,128)(2,1)} async-done(((bf16[192,1536]{1,0:T(8,128)(2,1)}), bf16[1536,1536]{1,0:T(8,128)(2,1)}) %all-gather.10.cloned.1.call-update) | async-done | bytes 4718608 | tf_op jit(solution)/shard_map/all_gather | solution.py:1394
  209.5 105.6 %shard_map.263 = (bf16[1536,1536]{1,0:T(8,128)(2,1)}, f32[192,1536]{1,0:T(8,128)}, bf16[2,2,3360,384]{3,2,1,0:T(8,128)(2,1)}, bf16[1536,1536]{1,0:T(8,128)(2,1)}) custom-call(bf16[1536,1536]{1,0:T(8,128)(2,1)} %all-gather.8.cloned.1.call-done.refs_0_, bf16[1536,1536]{1,0:T(8,128)(2,1)} %all-gather.10.cloned.1.call-done.refs_1_, ...), custom_call_target="tpu_custom_call" | custom-call | flops 47563407360 | bytes 94371840 | tf_op jit(solution)/shard_map/pallas_call | solution.py:1261
  315.2 118.0 %shard_map.264 = (bf16[1536,1536]{1,0:T(8,128)(2,1)}, f32[192,1536]{1,0:T(8,128)}, bf16[2,2,3360,384]{3,2,1,0:T(8,128)(2,1)}, bf16[3360,384]{1,0:T(8,128)(2,1)}, bf16[2,3360,384]{2,1,0:T(8,128)(2,1)}) custom-call(bf16[1536,1536]{1,0:T(8,128)(2,1)} %all-gather.12.cloned.1.call-done.refs_0_, bf16[1536,1536]{1,0:T(8,128)(2,1)} %get-tuple-element.76.refs_1_, ...), custom_call_target="tpu_custom_call" | custom-call | flops 47563407360 | bytes 94371840 | tf_op jit(solution)/shard_map/pallas_call | solution.py:1261
  433.3 2.2 multiply_convert_fusion
  442.4 3.0 convolution_convert_fusion.3.refs_4_
  445.4 48.8 %shard_map.265 = (bf16[384,1536]{1,0:T(8,128)(2,1)}, bf16[2,192,512]{2,1,0:T(8,128)(2,1)}) custom-call(s32[2]{0:T(128)} %bitcast.109, bf16[384,2048]{1,0:T(8,128)(2,1)} %shard_map.259.q_ref.refs_1_, bf16[8,2,192,512]{3,2,1,0:T(8,128)(2,1)} %bitcast.124, bf16[8,2,192,512]{3,2,1,0:T(8,128)(2,1)} %bitcast.125, ...), custom_call_target="tpu_custom_call" | custom-call | flops 18119393280 | bytes 13369344 | tf_op jit(solution)/shard_map/pallas_call | solution.py:732
  503.4 4.8 fusion
  508.2 2.6 multiply_reduce_fusion
  511.7 4.3 convolution_convert_fusion.1
  516.0 2.2 convolution_convert_fusion.2
  518.2 4.5 convolution_convert_fusion
  522.7 2.1 multiply_add_fusion
  524.8 9.6 %all-gather.16.cloned.1.call-done = bf16[13440,384]{1,0:T(8,128)(2,1)} async-done(((bf16[3360,384]{1,0:T(8,128)(2,1)}), bf16[13440,384]{1,0:T(8,128)(2,1)}) %all-gather.16.cloned.1.call-update) | async-done | bytes 10321936 | tf_op jit(solution)/shard_map/all_gather | solution.py:1409
  536.3 80.6 %shard_map.266 = (f32[48,1536]{1,0:T(8,128)}, f32[48,1536]{1,0:T(8,128)}, f32[48,512]{1,0:T(8,128)}, f32[48,128]{1,0:T(8,128)}) custom-call(bf16[16,2,48,1536]{3,2,1,0:T(8,128)(2,1)} %bitcast.97, bf16[16,2,48,1536]{3,2,1,0:T(8,128)(2,1)} %bitcast.98, bf16[16,2,48,512]{3,2,1,0:T(8,128)(2,1)} %bitcast.102, bf16[16,2,48,128]{3,2,1,0:T(8,128)(2,1)} %bitcast.100), custom_call_target="tpu_custom_call" | custom-call | bytes 45613056 | tf_op jit(solution)/shard_map/pallas_call | solution.py:446
  622.7 11.4 %shard_map.267 = (f32[1120,1536]{1,0:T(8,128)}, f32[1120,1536]{1,0:T(8,128)}, f32[1120,1536]{1,0:T(8,128)}) custom-call(bf16[4,3360,384]{2,1,0:T(8,128)(2,1)} %bitcast.83, bf16[4,3360,384]{2,1,0:T(8,128)(2,1)} %bitcast.84, bf16[4,3360,384]{2,1,0:T(8,128)(2,1)} %bitcast.85), custom_call_target="tpu_custom_call" | custom-call | bytes 30965760 | tf_op jit(solution)/shard_map/pallas_call | solution.py:1288
  (170 shorter events, 51.0 us)
Async XLA Ops:
  7.2 32.3 %copy-start.38 = (s32[2,1]{0,1:T(1,128)S(1)}, s32[2,1]{0,1:T(1,128)}, u32[]{:S(2)}) copy-start(s32[2,1]{0,1:T(1,128)} %param.16) | copy-start | bytes 28
  7.2 32.4 %copy-start.13 = (bf16[2,1,192,1536]{3,2,1,0:T(8,128)(2,1)S(1)}, bf16[2,1,192,1536]{3,2,1,0:T(8,128)(2,1)}, u32[]{:S(2)}) copy-start(bf16[2,1,192,1536]{3,2,1,0:T(8,128)(2,1)} %param.29) | copy-start | bytes 3538948
  7.2 96.4 %all-gather.8.cloned.1.call-start = ((), (), s32[]{:S(2)}) async-start(), calls=%async_computation.2 | async-start | bytes 5308416 | tf_op jit(solution)/shard_map/all_gather | solution.py:1356
  41.6 102.1 %all-gather.14.cloned.1.call-start = ((), (), s32[]{:S(2)}) async-start(), calls=%async_computation.7 | async-start | bytes 3538944 | tf_op jit(solution)/shard_map/all_gather | solution.py:1377
  42.3 46.3 %copy-start.33 = (f32[2,192]{1,0:T(2,128)}, f32[2,192]{1,0:T(2,128)S(1)}, u32[]{:S(2)}) copy-start(f32[2,192]{1,0:T(2,128)S(1)} %add_rsqrt_fusion) | copy-start | bytes 4612
  42.4 47.8 %copy-start.31 = (f32[384]{0:T(512)}, f32[384]{0:T(512)S(1)}, u32[]{:S(2)}) copy-start(f32[384]{0:T(512)S(1)} %rsqrt.29) | copy-start | bytes 4612
  103.7 105.8 %all-gather.10.cloned.1.call-start = ((), (), s32[]{:S(2)}) async-start(), calls=%async_computation.3 | async-start | bytes 5308416 | tf_op jit(solution)/shard_map/all_gather | solution.py:1394
  143.7 10.8 %copy-start = (bf16[32,48,1536]{2,1,0:T(8,128)(2,1)S(1)}, bf16[32,48,1536]{2,1,0:T(8,128)(2,1)}, u32[]{:S(2)}) copy-start(bf16[32,48,1536]{2,1,0:T(8,128)(2,1)} %shard_map.261) | copy-start | bytes 14155780
  158.7 12.1 %slice-start = ((s8[4718592]{0:T(1024)(128)(4,1)}), s8[524288]{0:T(1024)(128)(4,1)S(1)}, s32[]{:S(2)}) async-start(s8[4718592]{0:T(1024)(128)(4,1)} %bitcast.87), calls=%async_computation.9 | async-start | bytes 1048576
  158.7 156.5 %all-gather.12.cloned.1.call-start = ((), (), s32[]{:S(2)}) async-start(), calls=%async_computation.4 | async-start | bytes 5308416 | tf_op jit(solution)/shard_map/all_gather | solution.py:1399
  160.1 10.7 %slice-start.1 = ((s8[4718592]{0:T(1024)(128)(4,1)}), s8[4194304]{0:T(1024)(128)(4,1)S(1)}, s32[]{:S(2)}) async-start(s8[4718592]{0:T(1024)(128)(4,1)} %bitcast.87), calls=%async_computation.10 | async-start | bytes 8388608
  209.5 223.7 %reduce-scatter.3.cloned.1.call-start = ((), (), s32[]{:S(2)}) async-start(), calls=%async_computation.5 | async-start | bytes 5308416 | tf_op jit(solution)/shard_map/reduce_scatter | solution.py:1406
  315.1 219.3 %all-gather.16.cloned.1.call-start = ((), (), s32[]{:S(2)}) async-start(), calls=%async_computation.8 | async-start | bytes 12902400 | tf_op jit(solution)/shard_map/all_gather | solution.py:1409
  433.3 183.6 %reduce-scatter.5.cloned.1.call-start = ((), (), s32[]{:S(2)}) async-start(), calls=%async_computation.6 | async-start | bytes 5308416 | tf_op jit(solution)/shard_map/reduce_scatter | solution.py:1447
  435.5 3.2 copy-start.10
  438.7 3.3 slice-start.2
  445.4 50.5 %copy-start.27 = (f32[1536]{0:T(1024)S(1)}, f32[1536]{0:T(1024)}, u32[]{:S(2)}) copy-start(f32[1536]{0:T(1024)} %get-tuple-element.156) | copy-start | bytes 18436
  503.4 4.8 copy-start.21
  503.4 4.8 copy-start.32
  508.2 3.5 copy-start.8
  508.2 3.5 copy-start.18
  508.2 3.5 copy-start.19
  511.7 4.3 copy-start.15
  536.3 83.6 %copy-start.4 = (f32[192,1536]{1,0:T(8,128)S(1)}, f32[192,1536]{1,0:T(8,128)}, u32[]{:S(2)}) copy-start(f32[192,1536]{1,0:T(8,128)} %copy-done.2) | copy-start | bytes 3538948
  (27 other events, 52.7 us)
Sparse Core Ops, SparseCore 0:
  41.7 54.9 all-gather.7
  103.8 39.8 all-gather.13
  158.8 50.5 all-gather.9
  210.9 70.6 all-gather.11
  315.2 54.9 reduce-scatter.2
  433.4 100.9 all-gather.15
  536.7 77.4 reduce-scatter.4
